TPU v7x, 256 devices: a whole 4x4x8 slice. The times are simulated.
256 devices in a mesh: space: 64 (over y_lo, z, x), snap: 4 (over y_hi, core).
Axes of the slice: x: 4, y: 4 (y_hi: 2, y_lo: 2; y = y_hi * 2 + y_lo), z: 8, core: 2. Of those that a mesh axis runs over, the one named last changes fastest.
Arguments:
- snapshots: bfloat16 [64, 3, 128, 64, 128], P('snap', None, 'space'), may hold values from -8 to 8
- labels: int32 [128, 64, 128], P('space'), may hold values from 0 to 2
- free_mask: int32 [128, 64, 128], P('space'), may hold values 0 or 1
- density: float32 [3], replicated, may hold values from 0.5 to 2
Outputs:
- grams: float32 [4, 64, 64], P(None, 'space')
- slab_grams: float32 [64, 4, 64, 64], P('space')
All inputs are finite; a program needn't handle non-finite values. No bound on the sum of `free_mask` on one device may be relied on, other than what follows from the above.
Results may differ from a plain program's by a relative error of at most 0.0003.
Values may be sent and summed in bfloat16 or wider, within the bound.
No kernel may reach another device: no remote copies, remote signals or barrier semaphores. Data moves between devices by JAX's collectives and lax.ppermute only.
A program may use at most 128 MiB of HBM per device.

v0:
```python
import jax
import jax.numpy as jnp
from jax import lax
from jax.sharding import PartitionSpec as P


def extended(block, sides, width):
    for axis, dim in sides:
        count = lax.axis_size(axis)
        forward = [(i, i + 1) for i in range(count - 1)]
        backward = [(target, source) for source, target in forward]
        low = lax.ppermute(
            lax.slice_in_dim(block, block.shape[dim] - width, None, axis=dim), axis, forward
        )
        high = lax.ppermute(lax.slice_in_dim(block, 0, width, axis=dim), axis, backward)
        block = jnp.concatenate([low, block, high], axis=dim)
    return block


def mass_line(values, axis_dim):
    length = values.shape[axis_dim]
    before = lax.slice_in_dim(values, 0, length - 2, axis=axis_dim)
    centre = lax.slice_in_dim(values, 1, length - 1, axis=axis_dim)
    behind = lax.slice_in_dim(values, 2, length, axis=axis_dim)
    return (before + 4.0 * centre + behind) * (1.0 / 6.0)


def stiff_line(values, axis_dim):
    length = values.shape[axis_dim]
    before = lax.slice_in_dim(values, 0, length - 2, axis=axis_dim)
    centre = lax.slice_in_dim(values, 1, length - 1, axis=axis_dim)
    behind = lax.slice_in_dim(values, 2, length, axis=axis_dim)
    return 2.0 * centre - before - behind


def images(padded, density_field):
    values = padded.astype(jnp.float32)
    mass_x = mass_line(values, 2)
    stiff_x = stiff_line(values, 2)
    mass_xy = mass_line(mass_x, 3)
    mixed_xy = stiff_line(mass_x, 3)
    stiff_xy = mass_line(stiff_x, 3)
    mass_full = mass_line(mass_xy, 4)
    stiff_full = stiff_line(mass_xy, 4) + mass_line(mixed_xy, 4) + mass_line(stiff_xy, 4)
    return ((density_field * mass_full).astype(jnp.bfloat16), stiff_full.astype(jnp.bfloat16))


def density_of(cell_labels, density):
    density_field = jnp.zeros(cell_labels.shape, jnp.float32)
    for material in range(density.shape[0]):
        density_field = density_field + jnp.where(cell_labels == material, density[material], 0.0)
    return density_field


def stacked_images(mass_img, stiff_img, cell_labels, materials):
    zero_value = jnp.zeros((), stiff_img.dtype)
    blocks = [mass_img] + [
        jnp.where(cell_labels == material, stiff_img, zero_value) for material in range(materials)
    ]
    stacked = jnp.stack(blocks)
    return stacked.reshape(stacked.shape[0] * stacked.shape[1], -1)


def grams_of(snaps, stacked, count):
    flat_snaps = snaps.reshape(snaps.shape[0], -1)
    product = lax.dot_general(
        flat_snaps, stacked, (((1,), (1,)), ((), ())), preferred_element_type=jnp.float32
    )
    return product.reshape(snaps.shape[0], count, stacked.shape[0] // count).transpose(1, 0, 2)


def body(snapshots, labels, free_mask, density):
    materials = density.shape[0]
    masked = snapshots * free_mask.astype(jnp.bfloat16)[None, None]
    planes = snapshots.shape[2]
    columns = snapshots.shape[3]
    depth_z = snapshots.shape[4]
    slab_scale = 1.0 / (3.0 * planes * columns * depth_z)
    inverse = slab_scale / lax.axis_size("space")
    regrouped = lax.all_to_all(masked, "snap", split_axis=3, concat_axis=0, tiled=True)
    width_y = regrouped.shape[3]
    cell_labels = lax.dynamic_slice_in_dim(labels, lax.axis_index("snap") * width_y, width_y, 1)
    padded = extended(regrouped, (("space", 2), ("snap", 3)), 1)
    padded = jnp.pad(padded, ((0, 0), (0, 0), (0, 0), (0, 0), (1, 1)))
    mass_img, stiff_img = images(padded, density_of(cell_labels, density))
    stacked = stacked_images(mass_img, stiff_img, cell_labels, materials)
    partial_value = grams_of(regrouped, stacked, materials + 1)
    grouped = lax.psum(partial_value, "snap")
    slab_out = (grouped * slab_scale)[None]
    summed = lax.psum(grouped, "space")
    rows_out = summed.shape[1] // lax.axis_size("space")
    result = lax.dynamic_slice_in_dim(summed, lax.axis_index("space") * rows_out, rows_out, 1)
    return (result * inverse, slab_out)


def solution(mesh):
    in_specs = (
        P("snap", None, "space", None, None),
        P("space", None, None),
        P("space", None, None),
        P(),
    )
    out_specs = (P(None, "space", None), P("space", None, None, None))
    return jax.shard_map(body, mesh=mesh, in_specs=in_specs, out_specs=out_specs, check_vma=False)
```

profile of v0, /device:TPU:16, one launch (start us, length us, event | category | flops | bytes accessed | tf_op | source)
XLA Modules:
  0.0 747.6 jit_solution(10116323424417448862)
XLA Ops:
  7.2 0.0 all-reduce.4.cloned.1.call-start
  7.2 0.8 convert_element_type.14
  8.1 2.7 copy_multiply_fusion
  10.8 0.0 copy-start.5
  10.8 23.0 %all_to_all.18 = bf16[16,3,2,64,128]{4,0,2,1,3:T(8,128)(2,1)S(1)} all-to-all(bf16[16,3,2,64,128]{4,0,2,1,3:T(8,128)(2,1)S(1)} %copy_multiply_fusion), channel_id=1, replica_groups=mesh['space'=64,'snap'=4] {'snap'}, dimensions={3} | all-to-all | bytes 3145728 | tf_op jit(solution)/shard_map/all_to_all | solution.py:80
  33.8 0.6 copy.16
  34.4 1.4 fusion.29
  35.9 3.4 collective-permute-start
  39.3 1.3 collective-permute-start.1
  40.6 15.8 %collective-permute-done = bf16[64,3,1,16,128]{4,3,2,1,0:T(8,128)(2,1)S(1)} collective-permute-done((bf16[64,3,1,16,128]{4,3,2,1,0:T(8,128)(2,1)}, bf16[64,3,1,16,128]{4,3,2,1,0:T(8,128)(2,1)S(1)}, u32[]{:S(2)}, u32[]{:S(2)}) %collective-permute-start) | collective-permute-done | bytes 786464 | tf_op jit(solution)/shard_map/ppermute | solution.py:12
  56.4 4.1 collective-permute-done.1
  60.5 1.6 pad_maximum_fusion.2
  62.1 1.9 collective-permute-start.2
  64.0 5.3 collective-permute-start.3
  69.3 0.0 copy-done.5
  69.3 0.6 fusion.31
  70.0 3.2 add_multiply_fusion.2
  73.2 1.6 reshape.23
  74.8 0.0 collective-permute-done.2
  74.8 0.0 collective-permute-done.3
  74.8 12.2 %fusion.1 = f32[64,3,4,18,130]{4,3,2,1,0:T(8,128)S(1)} fusion(bf16[64,3,4,1,128]{4,3,2,1,0:T(2,128)(2,1)} %collective-permute-done.3, bf16[64,3,4,1,128]{4,3,2,1,0:T(2,128)(2,1)S(1)} %collective-permute-done.2, bf16[64,3,1,16,128]{4,3,2,1,0:T(8,128)(2,1)S(1)} %collective-permute-done.1, bf16[64,3,2,16,128]{4,3,2,1,0:T(8,128)(2,1)S(1)} %bitcast.26, ...), kind=kLoop, calls=%fused_computation.4 | loop fusion | flops 32348160 | bytes 10727424 | tf_op jit(solution)/shard_map/convert_element_type | solution.py:37
  86.9 7.8 %add_multiply_fusion = (f32[64,3,2,18,130]{4,3,2,1,0:T(8,128)}, f32[64,3,2,18,130]{4,3,2,1,0:T(8,128)}) fusion(f32[64,3,4,18,130]{4,3,2,1,0:T(8,128)S(1)} %fusion.1), kind=kLoop, calls=%fused_computation.12 | loop fusion | flops 6289920 | bytes 17971200 | tf_op jit(solution)/shard_map/mul | solution.py:25
  94.7 0.0 copy-start
  94.7 14.3 %add_multiply_fusion.1 = (f32[64,3,2,16,130]{4,3,2,1,0:T(8,128)}, f32[64,3,2,16,130]{4,3,2,1,0:T(8,128)}) fusion(f32[64,3,2,18,130]{4,3,2,1,0:T(8,128)} %get-tuple-element.8), kind=kLoop, calls=%fused_computation.26 | loop fusion | flops 5591040 | bytes 15974400 | tf_op jit(solution)/shard_map/mul | solution.py:25
  109.1 0.0 copy-done
  109.1 0.0 copy-start.4
  109.1 3.5 fusion.7
  112.6 0.0 copy-done.4
  112.6 0.0 copy-start.2
  112.6 0.0 copy-start.3
  112.6 17.5 %broadcast_select_fusion.2 = (bf16[64,3,2,16,128]{4,3,2,1,0:T(8,128)(2,1)S(1)}, bf16[64,3,2,16,128]{4,3,2,1,0:T(8,128)(2,1)S(1)}) fusion(pred[2,16,128]{2,1,0:T(8,128)(4,1)S(1)} %copy-done.4, f32[64,3,2,16,130]{4,3,2,1,0:T(8,128)} %fusion.7, f32[64,3,2,16,130]{4,3,2,1,0:T(8,128)} %get-tuple-element.11, f32[64,3,2,16,130]{4,3,2,1,0:T(8,128)} %get-tuple-element.10), kind=kLoop, calls=%fused_computation.42 | loop fusion | flops 11796480 | bytes 31461376 | tf_op jit(solution)/shard_map/jit(_where)/select_n | solution.py:58
  130.1 0.0 copy-done.2
  130.1 0.0 copy-done.3
  130.1 1.4 broadcast_select_fusion.1
  131.5 3.6 stack.17
  135.1 1.6 stack.18
  136.6 1.6 stack.16
  138.2 7.3 multiply_convert_fusion
  145.6 1.6 stack.15
  147.1 0.0 copy-done.1
  147.1 6.1 fusion.24
  153.3 0.0 all-reduce.4.cloned.1.call-update
  153.3 48.3 %all-reduce.4.cloned.1.call-done = f32[4,64,64]{2,1,0:T(8,128)} async-done(((f32[4,64,64]{2,1,0:T(8,128)}), f32[4,64,64]{2,1,0:T(8,128)}) %all-reduce.4.cloned.1.call-update) | async-done | bytes 65552 | tf_op jit(solution)/shard_map/psum | solution.py:88
  201.6 1.6 multiply_bitcast_fusion
  203.1 0.0 all-reduce.6.cloned.1.call-start
  203.1 0.7 all-reduce.6.cloned.1.call-update
  203.9 535.6 %all-reduce.6.cloned.1.call-done = f32[4,64,64]{2,1,0:T(8,128)} async-done(((f32[4,64,64]{2,1,0:T(8,128)}), f32[4,64,64]{2,1,0:T(8,128)}) %all-reduce.6.cloned.1.call-update) | async-done | bytes 65552 | tf_op jit(solution)/shard_map/psum | solution.py:90
  739.5 1.3 dynamic-slice_multiply_fusion
  (2 shorter events, 0.0 us)
Async XLA Ops:
  7.2 194.4 %all-reduce.4.cloned.1.call-start = ((), (), s32[]{:S(2)}) async-start(), calls=%async_computation.1 | async-start | bytes 262144 | tf_op jit(solution)/shard_map/psum | solution.py:88
  10.8 58.5 %copy-start.5 = (f32[3]{0:T(128)S(1)}, f32[3]{0:T(128)}, u32[]{:S(2)}) copy-start(f32[3]{0:T(128)} %param.7) | copy-start | bytes 40
  35.9 20.6 %collective-permute-start = (bf16[64,3,1,16,128]{4,3,2,1,0:T(8,128)(2,1)}, bf16[64,3,1,16,128]{4,3,2,1,0:T(8,128)(2,1)S(1)}, u32[]{:S(2)}, u32[]{:S(2)}) collective-permute-start(bf16[64,3,1,16,128]{4,3,2,1,0:T(8,128)(2,1)} %get-tuple-element.16), channel_id=1, source_target_pairs={{0,4},{4,8},{8,12},{12,16},{16,20},{20,24},{24,28},{28,32},{32,36}... | collective-permute-start | bytes 2359304 | tf_op jit(solution)/shard_map/ppermute | solution.py:12
  39.3 21.2 %collective-permute-start.1 = (bf16[64,3,1,16,128]{4,3,2,1,0:T(8,128)(2,1)}, bf16[64,3,1,16,128]{4,3,2,1,0:T(8,128)(2,1)S(1)}, u32[]{:S(2)}, u32[]{:S(2)}) collective-permute-start(bf16[64,3,1,16,128]{4,3,2,1,0:T(8,128)(2,1)} %get-tuple-element.17), channel_id=1, source_target_pairs={{4,0},{8,4},{12,8},{16,12},{20,16},{24,20},{28,24},{32,28},{36,32}... | collective-permute-start | bytes 2359304 | tf_op jit(solution)/shard_map/ppermute | solution.py:15
  62.1 12.7 %collective-permute-start.2 = (bf16[64,3,4,1,128]{4,3,2,1,0:T(2,128)(2,1)}, bf16[64,3,4,1,128]{4,3,2,1,0:T(2,128)(2,1)S(1)}, u32[]{:S(2)}, u32[]{:S(2)}) collective-permute-start(bf16[64,3,4,1,128]{4,3,2,1,0:T(2,128)(2,1)} %get-tuple-element.12), channel_id=1, source_target_pairs={{0,1},{1,2},{2,3},{4,5},{5,6},{6,7},{8,9},{9,10},{10,11},{12,13},{... | collective-permute-start | bytes 589832 | tf_op jit(solution)/shard_map/ppermute | solution.py:12
  64.0 10.8 %collective-permute-start.3 = (bf16[64,3,4,1,128]{4,3,2,1,0:T(2,128)(2,1)}, bf16[64,3,4,1,128]{4,3,2,1,0:T(2,128)(2,1)}, u32[]{:S(2)}, u32[]{:S(2)}) collective-permute-start(bf16[64,3,4,1,128]{4,3,2,1,0:T(2,128)(2,1)} %get-tuple-element.13), channel_id=1, source_target_pairs={{1,0},{2,1},{3,2},{5,4},{6,5},{7,6},{9,8},{10,9},{11,10},{13,12},{... | collective-permute-start | bytes 589832 | tf_op jit(solution)/shard_map/ppermute | solution.py:15
  94.7 14.3 %copy-start = (f32[64,3,2,18,130]{4,3,2,1,0:T(8,128)S(1)}, f32[64,3,2,18,130]{4,3,2,1,0:T(8,128)}, u32[]{:S(2)}) copy-start(f32[64,3,2,18,130]{4,3,2,1,0:T(8,128)} %get-tuple-element.9) | copy-start | bytes 10782724
  109.1 3.5 copy-start.4
  112.6 17.5 %copy-start.2 = (pred[2,16,128]{2,1,0:T(8,128)(4,1)S(1)}, pred[2,16,128]{2,1,0:T(8,128)(4,1)}, u32[]{:S(2)}) copy-start(pred[2,16,128]{2,1,0:T(8,128)(4,1)} %get-tuple-element.4) | copy-start | bytes 12292
  112.6 17.5 %copy-start.3 = (pred[2,16,128]{2,1,0:T(8,128)(4,1)S(1)}, pred[2,16,128]{2,1,0:T(8,128)(4,1)}, u32[]{:S(2)}) copy-start(pred[2,16,128]{2,1,0:T(8,128)(4,1)} %get-tuple-element.5) | copy-start | bytes 12292
  138.2 8.9 %copy-start.1 = (bf16[64,12288,1]{1,0,2:T(8,128)(2,1)S(1)}, bf16[64,12288,1]{1,0,2:T(8,128)(2,1)}, u32[]{:S(2)}) copy-start(bf16[64,12288,1]{1,0,2:T(8,128)(2,1)} %reshape.23) | copy-start | bytes 4718596
  203.1 536.3 %all-reduce.6.cloned.1.call-start = ((), (), s32[]{:S(2)}) async-start(), calls=%async_computation.2 | async-start | bytes 262144 | tf_op jit(solution)/shard_map/psum | solution.py:90
Sparse Core Ops, SparseCore 0:
  153.4 48.1 all-reduce.3
  206.8 532.6 all-reduce.5
where the time goes:
time: 748 us
  waiting for transfers between devices  605 us (81%)
  other arithmetic  75.1 us (10%)
  blocking collectives  23 us (3%)
  between operations  14.1 us (2%)
  local copies, waits for them, and re-layouts  12.7 us (2%)
  starting transfers between devices  12 us (2%)
    psum x1, waiting for transfers between devices, body(): summed = lax.psum(grouped, 'space')  536 us
    psum x1, waiting for transfers between devices, body(): grouped = lax.psum(partial_value, 'snap')  48.3 us
    mul x3, other arithmetic, mass_line(): return (before + 4.0 * centre + behind) * (1.0 / 6.0)  25.6 us
    all_to_all x1, blocking collectives, body(): lax.all_to_all(masked, 'snap', split_axis=3, concat_axis=0, tiled=True)  23 us
    select_n x2, other arithmetic, stacked_images(): jnp.where(cell_labels == material, stiff_img, zero_value)  18.9 us
    ppermute x2, waiting for transfers between devices, extended(): lax.ppermute(lax.slice_in_dim(block, block.shape[dim] - width, None, axis...  15.8 us
  transfers between devices with their start and end apart: 6, of which 4 were waited for; matrix products, arithmetic and copies ran while one was open for 1% of the time, Pallas kernels for 0%

commit v1 on v0

v1 whole, which is shorter than its diff:
```python
import functools

import jax
import jax.numpy as jnp
import numpy as np
from jax import lax
from jax.experimental import pallas as pl
from jax.experimental.pallas import tpu as pltpu
from jax.sharding import PartitionSpec as P


def spread_kernel(groups, width, me_ref, snaps_ref, mask_ref, *refs):
    outs, turned = refs[:groups], refs[groups]
    rows = snaps_ref.shape[3]
    me = me_ref[0]
    mask = mask_ref[0].astype(jnp.float32)
    values = snaps_ref[:, 0, 0].astype(jnp.float32) * mask[None]
    edge = jnp.zeros(turned.shape[1:], turned.dtype)
    turned[0] = edge
    turned[rows + 1] = edge
    turned[1 : rows + 1] = jnp.swapaxes(values, 0, 1).astype(turned.dtype)
    for m in range(groups):
        outs[m][0, 0] = turned[pl.ds((me ^ m) * width, width + 2)]


def spread(snapshots, free_mask, me, groups):
    members, comps, planes, rows, depth = snapshots.shape
    width = rows // groups
    block = jax.ShapeDtypeStruct((comps, planes, width + 2, members, depth), snapshots.dtype)
    out_spec = pl.BlockSpec((1, 1, width + 2, members, depth), lambda c, p, me: (c, p, 0, 0, 0))
    return pl.pallas_call(
        functools.partial(spread_kernel, groups, width),
        out_shape=[block] * groups,
        grid_spec=pltpu.PrefetchScalarGridSpec(
            num_scalar_prefetch=1,
            grid=(comps, planes),
            in_specs=[
                pl.BlockSpec((members, 1, 1, rows, depth), lambda c, p, me: (0, c, p, 0, 0)),
                pl.BlockSpec((1, rows, depth), lambda c, p, me: (p, 0, 0)),
            ],
            out_specs=[out_spec] * groups,
            scratch_shapes=[pltpu.VMEM((rows + 2, members, depth), snapshots.dtype)],
        ),
        compiler_params=pltpu.CompilerParams(vmem_limit_bytes=32 * 2**20),
        cost_estimate=pl.CostEstimate(flops=0, bytes_accessed=5 * 2**20, transcendentals=0),
    )(me, snapshots, free_mask)


def stencil_weights(depth):
    mass = {-1: 1.0, 0: 4.0, 1: 1.0}
    stiff = {-1: -1.0, 0: 2.0, 1: -1.0}
    near = np.eye(depth, k=1) + np.eye(depth, k=-1)
    mass_z = 4.0 * np.eye(depth) + near
    stiff_z = 2.0 * np.eye(depth) - near
    blocks = []
    for dx in (-1, 0, 1):
        for dy in (-1, 0, 1):
            both = mass[dx] * mass[dy]
            mixed = stiff[dx] * mass[dy] + mass[dx] * stiff[dy]
            blocks.append(np.concatenate([both * mass_z, mixed * mass_z + both * stiff_z], axis=1))
    return np.concatenate(blocks, axis=0)


def tiles_kernel(groups, materials, me_ref, density_ref, *refs):
    sources = refs[:groups]
    low_ref, high_ref, labels_ref, weights_ref, part_ref, wide_ref, left, right = refs[groups:]
    comp = pl.program_id(0)
    me = me_ref[0]
    planes, reach, members, depth = sources[0].shape[1:]
    width = reach - 2
    count = groups * members

    @pl.when(comp == 0)
    def _():
        part_ref[...] = jnp.zeros_like(part_ref)

    for p in range(planes):
        shifted = []
        for m in range(groups):
            pieces = []
            for dx in (-1, 0, 1):
                at = p + dx
                plane = low_ref.at[0, m] if at < 0 else high_ref.at[0, m] if at >= planes else sources[m].at[0, at]
                for dy in range(3):
                    pieces.append(plane[dy : dy + width].reshape(width * members, depth))
            shifted.append(jnp.concatenate(pieces, axis=1))
        image = jnp.dot(
            jnp.concatenate(shifted, axis=0), weights_ref[...], preferred_element_type=jnp.float32
        )
        mass = image[:, :depth].reshape(groups, width, members, depth)
        stiff = image[:, depth:].reshape(groups, width, members, depth) * (1.0 / 36.0)
        for y in range(width):
            label = labels_ref[p, pl.ds(me * width + y, 1), :]
            density = jnp.zeros(label.shape, jnp.float32)
            for j in range(materials):
                density = density + jnp.where(label == j, density_ref[j] * (1.0 / 216.0), 0.0)
            lanes = slice((p * width + y) * depth, (p * width + y + 1) * depth)
            for m in range(groups):
                start = pl.multiple_of((me ^ m) * members, members)
                left[pl.ds(start, members), lanes] = sources[m][0, p, y + 1]
                right[pl.ds(start, members), lanes] = (mass[m, y] * density).astype(right.dtype)
                for j in range(materials):
                    at = pl.multiple_of((j + 1) * count + start, members)
                    right[pl.ds(at, members), lanes] = jnp.where(label == j, stiff[m, y], 0.0).astype(right.dtype)
    part_ref[...] += lax.dot_general(
        left[...], right[...], (((1,), (1,)), ((), ())), preferred_element_type=jnp.float32
    )

    @pl.when(comp == pl.num_programs(0) - 1)
    def _():
        for s in range(count):
            row = part_ref[pl.ds(s, 1), :]
            wide_ref[pl.ds(s * groups, groups), :] = jnp.broadcast_to(row, (groups, row.shape[1]))


def tiles(blocks, low, high, labels, density, me):
    groups = len(blocks)
    comps, planes, reach, members, depth = blocks[0].shape
    materials = density.shape[0]
    count = groups * members
    cells = planes * (reach - 2) * depth
    columns = (materials + 1) * count
    weights = jnp.asarray(stencil_weights(depth), jnp.bfloat16)
    block = pl.BlockSpec((1, planes, reach, members, depth), lambda c, *_: (c, 0, 0, 0, 0))
    halo = pl.BlockSpec((1, groups, reach, members, depth), lambda c, *_: (c, 0, 0, 0, 0))
    whole = lambda a: pl.BlockSpec(a.shape, lambda c, *_: (0,) * a.ndim)
    part = jax.ShapeDtypeStruct((count, columns), jnp.float32)
    wide = jax.ShapeDtypeStruct((count * groups, columns), jnp.float32)
    return pl.pallas_call(
        functools.partial(tiles_kernel, groups, materials),
        out_shape=[part, wide],
        grid_spec=pltpu.PrefetchScalarGridSpec(
            num_scalar_prefetch=2,
            grid=(comps,),
            in_specs=[block] * groups + [halo, halo, whole(labels), whole(weights)],
            out_specs=[whole(part), whole(wide)],
            scratch_shapes=[
                pltpu.VMEM((count, cells), jnp.bfloat16),
                pltpu.VMEM((columns, cells), jnp.bfloat16),
            ],
        ),
        compiler_params=pltpu.CompilerParams(vmem_limit_bytes=48 * 2**20),
        cost_estimate=pl.CostEstimate(flops=5 * 10**9, bytes_accessed=5 * 2**20, transcendentals=0),
    )(me, density, *blocks, low, high, labels, weights)


def finish_kernel(count, slab_scale, gram_scale, *refs):
    parts, rows_ref, slab_ref, gram_ref = refs[:-3], refs[-3], refs[-2], refs[-1]
    terms = [p[...] for p in parts]
    while len(terms) > 1:
        terms = [terms[i] + terms[i + 1] for i in range(0, len(terms), 2)]
    slab = terms[0] * slab_scale
    gram = jnp.sum(rows_ref[...], axis=0, keepdims=True) * gram_scale
    for j in range(slab.shape[1] // count):
        slab_ref[0, j] = slab[:, j * count : (j + 1) * count]
        gram_ref[j] = gram[:, j * count : (j + 1) * count]


def finish(parts, rows, slab_scale, gram_scale):
    count, columns = parts[0].shape
    blocks = columns // count
    return pl.pallas_call(
        functools.partial(finish_kernel, count, slab_scale, gram_scale),
        out_shape=[
            jax.ShapeDtypeStruct((1, blocks, count, count), jnp.float32),
            jax.ShapeDtypeStruct((blocks, 1, count), jnp.float32),
        ],
    )(*parts, rows)


def body(snapshots, labels, free_mask, density):
    groups, slabs = lax.axis_size("snap"), lax.axis_size("space")
    planes, rows, depth = labels.shape
    me = lax.axis_index("snap").astype(jnp.int32).reshape(1)
    with jax.named_scope("spread"):
        mine = spread(snapshots, free_mask, me, groups)
    with jax.named_scope("regroup"):
        blocks = [mine[0]] + [
            lax.ppermute(mine[m], "snap", [(i, i ^ m) for i in range(groups)]) for m in range(1, groups)
        ]
    with jax.named_scope("halo"):
        forward = [(i, i + 1) for i in range(slabs - 1)]
        backward = [(b, a) for a, b in forward]
        low = lax.ppermute(jnp.stack([b[:, planes - 1] for b in blocks], axis=1), "space", forward)
        high = lax.ppermute(jnp.stack([b[:, 0] for b in blocks], axis=1), "space", backward)
    with jax.named_scope("tiles"):
        part, wide = tiles(blocks, low, high, labels, density, me)
    with jax.named_scope("sums"):
        parts = [part] + [
            lax.ppermute(part, "snap", [(i, i ^ m) for i in range(groups)]) for m in range(1, groups)
        ]
        sent = lax.all_to_all(wide, ("space", "snap"), 0, 0, tiled=True)
        slab_scale = 1.0 / (3.0 * planes * rows * depth)
        slab, gram = finish(parts, sent, slab_scale, slab_scale / slabs)
    return gram, slab


def solution(mesh):
    in_specs = (
        P("snap", None, "space", None, None),
        P("space", None, None),
        P("space", None, None),
        P(),
    )
    out_specs = (P(None, "space", None), P("space", None, None, None))
    return jax.shard_map(body, mesh=mesh, in_specs=in_specs, out_specs=out_specs, check_vma=False)
```

time: 748 us -> 104 us (0.14)
  the two profiles are of different devices: /device:TPU:16 before, /device:TPU:1 now
where the time goes in v1:
time: 104 us
  waiting for transfers between devices  51.5 us (50%)
  starting transfers between devices  32 us (31%)
  Pallas kernels  14.9 us (14%)
  local copies, waits for them, and re-layouts  4.7 us (5%)
    ppermute x3, waiting for transfers between devices, body(): lax.ppermute(mine[m], 'snap', [(i, i ^ m) for i in range(groups)])  19.5 us
    all_to_all x1, starting transfers between devices, body(): sent = lax.all_to_all(wide, ('space', 'snap'), 0, 0, tiled=True)  17.5 us
    ppermute x1, waiting for transfers between devices, body(): lax.ppermute(jnp.stack([b[:, planes - 1] for b in blocks], axis=1), 'spac...  17.3 us
    pallas_call x1, Pallas kernels, tiles(): pl.pallas_call(functools.partial(tiles_kernel, groups, materials), out_sh...  11.8 us
    all_to_all x1, waiting for transfers between devices, body(): sent = lax.all_to_all(wide, ('space', 'snap'), 0, 0, tiled=True)  10.6 us
    ppermute x3, starting transfers between devices, body(): lax.ppermute(mine[m], 'snap', [(i, i ^ m) for i in range(groups)])  6.56 us
    ppermute x3, starting transfers between devices, body(): lax.ppermute(part, 'snap', [(i, i ^ m) for i in range(groups)])  5.09 us
    ppermute x1, waiting for transfers between devices, body(): lax.ppermute(jnp.stack([b[:, 0] for b in blocks], axis=1), 'space', backw...  3.97 us
  transfers between devices with their start and end apart: 9, of which 5 were waited for; matrix products, arithmetic and copies ran while one was open for 1% of the time, Pallas kernels for 0%

profile of v1, /device:TPU:1, one launch (start us, length us, event | category | flops | bytes accessed | tf_op | source)
XLA Modules:
  0.0 104.1 jit_solution(18413978131400766338)
XLA Ops:
  0.6 0.0 copy-start
  0.6 1.4 %copy-done = bf16[16,3,2,64,128]{4,3,2,1,0:T(8,128)(2,1)S(1)} copy-done((bf16[16,3,2,64,128]{4,3,2,1,0:T(8,128)(2,1)S(1)}, bf16[16,3,2,64,128]{4,3,2,1,0:T(8,128)(2,1)}, u32[]{:S(2)}) %copy-start) | copy-done | bytes 1572888
  2.0 0.0 copy-start.1
  2.0 0.8 copy-done.1
  2.9 1.3 %spread.1 = (bf16[3,2,18,16,128]{4,3,2,1,0:T(8,128)(2,1)S(1)}, bf16[3,2,18,16,128]{4,3,2,1,0:T(8,128)(2,1)S(1)}, bf16[3,2,18,16,128]{4,3,2,1,0:T(8,128)(2,1)S(1)}, bf16[3,2,18,16,128]{4,3,2,1,0:T(8,128)(2,1)S(1)}) custom-call(s32[1]{0:T(128)} %bitcast.me_ref, bf16[16,3,2,64,128]{4,3,2,1,0:T(8,128)(2,1)S(1)} %copy-done, s32[2,64,128]{2,1,0:T(8,128)S(1)} %copy-done.1), custom_call_target="tpu_custom_call" | custom-call | bytes 5242880 | tf_op jit(solution)/shard_map/spread/pallas_call | solution.py:31
  4.2 3.3 %collective-permute-start = (bf16[3,2,18,16,128]{4,3,2,1,0:T(8,128)(2,1)S(1)}, bf16[3,2,18,16,128]{4,3,2,1,0:T(8,128)(2,1)S(1)}, u32[]{:S(2)}, u32[]{:S(2)}) collective-permute-start(bf16[3,2,18,16,128]{4,3,2,1,0:T(8,128)(2,1)S(1)} %get-tuple-element.11), channel_id=1, source_target_pairs={{0,1},{1,0},{2,3},{3,2},{4,5},{5,4},{6,7},{7,6},{8,9},{9,8},{10,11... | collective-permute-start | bytes 1327112 | tf_op jit(solution)/shard_map/regroup/ppermute | solution.py:179
  7.5 1.2 %collective-permute-start.1 = (bf16[3,2,18,16,128]{4,3,2,1,0:T(8,128)(2,1)S(1)}, bf16[3,2,18,16,128]{4,3,2,1,0:T(8,128)(2,1)S(1)}, u32[]{:S(2)}, u32[]{:S(2)}) collective-permute-start(bf16[3,2,18,16,128]{4,3,2,1,0:T(8,128)(2,1)S(1)} %get-tuple-element.12), channel_id=1, source_target_pairs={{0,2},{1,3},{2,0},{3,1},{4,6},{5,7},{6,4},{7,5},{8,10},{9,11},{10,... | collective-permute-start | bytes 1327112 | tf_op jit(solution)/shard_map/regroup/ppermute | solution.py:179
  8.7 2.0 %collective-permute-start.2 = (bf16[3,2,18,16,128]{4,3,2,1,0:T(8,128)(2,1)S(1)}, bf16[3,2,18,16,128]{4,3,2,1,0:T(8,128)(2,1)S(1)}, u32[]{:S(2)}, u32[]{:S(2)}) collective-permute-start(bf16[3,2,18,16,128]{4,3,2,1,0:T(8,128)(2,1)S(1)} %get-tuple-element.13), channel_id=1, source_target_pairs={{0,3},{1,2},{2,1},{3,0},{4,7},{5,6},{6,5},{7,4},{8,11},{9,10},{10,... | collective-permute-start | bytes 1327112 | tf_op jit(solution)/shard_map/regroup/ppermute | solution.py:179
  10.8 0.0 collective-permute-done.refs_1_
  10.8 9.9 %collective-permute-done.1.refs_2_ = bf16[3,2,18,16,128]{4,3,2,1,0:T(8,128)(2,1)S(1)} collective-permute-done((bf16[3,2,18,16,128]{4,3,2,1,0:T(8,128)(2,1)S(1)}, bf16[3,2,18,16,128]{4,3,2,1,0:T(8,128)(2,1)S(1)}, u32[]{:S(2)}, u32[]{:S(2)}) %collective-permute-start.1) | collective-permute-done | bytes 442400 | tf_op jit(solution)/shard_map/regroup/ppermute | solution.py:179
  20.8 9.6 %collective-permute-done.2.refs_3_ = bf16[3,2,18,16,128]{4,3,2,1,0:T(8,128)(2,1)S(1)} collective-permute-done((bf16[3,2,18,16,128]{4,3,2,1,0:T(8,128)(2,1)S(1)}, bf16[3,2,18,16,128]{4,3,2,1,0:T(8,128)(2,1)S(1)}, u32[]{:S(2)}, u32[]{:S(2)}) %collective-permute-start.2) | collective-permute-done | bytes 442400 | tf_op jit(solution)/shard_map/regroup/ppermute | solution.py:179
  30.4 0.0 copy-start.3
  30.4 0.0 copy-start.4
  30.4 0.0 copy-start.5
  30.5 0.1 pad_maximum_fusion
  30.6 1.6 %collective-permute-start.3 = (bf16[3,4,18,16,128]{4,3,2,1,0:T(8,128)(2,1)S(1)}, bf16[3,4,18,16,128]{4,3,2,1,0:T(8,128)(2,1)S(1)}, u32[]{:S(2)}, u32[]{:S(2)}) collective-permute-start(bf16[3,4,18,16,128]{4,3,2,1,0:T(8,128)(2,1)S(1)} %pad_maximum_fusion), channel_id=1, source_target_pairs={{0,4},{4,8},{8,12},{12,16},{16,20},{20,24},{24,28},{28,32},{32,36}... | collective-permute-start | bytes 2654216 | tf_op jit(solution)/shard_map/halo/ppermute | solution.py:184
  32.2 0.1 pad_maximum_fusion.1
  32.3 1.3 %collective-permute-start.4 = (bf16[3,4,18,16,128]{4,3,2,1,0:T(8,128)(2,1)S(1)}, bf16[3,4,18,16,128]{4,3,2,1,0:T(8,128)(2,1)S(1)}, u32[]{:S(2)}, u32[]{:S(2)}) collective-permute-start(bf16[3,4,18,16,128]{4,3,2,1,0:T(8,128)(2,1)S(1)} %pad_maximum_fusion.1), channel_id=1, source_target_pairs={{4,0},{8,4},{12,8},{16,12},{20,16},{24,20},{28,24},{32,28},{36,32}... | collective-permute-start | bytes 2654216 | tf_op jit(solution)/shard_map/halo/ppermute | solution.py:185
  33.6 17.3 %collective-permute-done.3.refs_4_ = bf16[3,4,18,16,128]{4,3,2,1,0:T(8,128)(2,1)S(1)} collective-permute-done((bf16[3,4,18,16,128]{4,3,2,1,0:T(8,128)(2,1)S(1)}, bf16[3,4,18,16,128]{4,3,2,1,0:T(8,128)(2,1)S(1)}, u32[]{:S(2)}, u32[]{:S(2)}) %collective-permute-start.3) | collective-permute-done | bytes 884768 | tf_op jit(solution)/shard_map/halo/ppermute | solution.py:184
  50.9 4.0 %collective-permute-done.4.refs_5_ = bf16[3,4,18,16,128]{4,3,2,1,0:T(8,128)(2,1)S(1)} collective-permute-done((bf16[3,4,18,16,128]{4,3,2,1,0:T(8,128)(2,1)S(1)}, bf16[3,4,18,16,128]{4,3,2,1,0:T(8,128)(2,1)S(1)}, u32[]{:S(2)}, u32[]{:S(2)}) %collective-permute-start.4) | collective-permute-done | bytes 884768 | tf_op jit(solution)/shard_map/halo/ppermute | solution.py:185
  54.9 0.0 copy-done.3
  54.9 0.0 copy-done.4
  54.9 0.0 copy-done.5
  54.9 11.8 %tiles.1 = (f32[64,256]{1,0:T(8,128)S(1)}, f32[256,256]{1,0:T(8,128)S(1)}) custom-call(s32[1]{0:T(128)} %bitcast.me_ref, f32[3]{0:T(128)S(1)} %copy-done.4, bf16[3,2,18,16,128]{4,3,2,1,0:T(8,128)(2,1)S(1)} %get-tuple-element.10.refs_0_, bf16[3,2,18,16,128]{4,3,2,1,0:T(8,128)(2,1)S(1)} %collective-permute-done.refs_1_, ...), custom_call_target="tpu_custom_call" | custom-call | flops 5000000000 | bytes 5242880 | tf_op jit(solution)/shard_map/tiles/pallas_call | solution.py:129
  66.7 0.0 copy-start.2
  66.7 1.0 copy.7
  67.7 17.5 %all-to-all-start = ((f32[256,1,256]{2,1,0:T(1,128)}), f32[256,1,256]{2,1,0:T(1,128)S(1)}, u32[]{:S(2)}, u32[]{:S(2)}) async-start(f32[256,1,256]{2,1,0:T(1,128)} %copy.7), calls=%async_computation | async-start | bytes 524288 | tf_op jit(solution)/shard_map/sums/all_to_all | solution.py:192
  85.2 3.2 %collective-permute-start.7 = (f32[64,256]{1,0:T(8,128)S(1)}, f32[64,256]{1,0:T(8,128)S(1)}, u32[]{:S(2)}, u32[]{:S(2)}) collective-permute-start(f32[64,256]{1,0:T(8,128)S(1)} %get-tuple-element.14.refs_0_), channel_id=1, source_target_pairs={{0,3},{1,2},{2,1},{3,0},{4,7},{5,6},{6,5},{7,4},{8,11},{9,10},{10,... | collective-permute-start | bytes 196616 | tf_op jit(solution)/shard_map/sums/ppermute | solution.py:190
  88.4 1.9 %collective-permute-start.6 = (f32[64,256]{1,0:T(8,128)S(1)}, f32[64,256]{1,0:T(8,128)S(1)}, u32[]{:S(2)}, u32[]{:S(2)}) collective-permute-start(f32[64,256]{1,0:T(8,128)S(1)} %get-tuple-element.14.refs_0_), channel_id=1, source_target_pairs={{0,2},{1,3},{2,0},{3,1},{4,6},{5,7},{6,4},{7,5},{8,10},{9,11},{10,... | collective-permute-start | bytes 196616 | tf_op jit(solution)/shard_map/sums/ppermute | solution.py:190
  90.3 0.0 collective-permute-start.5
  90.3 10.6 %all-to-all-done = f32[256,1,256]{2,1,0:T(1,128)S(1)} async-done(((f32[256,1,256]{2,1,0:T(1,128)}), f32[256,1,256]{2,1,0:T(1,128)S(1)}, u32[]{:S(2)}, u32[]{:S(2)}) %all-to-all-start) | async-done | bytes 262176 | tf_op jit(solution)/shard_map/sums/all_to_all | solution.py:192
  100.8 0.7 copy.10
  101.6 0.0 collective-permute-done.7.refs_3_
  101.6 0.0 copy-start.6
  101.6 0.0 collective-permute-done.6.refs_2_
  101.6 0.0 copy-start.7
  101.6 0.0 collective-permute-done.5.refs_1_
  101.6 0.0 copy-start.8
  101.6 0.0 copy-done.2
  101.6 0.6 copy-done.6
  102.2 0.0 copy-done.7
  102.2 0.0 copy-done.8
  102.2 1.9 %sums.1 = (f32[1,4,64,64]{3,2,1,0:T(8,128)}, f32[4,1,64]{2,1,0:T(1,128)}) custom-call(f32[64,256]{1,0:T(8,128)} %copy-done.2, f32[64,256]{1,0:T(8,128)} %copy-done.8, f32[64,256]{1,0:T(8,128)} %copy-done.7, f32[64,256]{1,0:T(8,128)} %copy-done.6, f32[256,256]{1,0:T(8,128)} %bitcast.6), custom_call_target="tpu_custom_call" | custom-call | tf_op jit(solution)/shard_map/sums/pallas_call | solution.py:162
  (4 shorter events, 0.1 us)
Async XLA Ops:
  0.6 1.4 %copy-start = (bf16[16,3,2,64,128]{4,3,2,1,0:T(8,128)(2,1)S(1)}, bf16[16,3,2,64,128]{4,3,2,1,0:T(8,128)(2,1)}, u32[]{:S(2)}) copy-start(bf16[16,3,2,64,128]{4,3,2,1,0:T(8,128)(2,1)} %snaps_ref.1) | copy-start | bytes 4718596
  2.0 0.8 copy-start.1
  4.2 6.6 %collective-permute-start = (bf16[3,2,18,16,128]{4,3,2,1,0:T(8,128)(2,1)S(1)}, bf16[3,2,18,16,128]{4,3,2,1,0:T(8,128)(2,1)S(1)}, u32[]{:S(2)}, u32[]{:S(2)}) collective-permute-start(bf16[3,2,18,16,128]{4,3,2,1,0:T(8,128)(2,1)S(1)} %get-tuple-element.11), channel_id=1, source_target_pairs={{0,1},{1,0},{2,3},{3,2},{4,5},{5,4},{6,7},{7,6},{8,9},{9,8},{10,11... | collective-permute-start | bytes 1327112 | tf_op jit(solution)/shard_map/regroup/ppermute | solution.py:179
  7.5 13.2 %collective-permute-start.1 = (bf16[3,2,18,16,128]{4,3,2,1,0:T(8,128)(2,1)S(1)}, bf16[3,2,18,16,128]{4,3,2,1,0:T(8,128)(2,1)S(1)}, u32[]{:S(2)}, u32[]{:S(2)}) collective-permute-start(bf16[3,2,18,16,128]{4,3,2,1,0:T(8,128)(2,1)S(1)} %get-tuple-element.12), channel_id=1, source_target_pairs={{0,2},{1,3},{2,0},{3,1},{4,6},{5,7},{6,4},{7,5},{8,10},{9,11},{10,... | collective-permute-start | bytes 1327112 | tf_op jit(solution)/shard_map/regroup/ppermute | solution.py:179
  8.7 21.7 %collective-permute-start.2 = (bf16[3,2,18,16,128]{4,3,2,1,0:T(8,128)(2,1)S(1)}, bf16[3,2,18,16,128]{4,3,2,1,0:T(8,128)(2,1)S(1)}, u32[]{:S(2)}, u32[]{:S(2)}) collective-permute-start(bf16[3,2,18,16,128]{4,3,2,1,0:T(8,128)(2,1)S(1)} %get-tuple-element.13), channel_id=1, source_target_pairs={{0,3},{1,2},{2,1},{3,0},{4,7},{5,6},{6,5},{7,4},{8,11},{9,10},{10,... | collective-permute-start | bytes 1327112 | tf_op jit(solution)/shard_map/regroup/ppermute | solution.py:179
  30.4 24.5 %copy-start.3 = (s32[2,64,128]{2,1,0:T(8,128)S(1)}, s32[2,64,128]{2,1,0:T(8,128)}, u32[]{:S(2)}) copy-start(s32[2,64,128]{2,1,0:T(8,128)} %refs_6_.1) | copy-start | bytes 196612
  30.4 24.5 %copy-start.4 = (f32[3]{0:T(128)S(1)}, f32[3]{0:T(128)}, u32[]{:S(2)}) copy-start(f32[3]{0:T(128)} %density_ref.1) | copy-start | bytes 40
  30.4 24.5 %copy-start.5 = (bf16[1152,256]{1,0:T(8,128)(2,1)S(1)}, bf16[1152,256]{1,0:T(8,128)(2,1)}, u32[]{:S(2)}) copy-start(bf16[1152,256]{1,0:T(8,128)(2,1)} %constant.6.clone.refs_7_) | copy-start | bytes 1769476
  30.6 20.3 %collective-permute-start.3 = (bf16[3,4,18,16,128]{4,3,2,1,0:T(8,128)(2,1)S(1)}, bf16[3,4,18,16,128]{4,3,2,1,0:T(8,128)(2,1)S(1)}, u32[]{:S(2)}, u32[]{:S(2)}) collective-permute-start(bf16[3,4,18,16,128]{4,3,2,1,0:T(8,128)(2,1)S(1)} %pad_maximum_fusion), channel_id=1, source_target_pairs={{0,4},{4,8},{8,12},{12,16},{16,20},{20,24},{24,28},{28,32},{32,36}... | collective-permute-start | bytes 2654216 | tf_op jit(solution)/shard_map/halo/ppermute | solution.py:184
  32.3 22.6 %collective-permute-start.4 = (bf16[3,4,18,16,128]{4,3,2,1,0:T(8,128)(2,1)S(1)}, bf16[3,4,18,16,128]{4,3,2,1,0:T(8,128)(2,1)S(1)}, u32[]{:S(2)}, u32[]{:S(2)}) collective-permute-start(bf16[3,4,18,16,128]{4,3,2,1,0:T(8,128)(2,1)S(1)} %pad_maximum_fusion.1), channel_id=1, source_target_pairs={{4,0},{8,4},{12,8},{16,12},{20,16},{24,20},{28,24},{32,28},{36,32}... | collective-permute-start | bytes 2654216 | tf_op jit(solution)/shard_map/halo/ppermute | solution.py:185
  66.7 34.9 %copy-start.2 = (f32[64,256]{1,0:T(8,128)}, f32[64,256]{1,0:T(8,128)S(1)}, u32[]{:S(2)}) copy-start(f32[64,256]{1,0:T(8,128)S(1)} %get-tuple-element.14.refs_0_) | copy-start | bytes 196612
  67.7 33.2 %all-to-all-start = ((f32[256,1,256]{2,1,0:T(1,128)}), f32[256,1,256]{2,1,0:T(1,128)S(1)}, u32[]{:S(2)}, u32[]{:S(2)}) async-start(f32[256,1,256]{2,1,0:T(1,128)} %copy.7), calls=%async_computation | async-start | bytes 524288 | tf_op jit(solution)/shard_map/sums/all_to_all | solution.py:192
  85.2 16.4 %collective-permute-start.7 = (f32[64,256]{1,0:T(8,128)S(1)}, f32[64,256]{1,0:T(8,128)S(1)}, u32[]{:S(2)}, u32[]{:S(2)}) collective-permute-start(f32[64,256]{1,0:T(8,128)S(1)} %get-tuple-element.14.refs_0_), channel_id=1, source_target_pairs={{0,3},{1,2},{2,1},{3,0},{4,7},{5,6},{6,5},{7,4},{8,11},{9,10},{10,... | collective-permute-start | bytes 196616 | tf_op jit(solution)/shard_map/sums/ppermute | solution.py:190
  88.4 13.2 %collective-permute-start.6 = (f32[64,256]{1,0:T(8,128)S(1)}, f32[64,256]{1,0:T(8,128)S(1)}, u32[]{:S(2)}, u32[]{:S(2)}) collective-permute-start(f32[64,256]{1,0:T(8,128)S(1)} %get-tuple-element.14.refs_0_), channel_id=1, source_target_pairs={{0,2},{1,3},{2,0},{3,1},{4,6},{5,7},{6,4},{7,5},{8,10},{9,11},{10,... | collective-permute-start | bytes 196616 | tf_op jit(solution)/shard_map/sums/ppermute | solution.py:190
  90.3 11.3 %collective-permute-start.5 = (f32[64,256]{1,0:T(8,128)S(1)}, f32[64,256]{1,0:T(8,128)S(1)}, u32[]{:S(2)}, u32[]{:S(2)}) collective-permute-start(f32[64,256]{1,0:T(8,128)S(1)} %get-tuple-element.14.refs_0_), channel_id=1, source_target_pairs={{0,1},{1,0},{2,3},{3,2},{4,5},{5,4},{6,7},{7,6},{8,9},{9,8},{10,11... | collective-permute-start | bytes 196616 | tf_op jit(solution)/shard_map/sums/ppermute | solution.py:190
  101.6 0.6 copy-start.6
  101.6 0.6 copy-start.7
  101.6 0.6 copy-start.8

commit v2 on v1

v2 whole, which is shorter than its diff:
```python
import functools

import jax
import jax.numpy as jnp
import numpy as np
from jax import lax
from jax.experimental import pallas as pl
from jax.experimental.pallas import tpu as pltpu
from jax.sharding import PartitionSpec as P


def spread_kernel(groups, me_ref, snaps_ref, mask_ref, *refs):
    outs, (held, mask, turned, sems) = refs[:groups], refs[groups:]
    comps, planes, reach = outs[0].shape[:3]
    width = reach - 2
    rows = groups * width
    me = me_ref[0]
    steps = [(c, p) for c in range(comps) for p in range(planes)]
    mask_copy = pltpu.make_async_copy(mask_ref, mask, sems.at[len(steps)])
    mask_copy.start()
    copies = [
        pltpu.make_async_copy(snaps_ref.at[:, c, p], held.at[i], sems.at[i]) for i, (c, p) in enumerate(steps)
    ]
    for copy in copies:
        copy.start()
    edge = jnp.zeros(turned.shape[1:], turned.dtype)
    turned[0] = edge
    turned[rows + 1] = edge
    mask_copy.wait()
    for i, (c, p) in enumerate(steps):
        copies[i].wait()
        values = held[i].astype(jnp.float32) * mask[p].astype(jnp.float32)[None]
        turned[1 : rows + 1] = jnp.swapaxes(values, 0, 1).astype(turned.dtype)
        for m in range(groups):
            outs[m][c, p] = turned[pl.ds((me ^ m) * width, reach)]


def spread(snapshots, free_mask, me, groups):
    members, comps, planes, rows, depth = snapshots.shape
    block = jax.ShapeDtypeStruct((comps, planes, rows // groups + 2, members, depth), snapshots.dtype)
    hbm = pl.BlockSpec(memory_space=pltpu.HBM)
    return pl.pallas_call(
        functools.partial(spread_kernel, groups),
        out_shape=[block] * groups,
        in_specs=[smem_spec(), hbm, hbm],
        out_specs=[vmem_spec()] * groups,
        scratch_shapes=[
            pltpu.VMEM((comps * planes, members, rows, depth), snapshots.dtype),
            pltpu.VMEM(free_mask.shape, free_mask.dtype),
            pltpu.VMEM((rows + 2, members, depth), snapshots.dtype),
            pltpu.SemaphoreType.DMA((comps * planes + 1,)),
        ],
        compiler_params=pltpu.CompilerParams(vmem_limit_bytes=16 * 2**20),
        cost_estimate=pl.CostEstimate(flops=0, bytes_accessed=5 * 2**20, transcendentals=0),
    )(me, snapshots, free_mask)


def stencil_weights(depth):
    mass = {-1: 1.0, 0: 4.0, 1: 1.0}
    stiff = {-1: -1.0, 0: 2.0, 1: -1.0}
    near = np.eye(depth, k=1) + np.eye(depth, k=-1)
    mass_z = 4.0 * np.eye(depth) + near
    stiff_z = 2.0 * np.eye(depth) - near

    def plane(dx):
        blocks = []
        for dy in (-1, 0, 1):
            both = mass[dx] * mass[dy]
            mixed = stiff[dx] * mass[dy] + mass[dx] * stiff[dy]
            blocks.append(np.concatenate([both * mass_z, mixed * mass_z + both * stiff_z], axis=1))
        return np.concatenate(blocks, axis=0)

    return plane(0), plane(1)


def three_rows(block, first, height):
    members, depth = block.shape[-2:]
    return [block[first + dy : first + dy + height].reshape(height * members, depth) for dy in range(3)]


def density_at(label, density_ref, materials):
    density = jnp.zeros(label.shape, jnp.float32)
    for j in range(materials):
        density = density + jnp.where(label == j, density_ref[j] * (1.0 / 216.0), 0.0)
    return density


def put_images(image, label, density, right, start, lanes, count, materials):
    members, depth = image.shape[0], image.shape[1] // 2
    right[pl.ds(start, members), lanes] = (image[:, :depth] * density).astype(right.dtype)
    stiff = image[:, depth:] * (1.0 / 36.0)
    for j in range(materials):
        at = pl.multiple_of((j + 1) * count + start, members)
        right[pl.ds(at, members), lanes] = jnp.where(label == j, stiff, 0.0).astype(right.dtype)


def correlate(left, right):
    return lax.dot_general(left, right, (((1,), (1,)), ((), ())), preferred_element_type=jnp.float32)


def local_kernel(groups, materials, me_ref, density_ref, *refs):
    sources = refs[:groups]
    labels_ref, weights_ref, part_ref, edge_ref, cross_ref, left_ref, near_left, near_right = refs[groups:]
    me = me_ref[0]
    comps, planes, reach, members, depth = sources[0].shape
    width = reach - 2
    half = width // 2
    count = groups * members
    wide = 2 * depth

    @pl.loop(0, comps)
    def _(c):
        for g in range(2):
            first = g * half
            lhs = jnp.concatenate(
                [
                    jnp.concatenate(
                        [piece for p in range(planes) for piece in three_rows(source.at[c, p], first, half)], axis=1
                    )
                    for source in sources
                ],
                axis=0,
            )
            both = jnp.dot(lhs, weights_ref[...], preferred_element_type=jnp.float32)
            edge_ref[c, g] = both[:, g * wide : (g + 1) * wide]
            beside = weights_ref[3 * depth : 6 * depth, :wide]
            cross_ref[c, g] = jnp.dot(
                lhs[:, 3 * g * depth : 3 * (g + 1) * depth], beside, preferred_element_type=jnp.float32
            )
            inner = both[:, (1 - g) * wide : (2 - g) * wide]
            for y in range(half):
                label = labels_ref[1 - g, pl.ds(me * width + first + y, 1), :]
                density = density_at(label, density_ref, materials)
                near = pl.ds(pl.multiple_of(((c * 2 + g) * half + y) * depth, depth), depth)
                edge = pl.ds(pl.multiple_of((c * half + y) * depth, depth), depth)
                for m in range(groups):
                    start = pl.multiple_of((me ^ m) * members, members)
                    near_left[pl.ds(start, members), near] = sources[m][c, 1 - g, first + y + 1]
                    left_ref[g, pl.ds(start, members), edge] = sources[m][c, g, first + y + 1]
                    at = (m * half + y) * members
                    put_images(
                        inner[at : at + members], label, density, near_right, start, near, count, materials
                    )

    part_ref[...] = correlate(near_left[...], near_right[...])


def vmem_spec():
    return pl.BlockSpec(memory_space=pltpu.VMEM)


def smem_spec():
    return pl.BlockSpec(memory_space=pltpu.SMEM)


def pack_kernel(pairs, me_ref, *refs):
    blocks, up_ref, down_ref = refs[:pairs], refs[-2], refs[-1]
    comps, planes, reach, members, depth = blocks[0].shape
    half = (reach - 2) // 2
    for i, block in enumerate(blocks):
        for c in range(comps):
            up_ref[i * comps + c] = block[c, planes - 1, 0 : half + 2]
            down_ref[i * comps + c] = block[c, 0, half : 2 * half + 2]
    if up_ref.shape[0] > pairs * comps:
        labels_ref = refs[pairs]
        for out, plane, first in ((up_ref, planes - 1, 0), (down_ref, 0, half)):
            for y in range(half + 2):
                row = labels_ref[plane, pl.ds(me_ref[0] * 2 * half + first + min(y, half - 1), 1), :]
                out[pairs * comps, y] = jnp.broadcast_to(row, (members, depth)).astype(jnp.float32).astype(out.dtype)


def pack(pair, labels, me):
    comps, planes, reach, members, depth = pair[0].shape
    extra = [] if labels is None else [labels]
    out = jax.ShapeDtypeStruct(
        (len(pair) * comps + len(extra), (reach - 2) // 2 + 2, members, depth), pair[0].dtype
    )
    return pl.pallas_call(
        functools.partial(pack_kernel, len(pair)),
        out_shape=[out, out],
        in_specs=[smem_spec()] + [vmem_spec()] * (len(pair) + len(extra)),
        out_specs=[vmem_spec()] * 2,
        compiler_params=pltpu.CompilerParams(vmem_limit_bytes=16 * 2**20),
        cost_estimate=pl.CostEstimate(flops=0, bytes_accessed=2**20, transcendentals=0),
    )(me, *pair, *extra)


def local_tiles(blocks, labels, density, me):
    groups = len(blocks)
    comps, planes, reach, members, depth = blocks[0].shape
    half = (reach - 2) // 2
    count = groups * members
    columns = (density.shape[0] + 1) * count
    same, beside = stencil_weights(depth)
    weights = jnp.asarray(
        np.concatenate([np.concatenate([same, beside], axis=0), np.concatenate([beside, same], axis=0)], axis=1),
        jnp.bfloat16,
    )
    image = jax.ShapeDtypeStruct((comps, 2, groups * half * members, 2 * depth), jnp.float32)
    return pl.pallas_call(
        functools.partial(local_kernel, groups, density.shape[0]),
        out_shape=[
            jax.ShapeDtypeStruct((count, columns), jnp.float32),
            image,
            image,
            jax.ShapeDtypeStruct((2, count, comps * half * depth), jnp.bfloat16),
        ],
        in_specs=[smem_spec(), smem_spec()] + [vmem_spec()] * (groups + 2),
        out_specs=[vmem_spec()] * 4,
        scratch_shapes=[
            pltpu.VMEM((count, comps * 2 * half * depth), jnp.bfloat16),
            pltpu.VMEM((columns, comps * 2 * half * depth), jnp.bfloat16),
        ],
        compiler_params=pltpu.CompilerParams(vmem_limit_bytes=40 * 2**20),
        cost_estimate=pl.CostEstimate(flops=5 * 10**9, bytes_accessed=12 * 2**20, transcendentals=0),
    )(me, density, *blocks, labels, weights)


def received_at(side, m, groups, comps, c):
    each = groups // len(side)
    return side[m // each].at[(m % each) * comps + c]


def returns_kernel(groups, materials, pairs, me_ref, density_ref, cross_ref, *refs):
    sides = (refs[:pairs], refs[pairs : 2 * pairs])
    below_ref, above_ref, left, right = refs[2 * pairs :]
    me = me_ref[0]
    comps = cross_ref.shape[0]
    reach, members, depth = sides[0][0].shape[1:]
    half = reach - 2
    count = groups * members

    @pl.loop(0, comps)
    def _(c):
        for g in range(2):
            cross = cross_ref[c, g]
            for y in range(half):
                label = sides[g][0][(groups // pairs) * comps, y].astype(jnp.float32)
                density = density_at(label, density_ref, materials)
                lanes = pl.ds(pl.multiple_of((c * half + y) * depth, depth), depth)
                for m in range(groups):
                    start = pl.multiple_of((me ^ m) * members, members)
                    left[g, pl.ds(start, members), lanes] = received_at(sides[g], m, groups, comps, c)[y + 1]
                    at = (m * half + y) * members
                    put_images(
                        cross[at : at + members], label, density, right.at[g], start, lanes, count, materials
                    )

    below_ref[...] = correlate(left[0], right[0])
    above_ref[...] = correlate(left[1], right[1])


def return_tiles(cross, lows, highs, density, me, groups):
    materials = density.shape[0]
    comps = cross.shape[0]
    reach, members, depth = lows[0].shape[1:]
    count = groups * members
    cells = comps * (reach - 2) * depth
    columns = (materials + 1) * count
    part = jax.ShapeDtypeStruct((count, columns), jnp.float32)
    halos = [*lows, *highs]
    return pl.pallas_call(
        functools.partial(returns_kernel, groups, materials, len(lows)),
        out_shape=[part, part],
        in_specs=[smem_spec(), smem_spec()] + [vmem_spec()] * (1 + len(halos)),
        out_specs=[vmem_spec()] * 2,
        scratch_shapes=[
            pltpu.VMEM((2, count, cells), jnp.bfloat16),
            pltpu.VMEM((2, columns, cells), jnp.bfloat16),
        ],
        compiler_params=pltpu.CompilerParams(vmem_limit_bytes=40 * 2**20),
        cost_estimate=pl.CostEstimate(flops=3 * 10**9, bytes_accessed=6 * 2**20, transcendentals=0),
    )(me, density, cross, *halos)


def edge_kernel(groups, materials, pairs, me_ref, density_ref, near_ref, edge_ref, left_ref, *refs):
    sides = (refs[:pairs], refs[pairs : 2 * pairs])
    labels_ref, weights_ref, part_ref, right = refs[2 * pairs :]
    me = me_ref[0]
    comps = edge_ref.shape[0]
    reach, members, depth = sides[0][0].shape[1:]
    half = reach - 2
    width = 2 * half
    count = groups * members

    @pl.loop(0, comps)
    def _(c):
        for g in range(2):
            lhs = jnp.concatenate(
                [
                    jnp.concatenate(three_rows(received_at(sides[g], m, groups, comps, c), 0, half), axis=1)
                    for m in range(groups)
                ],
                axis=0,
            )
            image = edge_ref[c, g] + jnp.dot(lhs, weights_ref[...], preferred_element_type=jnp.float32)
            for y in range(half):
                label = labels_ref[g, pl.ds(me * width + g * half + y, 1), :]
                density = density_at(label, density_ref, materials)
                lanes = pl.ds(pl.multiple_of((c * half + y) * depth, depth), depth)
                for m in range(groups):
                    start = pl.multiple_of((me ^ m) * members, members)
                    at = (m * half + y) * members
                    put_images(
                        image[at : at + members], label, density, right.at[g], start, lanes, count, materials
                    )

    part_ref[...] = near_ref[...] + correlate(left_ref[0], right[0]) + correlate(left_ref[1], right[1])


def combine_kernel(part_ref, below_ref, above_ref, from_below_ref, from_above_ref, slab_ref, wide_ref):
    count = part_ref.shape[0]
    copies = wide_ref.shape[0] // count
    part = part_ref[...]
    slab_ref[...] = part + (from_below_ref[...] + from_above_ref[...])
    total = part + (below_ref[...] + above_ref[...])
    for s in range(count):
        for r in range(copies):
            wide_ref[s * copies + r] = total[s : s + 1]


def combine(part, returns, copies):
    count, columns = part.shape
    return pl.pallas_call(
        combine_kernel,
        out_shape=[
            jax.ShapeDtypeStruct((count, columns), jnp.float32),
            jax.ShapeDtypeStruct((count * copies, 1, columns), jnp.float32),
        ],
        in_specs=[vmem_spec()] * (1 + len(returns)),
        out_specs=[vmem_spec()] * 2,
        compiler_params=pltpu.CompilerParams(vmem_limit_bytes=16 * 2**20),
        cost_estimate=pl.CostEstimate(flops=0, bytes_accessed=2**19, transcendentals=0),
    )(part, *returns)


def edge_tiles(near, edge, left, lows, highs, labels, density, me, groups):
    count, columns = near.shape
    materials = density.shape[0]
    weights = jnp.asarray(stencil_weights(labels.shape[2])[1], jnp.bfloat16)
    part = jax.ShapeDtypeStruct((count, columns), jnp.float32)
    halos = [*lows, *highs]
    return pl.pallas_call(
        functools.partial(edge_kernel, groups, materials, len(lows)),
        out_shape=part,
        in_specs=[smem_spec(), smem_spec()] + [vmem_spec()] * (5 + len(halos)),
        out_specs=vmem_spec(),
        scratch_shapes=[pltpu.VMEM((2, columns, left.shape[2]), jnp.bfloat16)],
        compiler_params=pltpu.CompilerParams(vmem_limit_bytes=40 * 2**20),
        cost_estimate=pl.CostEstimate(flops=5 * 10**9, bytes_accessed=20 * 2**20, transcendentals=0),
    )(me, density, near, edge, left, *halos, labels, weights)


def finish_kernel(count, slab_scale, gram_scale, *refs):
    parts, rows_ref, slab_ref, gram_ref = refs[:-3], refs[-3], refs[-2], refs[-1]
    terms = [p[...] for p in parts]
    while len(terms) > 1:
        terms = [terms[i] + terms[i + 1] for i in range(0, len(terms), 2)]
    slab = terms[0] * slab_scale
    gram = jnp.sum(rows_ref[...], axis=0) * gram_scale
    for j in range(slab.shape[1] // count):
        slab_ref[0, j] = slab[:, j * count : (j + 1) * count]
        gram_ref[j] = gram[:, j * count : (j + 1) * count]


def finish(parts, rows, slab_scale, gram_scale):
    count, columns = parts[0].shape
    blocks = columns // count
    return pl.pallas_call(
        functools.partial(finish_kernel, count, slab_scale, gram_scale),
        out_shape=[
            jax.ShapeDtypeStruct((1, blocks, count, count), jnp.float32),
            jax.ShapeDtypeStruct((blocks, 1, count), jnp.float32),
        ],
        in_specs=[vmem_spec()] * (1 + len(parts)),
        out_specs=[vmem_spec()] * 2,
        compiler_params=pltpu.CompilerParams(vmem_limit_bytes=16 * 2**20),
    )(*parts, rows)


def body(snapshots, labels, free_mask, density):
    groups, slabs = lax.axis_size("snap"), lax.axis_size("space")
    planes, rows, depth = labels.shape
    me = lax.axis_index("snap").astype(jnp.int32).reshape(1)
    with jax.named_scope("spread"):
        mine = spread(snapshots, free_mask, me, groups)
    with jax.named_scope("regroup"):
        blocks = [mine[0]] + [
            lax.ppermute(mine[m], "snap", [(i, i ^ m) for i in range(groups)]) for m in range(1, groups)
        ]
    with jax.named_scope("halo"):
        forward = [(i, i + 1) for i in range(slabs - 1)]
        backward = [(b, a) for a, b in forward]
        lows, highs = [], []
        for start in range(0, groups, 2):
            pair = blocks[start : start + 2]
            if lows:
                pair, *_ = lax.optimization_barrier((pair, sent_up, sent_down))
            sent_up, sent_down = pack(pair, None if lows else labels, me)
            if not lows:
                pair, sent_up, sent_down = lax.optimization_barrier((pair, sent_up, sent_down))
            lows.append(lax.ppermute(sent_up, "space", forward))
            highs.append(lax.ppermute(sent_down, "space", backward))
    with jax.named_scope("local_tiles"):
        near, edge, cross, left = local_tiles(blocks, labels, density, me)
    with jax.named_scope("return_tiles"):
        below, above = return_tiles(cross, lows, highs, density, me, groups)
        from_above = lax.ppermute(below, "space", backward)
        from_below = lax.ppermute(above, "space", forward)
    with jax.named_scope("edge_tiles"):
        part = edge_tiles(near, edge, left, lows, highs, labels, density, me, groups)
    with jax.named_scope("sums"):
        part, wide = combine(part, (below, above, from_below, from_above), groups)
        sent = lax.all_to_all(wide, ("space", "snap"), 0, 0, tiled=True)
        parts = [part] + [
            lax.ppermute(part, "snap", [(i, i ^ m) for i in range(groups)]) for m in range(1, groups)
        ]
        slab_scale = 1.0 / (3.0 * planes * rows * depth)
        slab, gram = finish(parts, sent, slab_scale, slab_scale / slabs)
    return gram, slab


def solution(mesh):
    in_specs = (
        P("snap", None, "space", None, None),
        P("space", None, None),
        P("space", None, None),
        P(),
    )
    out_specs = (P(None, "space", None), P("space", None, None, None))
    return jax.shard_map(body, mesh=mesh, in_specs=in_specs, out_specs=out_specs, check_vma=False)
```

time: 104 us -> 91.2 us (0.88)
  waiting for transfers between devices: 51.5 us -> 34.3 us
  starting transfers between devices: 32 us -> 36.6 us
  local copies, waits for them, and re-layouts: 4.7 us -> 3.1 us
  Pallas kernels: 14.9 us -> 16.1 us
    ppermute x2 -> x6, waiting for transfers between devices: 21.3 us -> 1.87 us  [the longest x2 1.86 us: body(): highs.append(lax.ppermute(sent_down, 'space', backward))]
    ppermute x2 -> x6, starting transfers between devices: 2.86 us -> 8.75 us  [the longest x2 2.7 us: body(): lows.append(lax.ppermute(sent_up, 'space', forward))]
    all_to_all x1, waiting for transfers between devices: 10.6 us -> 5.02 us  [body(): sent = lax.all_to_all(wide, ('space', 'snap'), 0, 0, tiled=True)]
    ppermute x3, waiting for transfers between devices: 0.01 us -> 5.18 us  [body(): lax.ppermute(part, 'snap', [(i, i ^ m) for i in range(groups)])]
    ppermute x3, waiting for transfers between devices: 19.5 us -> 22.2 us  [body(): lax.ppermute(mine[m], 'snap', [(i, i ^ m) for i in range(groups)])]
    pallas_call x2 -> x7, Pallas kernels: 13 us -> 15.1 us  [the longest x1 6.04 us: local_tiles(): pl.pallas_call(functools.partial(local_kernel, groups, density.shape[0]),...]
    all_to_all x1, starting transfers between devices: 17.5 us -> 15.8 us  [body(): sent = lax.all_to_all(wide, ('space', 'snap'), 0, 0, tiled=True)]
    unnamed x19 -> x14, local copies, waits for them, and re-layouts: 3.61 us -> 3.1 us
  transfers between devices with their start and end apart: 9 -> 13, of which waited for: 5 -> 6; matrix products, arithmetic and copies ran while one was open for 1% -> 0% of each run, Pallas kernels for 0% -> 11%
where the time goes in v2:
time: 91.2 us; the launch traced here: 90.8 us
  starting transfers between devices  36.6 us (40%)
  waiting for transfers between devices  34.3 us (38%)
  Pallas kernels  16.1 us (18%)
  local copies, waits for them, and re-layouts  3.1 us (3%)
    ppermute x3, waiting for transfers between devices, body(): lax.ppermute(mine[m], 'snap', [(i, i ^ m) for i in range(groups)])  22.2 us
    all_to_all x1, starting transfers between devices, body(): sent = lax.all_to_all(wide, ('space', 'snap'), 0, 0, tiled=True)  15.8 us
    ppermute x3, starting transfers between devices, body(): lax.ppermute(mine[m], 'snap', [(i, i ^ m) for i in range(groups)])  6.56 us
    pallas_call x1, Pallas kernels, local_tiles(): pl.pallas_call(functools.partial(local_kernel, groups, density.shape[0]),...  6.04 us
    ppermute x3, starting transfers between devices, body(): lax.ppermute(part, 'snap', [(i, i ^ m) for i in range(groups)])  5.47 us
    ppermute x3, waiting for transfers between devices, body(): lax.ppermute(part, 'snap', [(i, i ^ m) for i in range(groups)])  5.18 us
    all_to_all x1, waiting for transfers between devices, body(): sent = lax.all_to_all(wide, ('space', 'snap'), 0, 0, tiled=True)  5.02 us
    pallas_call x1, Pallas kernels, edge_tiles(): pl.pallas_call(functools.partial(edge_kernel, groups, materials, len(lows...  3.94 us
  transfers between devices with their start and end apart: 13, of which 6 were waited for; matrix products, arithmetic and copies ran while one was open for 0% of the time, Pallas kernels for 11%

profile of v2, /device:TPU:1, one launch (start us, length us, event | category | flops | bytes accessed | tf_op | source)
XLA Modules:
  0.0 90.8 jit_solution(5984881233225103572)
XLA Ops:
  0.6 0.0 copy-start.4
  0.6 0.0 copy-start
  0.7 1.4 %copy-done = bf16[16,3,2,64,128]{4,3,2,1,0:T(8,128)(2,1)S(1)} copy-done((bf16[16,3,2,64,128]{4,3,2,1,0:T(8,128)(2,1)S(1)}, bf16[16,3,2,64,128]{4,3,2,1,0:T(8,128)(2,1)}, u32[]{:S(2)}) %copy-start) | copy-done | bytes 1572888
  2.1 0.0 copy-start.1
  2.1 0.8 copy-done.1
  2.9 0.0 copy-start.3
  2.9 0.0 copy-start.5
  2.9 1.3 %spread.1 = (bf16[3,2,18,16,128]{4,3,2,1,0:T(8,128)(2,1)S(1)}, bf16[3,2,18,16,128]{4,3,2,1,0:T(8,128)(2,1)S(1)}, bf16[3,2,18,16,128]{4,3,2,1,0:T(8,128)(2,1)S(1)}, bf16[3,2,18,16,128]{4,3,2,1,0:T(8,128)(2,1)S(1)}) custom-call(s32[1]{0:T(128)} %bitcast.me_ref, bf16[16,3,2,64,128]{4,3,2,1,0:T(8,128)(2,1)S(1)} %copy-done, s32[2,64,128]{2,1,0:T(8,128)S(1)} %copy-done.1), custom_call_target="tpu_custom_call" | custom-call | bytes 5242880 | tf_op jit(solution)/shard_map/spread/pallas_call | solution.py:42
  4.2 3.3 %collective-permute-start = (bf16[3,2,18,16,128]{4,3,2,1,0:T(8,128)(2,1)S(1)}, bf16[3,2,18,16,128]{4,3,2,1,0:T(8,128)(2,1)S(1)}, u32[]{:S(2)}, u32[]{:S(2)}) collective-permute-start(bf16[3,2,18,16,128]{4,3,2,1,0:T(8,128)(2,1)S(1)} %get-tuple-element.25), channel_id=1, source_target_pairs={{0,1},{1,0},{2,3},{3,2},{4,5},{5,4},{6,7},{7,6},{8,9},{9,8},{10,11... | collective-permute-start | bytes 1327112 | tf_op jit(solution)/shard_map/regroup/ppermute | solution.py:389
  7.5 1.2 %collective-permute-start.1 = (bf16[3,2,18,16,128]{4,3,2,1,0:T(8,128)(2,1)S(1)}, bf16[3,2,18,16,128]{4,3,2,1,0:T(8,128)(2,1)S(1)}, u32[]{:S(2)}, u32[]{:S(2)}) collective-permute-start(bf16[3,2,18,16,128]{4,3,2,1,0:T(8,128)(2,1)S(1)} %get-tuple-element.26), channel_id=1, source_target_pairs={{0,2},{1,3},{2,0},{3,1},{4,6},{5,7},{6,4},{7,5},{8,10},{9,11},{10,... | collective-permute-start | bytes 1327112 | tf_op jit(solution)/shard_map/regroup/ppermute | solution.py:389
  8.7 2.0 %collective-permute-start.2 = (bf16[3,2,18,16,128]{4,3,2,1,0:T(8,128)(2,1)S(1)}, bf16[3,2,18,16,128]{4,3,2,1,0:T(8,128)(2,1)S(1)}, u32[]{:S(2)}, u32[]{:S(2)}) collective-permute-start(bf16[3,2,18,16,128]{4,3,2,1,0:T(8,128)(2,1)S(1)} %get-tuple-element.27), channel_id=1, source_target_pairs={{0,3},{1,2},{2,1},{3,0},{4,7},{5,6},{6,5},{7,4},{8,11},{9,10},{10,... | collective-permute-start | bytes 1327112 | tf_op jit(solution)/shard_map/regroup/ppermute | solution.py:389
  10.8 0.0 collective-permute-done.refs_1_
  10.8 0.0 copy-start.2
  10.8 0.8 copy-done.2
  11.7 1.4 %collective-permute-start.3 = (bf16[7,10,16,128]{3,2,1,0:T(8,128)(2,1)S(1)}, bf16[7,10,16,128]{3,2,1,0:T(8,128)(2,1)S(1)}, u32[]{:S(2)}, u32[]{:S(2)}) collective-permute-start(bf16[7,10,16,128]{3,2,1,0:T(8,128)(2,1)S(1)} %get-tuple-element.33), channel_id=1, source_target_pairs={{0,4},{4,8},{8,12},{12,16},{16,20},{20,24},{24,28},{28,32},{32,36}... | collective-permute-start | bytes 860168 | tf_op jit(solution)/shard_map/halo/ppermute | solution.py:402
  13.1 1.3 %collective-permute-start.5 = (bf16[7,10,16,128]{3,2,1,0:T(8,128)(2,1)S(1)}, bf16[7,10,16,128]{3,2,1,0:T(8,128)(2,1)S(1)}, u32[]{:S(2)}, u32[]{:S(2)}) collective-permute-start(bf16[7,10,16,128]{3,2,1,0:T(8,128)(2,1)S(1)} %get-tuple-element.34), channel_id=1, source_target_pairs={{4,0},{8,4},{12,8},{16,12},{20,16},{24,20},{28,24},{32,28},{36,32}... | collective-permute-start | bytes 860168 | tf_op jit(solution)/shard_map/halo/ppermute | solution.py:403
  14.4 6.4 %collective-permute-done.1.refs_2_.refs_0_ = bf16[3,2,18,16,128]{4,3,2,1,0:T(8,128)(2,1)S(1)} collective-permute-done((bf16[3,2,18,16,128]{4,3,2,1,0:T(8,128)(2,1)S(1)}, bf16[3,2,18,16,128]{4,3,2,1,0:T(8,128)(2,1)S(1)}, u32[]{:S(2)}, u32[]{:S(2)}) %collective-permute-start.1) | collective-permute-done | bytes 442400 | tf_op jit(solution)/shard_map/regroup/ppermute | solution.py:389
  20.8 15.8 %collective-permute-done.2.refs_3_.refs_1_ = bf16[3,2,18,16,128]{4,3,2,1,0:T(8,128)(2,1)S(1)} collective-permute-done((bf16[3,2,18,16,128]{4,3,2,1,0:T(8,128)(2,1)S(1)}, bf16[3,2,18,16,128]{4,3,2,1,0:T(8,128)(2,1)S(1)}, u32[]{:S(2)}, u32[]{:S(2)}) %collective-permute-start.2) | collective-permute-done | bytes 442400 | tf_op jit(solution)/shard_map/regroup/ppermute | solution.py:389
  36.6 1.3 %collective-permute-start.4 = (bf16[6,10,16,128]{3,2,1,0:T(8,128)(2,1)S(1)}, bf16[6,10,16,128]{3,2,1,0:T(8,128)(2,1)S(1)}, u32[]{:S(2)}, u32[]{:S(2)}) collective-permute-start(bf16[6,10,16,128]{3,2,1,0:T(8,128)(2,1)S(1)} %get-tuple-element.37), channel_id=1, source_target_pairs={{0,4},{4,8},{8,12},{12,16},{16,20},{20,24},{24,28},{28,32},{32,36}... | collective-permute-start | bytes 737288 | tf_op jit(solution)/shard_map/halo/ppermute | solution.py:402
  37.9 1.3 %collective-permute-start.6 = (bf16[6,10,16,128]{3,2,1,0:T(8,128)(2,1)S(1)}, bf16[6,10,16,128]{3,2,1,0:T(8,128)(2,1)S(1)}, u32[]{:S(2)}, u32[]{:S(2)}) collective-permute-start(bf16[6,10,16,128]{3,2,1,0:T(8,128)(2,1)S(1)} %get-tuple-element.38), channel_id=1, source_target_pairs={{4,0},{8,4},{12,8},{16,12},{20,16},{24,20},{28,24},{32,28},{36,32}... | collective-permute-start | bytes 737288 | tf_op jit(solution)/shard_map/halo/ppermute | solution.py:403
  39.2 0.0 copy-done.4
  39.2 0.0 copy-done.3
  39.2 0.0 copy-done.5
  39.2 6.0 %local_tiles.1 = (f32[64,256]{1,0:T(8,128)S(1)}, f32[3,2,512,256]{3,2,1,0:T(8,128)S(1)}, f32[3,2,512,256]{3,2,1,0:T(8,128)S(1)}, bf16[2,64,3072]{2,1,0:T(8,128)(2,1)S(1)}) custom-call(s32[1]{0:T(128)} %bitcast.me_ref, f32[3]{0:T(128)S(1)} %copy-done.4, bf16[3,2,18,16,128]{4,3,2,1,0:T(8,128)(2,1)S(1)} %get-tuple-element.24.refs_0_, ...), custom_call_target="tpu_custom_call" | custom-call | flops 5000000000 | bytes 12582912 | tf_op jit(solution)/shard_map/local_tiles/pallas_call | solution.py:200
  45.3 0.0 collective-permute-done.4.refs_1_
  45.3 1.9 %collective-permute-done.6.refs_3_ = bf16[6,10,16,128]{3,2,1,0:T(8,128)(2,1)S(1)} collective-permute-done((bf16[6,10,16,128]{3,2,1,0:T(8,128)(2,1)S(1)}, bf16[6,10,16,128]{3,2,1,0:T(8,128)(2,1)S(1)}, u32[]{:S(2)}, u32[]{:S(2)}) %collective-permute-start.6) | collective-permute-done | bytes 245792 | tf_op jit(solution)/shard_map/halo/ppermute | solution.py:403
  47.2 0.0 collective-permute-done.3.refs_0_
  47.2 0.0 collective-permute-done.5.refs_2_
  47.2 0.0 copy-start.6
  47.2 2.9 %return_tiles.1 = (f32[64,256]{1,0:T(8,128)S(1)}, f32[64,256]{1,0:T(8,128)S(1)}) custom-call(s32[1]{0:T(128)} %bitcast.me_ref, f32[3]{0:T(128)S(1)} %copy-done.4, f32[3,2,512,256]{3,2,1,0:T(8,128)S(1)} %get-tuple-element.39.cross_ref, bf16[7,10,16,128]{3,2,1,0:T(8,128)(2,1)S(1)} %collective-permute-done.3.refs_0_, ...), custom_call_target="tpu_custom_call" | custom-call | flops 3000000000 | bytes 6291456 | tf_op jit(solution)/shard_map/return_tiles/pallas_call | solution.py:262
  50.1 2.2 %collective-permute-start.7 = (f32[64,256]{1,0:T(8,128)S(1)}, f32[64,256]{1,0:T(8,128)S(1)}, u32[]{:S(2)}, u32[]{:S(2)}) collective-permute-start(f32[64,256]{1,0:T(8,128)S(1)} %get-tuple-element.41.above_ref), channel_id=1, source_target_pairs={{0,4},{4,8},{8,12},{12,16},{16,20},{20,24},{24,28},{28,32},{32,36}... | collective-permute-start | bytes 196616 | tf_op jit(solution)/shard_map/return_tiles/ppermute | solution.py:409
  52.3 1.3 %collective-permute-start.8 = (f32[64,256]{1,0:T(8,128)S(1)}, f32[64,256]{1,0:T(8,128)S(1)}, u32[]{:S(2)}, u32[]{:S(2)}) collective-permute-start(f32[64,256]{1,0:T(8,128)S(1)} %get-tuple-element.40.below_ref), channel_id=1, source_target_pairs={{4,0},{8,4},{12,8},{16,12},{20,16},{24,20},{28,24},{32,28},{36,32}... | collective-permute-start | bytes 196616 | tf_op jit(solution)/shard_map/return_tiles/ppermute | solution.py:408
  53.6 0.0 copy-done.6
  53.6 3.9 %edge_tiles.1.part_ref = f32[64,256]{1,0:T(8,128)S(1)} custom-call(s32[1]{0:T(128)} %bitcast.me_ref, f32[3]{0:T(128)S(1)} %copy-done.4, f32[64,256]{1,0:T(8,128)S(1)} %get-tuple-element.28.near_ref, f32[3,2,512,256]{3,2,1,0:T(8,128)S(1)} %get-tuple-element.29.edge_ref, bf16[2,64,3072]{2,1,0:T(8,128)(2,1)S(1)} %get-tuple-element.30.left_ref, ...), custom_call_target="tpu_custom_call" | custom-call | flops 5000000000 | bytes 20971520 | tf_op jit(solution)/shard_map/edge_tiles/pallas_call | solution.py:343
  57.5 0.0 collective-permute-done.7.from_below_ref
  57.5 0.0 collective-permute-done.8.from_above_ref
  57.5 0.8 sums.2
  58.3 15.8 %all-to-all-start = ((f32[256,1,256]{2,1,0:T(1,128)}), f32[256,1,256]{2,1,0:T(1,128)S(1)}, u32[]{:S(2)}, u32[]{:S(2)}) async-start(f32[256,1,256]{2,1,0:T(1,128)} %get-tuple-element.43), calls=%async_computation | async-start | bytes 524288 | tf_op jit(solution)/shard_map/sums/all_to_all | solution.py:414
  74.2 2.2 %collective-permute-start.9 = (f32[64,256]{1,0:T(8,128)S(1)}, f32[64,256]{1,0:T(8,128)S(1)}, u32[]{:S(2)}, u32[]{:S(2)}) collective-permute-start(f32[64,256]{1,0:T(8,128)S(1)} %get-tuple-element.42.refs_0_), channel_id=1, source_target_pairs={{0,1},{1,0},{2,3},{3,2},{4,5},{5,4},{6,7},{7,6},{8,9},{9,8},{10,11... | collective-permute-start | bytes 196616 | tf_op jit(solution)/shard_map/sums/ppermute | solution.py:416
  76.4 1.1 %collective-permute-start.10 = (f32[64,256]{1,0:T(8,128)S(1)}, f32[64,256]{1,0:T(8,128)S(1)}, u32[]{:S(2)}, u32[]{:S(2)}) collective-permute-start(f32[64,256]{1,0:T(8,128)S(1)} %get-tuple-element.42.refs_0_), channel_id=1, source_target_pairs={{0,2},{1,3},{2,0},{3,1},{4,6},{5,7},{6,4},{7,5},{8,10},{9,11},{10,... | collective-permute-start | bytes 196616 | tf_op jit(solution)/shard_map/sums/ppermute | solution.py:416
  77.5 2.1 %collective-permute-start.11 = (f32[64,256]{1,0:T(8,128)S(1)}, f32[64,256]{1,0:T(8,128)S(1)}, u32[]{:S(2)}, u32[]{:S(2)}) collective-permute-start(f32[64,256]{1,0:T(8,128)S(1)} %get-tuple-element.42.refs_0_), channel_id=1, source_target_pairs={{0,3},{1,2},{2,1},{3,0},{4,7},{5,6},{6,5},{7,4},{8,11},{9,10},{10,... | collective-permute-start | bytes 196616 | tf_op jit(solution)/shard_map/sums/ppermute | solution.py:416
  79.6 0.0 collective-permute-done.9.refs_1_
  79.6 2.4 %collective-permute-done.10.refs_2_ = f32[64,256]{1,0:T(8,128)S(1)} collective-permute-done((f32[64,256]{1,0:T(8,128)S(1)}, f32[64,256]{1,0:T(8,128)S(1)}, u32[]{:S(2)}, u32[]{:S(2)}) %collective-permute-start.10) | collective-permute-done | bytes 65568 | tf_op jit(solution)/shard_map/sums/ppermute | solution.py:416
  82.0 2.8 %collective-permute-done.11.refs_3_ = f32[64,256]{1,0:T(8,128)S(1)} collective-permute-done((f32[64,256]{1,0:T(8,128)S(1)}, f32[64,256]{1,0:T(8,128)S(1)}, u32[]{:S(2)}, u32[]{:S(2)}) %collective-permute-start.11) | collective-permute-done | bytes 65568 | tf_op jit(solution)/shard_map/sums/ppermute | solution.py:416
  84.8 5.0 %all-to-all-done.refs_4_ = f32[256,1,256]{2,1,0:T(1,128)S(1)} async-done(((f32[256,1,256]{2,1,0:T(1,128)}), f32[256,1,256]{2,1,0:T(1,128)S(1)}, u32[]{:S(2)}, u32[]{:S(2)}) %all-to-all-start) | async-done | bytes 262176 | tf_op jit(solution)/shard_map/sums/all_to_all | solution.py:414
  89.8 1.0 %sums.3 = (f32[1,4,64,64]{3,2,1,0:T(8,128)}, f32[4,1,64]{2,1,0:T(1,128)}) custom-call(f32[64,256]{1,0:T(8,128)S(1)} %get-tuple-element.42.refs_0_, f32[64,256]{1,0:T(8,128)S(1)} %collective-permute-done.9.refs_1_, f32[64,256]{1,0:T(8,128)S(1)} %collective-permute-done.10.refs_2_, f32[64,256]{1,0:T(8,128)S(1)} %collective-permute-done.11.refs_3_, ...), custom_call_target="tpu_custom_call" | custom-call | tf_op jit(solution)/shard_map/sums/pallas_call | solution.py:369
  (2 shorter events, 0.1 us)
Async XLA Ops:
  0.6 38.6 %copy-start.4 = (f32[3]{0:T(128)S(1)}, f32[3]{0:T(128)}, u32[]{:S(2)}) copy-start(f32[3]{0:T(128)} %density_ref.5) | copy-start | bytes 40
  0.6 1.4 %copy-start = (bf16[16,3,2,64,128]{4,3,2,1,0:T(8,128)(2,1)S(1)}, bf16[16,3,2,64,128]{4,3,2,1,0:T(8,128)(2,1)}, u32[]{:S(2)}) copy-start(bf16[16,3,2,64,128]{4,3,2,1,0:T(8,128)(2,1)} %snaps_ref.1) | copy-start | bytes 4718596
  2.1 0.8 copy-start.1
  2.9 36.3 %copy-start.3 = (s32[2,64,128]{2,1,0:T(8,128)S(1)}, s32[2,64,128]{2,1,0:T(8,128)}, u32[]{:S(2)}) copy-start(s32[2,64,128]{2,1,0:T(8,128)} %refs_4_.3) | copy-start | bytes 196612
  2.9 36.3 %copy-start.5 = (bf16[768,512]{1,0:T(8,128)(2,1)S(1)}, bf16[768,512]{1,0:T(8,128)(2,1)}, u32[]{:S(2)}) copy-start(bf16[768,512]{1,0:T(8,128)(2,1)} %constant.8.clone.refs_5_) | copy-start | bytes 2359300
  4.2 6.6 %collective-permute-start = (bf16[3,2,18,16,128]{4,3,2,1,0:T(8,128)(2,1)S(1)}, bf16[3,2,18,16,128]{4,3,2,1,0:T(8,128)(2,1)S(1)}, u32[]{:S(2)}, u32[]{:S(2)}) collective-permute-start(bf16[3,2,18,16,128]{4,3,2,1,0:T(8,128)(2,1)S(1)} %get-tuple-element.25), channel_id=1, source_target_pairs={{0,1},{1,0},{2,3},{3,2},{4,5},{5,4},{6,7},{7,6},{8,9},{9,8},{10,11... | collective-permute-start | bytes 1327112 | tf_op jit(solution)/shard_map/regroup/ppermute | solution.py:389
  7.5 13.2 %collective-permute-start.1 = (bf16[3,2,18,16,128]{4,3,2,1,0:T(8,128)(2,1)S(1)}, bf16[3,2,18,16,128]{4,3,2,1,0:T(8,128)(2,1)S(1)}, u32[]{:S(2)}, u32[]{:S(2)}) collective-permute-start(bf16[3,2,18,16,128]{4,3,2,1,0:T(8,128)(2,1)S(1)} %get-tuple-element.26), channel_id=1, source_target_pairs={{0,2},{1,3},{2,0},{3,1},{4,6},{5,7},{6,4},{7,5},{8,10},{9,11},{10,... | collective-permute-start | bytes 1327112 | tf_op jit(solution)/shard_map/regroup/ppermute | solution.py:389
  8.7 27.8 %collective-permute-start.2 = (bf16[3,2,18,16,128]{4,3,2,1,0:T(8,128)(2,1)S(1)}, bf16[3,2,18,16,128]{4,3,2,1,0:T(8,128)(2,1)S(1)}, u32[]{:S(2)}, u32[]{:S(2)}) collective-permute-start(bf16[3,2,18,16,128]{4,3,2,1,0:T(8,128)(2,1)S(1)} %get-tuple-element.27), channel_id=1, source_target_pairs={{0,3},{1,2},{2,1},{3,0},{4,7},{5,6},{6,5},{7,4},{8,11},{9,10},{10,... | collective-permute-start | bytes 1327112 | tf_op jit(solution)/shard_map/regroup/ppermute | solution.py:389
  10.8 0.8 copy-start.2
  11.7 35.5 %collective-permute-start.3 = (bf16[7,10,16,128]{3,2,1,0:T(8,128)(2,1)S(1)}, bf16[7,10,16,128]{3,2,1,0:T(8,128)(2,1)S(1)}, u32[]{:S(2)}, u32[]{:S(2)}) collective-permute-start(bf16[7,10,16,128]{3,2,1,0:T(8,128)(2,1)S(1)} %get-tuple-element.33), channel_id=1, source_target_pairs={{0,4},{4,8},{8,12},{12,16},{16,20},{20,24},{24,28},{28,32},{32,36}... | collective-permute-start | bytes 860168 | tf_op jit(solution)/shard_map/halo/ppermute | solution.py:402
  13.1 34.1 %collective-permute-start.5 = (bf16[7,10,16,128]{3,2,1,0:T(8,128)(2,1)S(1)}, bf16[7,10,16,128]{3,2,1,0:T(8,128)(2,1)S(1)}, u32[]{:S(2)}, u32[]{:S(2)}) collective-permute-start(bf16[7,10,16,128]{3,2,1,0:T(8,128)(2,1)S(1)} %get-tuple-element.34), channel_id=1, source_target_pairs={{4,0},{8,4},{12,8},{16,12},{20,16},{24,20},{28,24},{32,28},{36,32}... | collective-permute-start | bytes 860168 | tf_op jit(solution)/shard_map/halo/ppermute | solution.py:403
  36.6 8.7 %collective-permute-start.4 = (bf16[6,10,16,128]{3,2,1,0:T(8,128)(2,1)S(1)}, bf16[6,10,16,128]{3,2,1,0:T(8,128)(2,1)S(1)}, u32[]{:S(2)}, u32[]{:S(2)}) collective-permute-start(bf16[6,10,16,128]{3,2,1,0:T(8,128)(2,1)S(1)} %get-tuple-element.37), channel_id=1, source_target_pairs={{0,4},{4,8},{8,12},{12,16},{16,20},{20,24},{24,28},{28,32},{32,36}... | collective-permute-start | bytes 737288 | tf_op jit(solution)/shard_map/halo/ppermute | solution.py:402
  37.9 9.2 %collective-permute-start.6 = (bf16[6,10,16,128]{3,2,1,0:T(8,128)(2,1)S(1)}, bf16[6,10,16,128]{3,2,1,0:T(8,128)(2,1)S(1)}, u32[]{:S(2)}, u32[]{:S(2)}) collective-permute-start(bf16[6,10,16,128]{3,2,1,0:T(8,128)(2,1)S(1)} %get-tuple-element.38), channel_id=1, source_target_pairs={{4,0},{8,4},{12,8},{16,12},{20,16},{24,20},{28,24},{32,28},{36,32}... | collective-permute-start | bytes 737288 | tf_op jit(solution)/shard_map/halo/ppermute | solution.py:403
  47.2 6.4 %copy-start.6 = (bf16[384,256]{1,0:T(8,128)(2,1)S(1)}, bf16[384,256]{1,0:T(8,128)(2,1)}, u32[]{:S(2)}) copy-start(bf16[384,256]{1,0:T(8,128)(2,1)} %constant.9.clone.refs_5_) | copy-start | bytes 589828
  50.1 7.4 %collective-permute-start.7 = (f32[64,256]{1,0:T(8,128)S(1)}, f32[64,256]{1,0:T(8,128)S(1)}, u32[]{:S(2)}, u32[]{:S(2)}) collective-permute-start(f32[64,256]{1,0:T(8,128)S(1)} %get-tuple-element.41.above_ref), channel_id=1, source_target_pairs={{0,4},{4,8},{8,12},{12,16},{16,20},{20,24},{24,28},{28,32},{32,36}... | collective-permute-start | bytes 196616 | tf_op jit(solution)/shard_map/return_tiles/ppermute | solution.py:409
  52.3 5.3 %collective-permute-start.8 = (f32[64,256]{1,0:T(8,128)S(1)}, f32[64,256]{1,0:T(8,128)S(1)}, u32[]{:S(2)}, u32[]{:S(2)}) collective-permute-start(f32[64,256]{1,0:T(8,128)S(1)} %get-tuple-element.40.below_ref), channel_id=1, source_target_pairs={{4,0},{8,4},{12,8},{16,12},{20,16},{24,20},{28,24},{32,28},{36,32}... | collective-permute-start | bytes 196616 | tf_op jit(solution)/shard_map/return_tiles/ppermute | solution.py:408
  58.3 31.5 %all-to-all-start = ((f32[256,1,256]{2,1,0:T(1,128)}), f32[256,1,256]{2,1,0:T(1,128)S(1)}, u32[]{:S(2)}, u32[]{:S(2)}) async-start(f32[256,1,256]{2,1,0:T(1,128)} %get-tuple-element.43), calls=%async_computation | async-start | bytes 524288 | tf_op jit(solution)/shard_map/sums/all_to_all | solution.py:414
  74.2 5.5 %collective-permute-start.9 = (f32[64,256]{1,0:T(8,128)S(1)}, f32[64,256]{1,0:T(8,128)S(1)}, u32[]{:S(2)}, u32[]{:S(2)}) collective-permute-start(f32[64,256]{1,0:T(8,128)S(1)} %get-tuple-element.42.refs_0_), channel_id=1, source_target_pairs={{0,1},{1,0},{2,3},{3,2},{4,5},{5,4},{6,7},{7,6},{8,9},{9,8},{10,11... | collective-permute-start | bytes 196616 | tf_op jit(solution)/shard_map/sums/ppermute | solution.py:416
  76.4 5.6 %collective-permute-start.10 = (f32[64,256]{1,0:T(8,128)S(1)}, f32[64,256]{1,0:T(8,128)S(1)}, u32[]{:S(2)}, u32[]{:S(2)}) collective-permute-start(f32[64,256]{1,0:T(8,128)S(1)} %get-tuple-element.42.refs_0_), channel_id=1, source_target_pairs={{0,2},{1,3},{2,0},{3,1},{4,6},{5,7},{6,4},{7,5},{8,10},{9,11},{10,... | collective-permute-start | bytes 196616 | tf_op jit(solution)/shard_map/sums/ppermute | solution.py:416
  77.5 7.3 %collective-permute-start.11 = (f32[64,256]{1,0:T(8,128)S(1)}, f32[64,256]{1,0:T(8,128)S(1)}, u32[]{:S(2)}, u32[]{:S(2)}) collective-permute-start(f32[64,256]{1,0:T(8,128)S(1)} %get-tuple-element.42.refs_0_), channel_id=1, source_target_pairs={{0,3},{1,2},{2,1},{3,0},{4,7},{5,6},{6,5},{7,4},{8,11},{9,10},{10,... | collective-permute-start | bytes 196616 | tf_op jit(solution)/shard_map/sums/ppermute | solution.py:416

commit v3 on v2

--- a/solution.py
+++ b/solution.py
@@ -9,48 +9,39 @@
 from jax.sharding import PartitionSpec as P
 
 
-def spread_kernel(groups, me_ref, snaps_ref, mask_ref, *refs):
-    outs, (held, mask, turned, sems) = refs[:groups], refs[groups:]
-    comps, planes, reach = outs[0].shape[:3]
-    width = reach - 2
-    rows = groups * width
+def spread_kernel(groups, width, me_ref, snaps_ref, mask_ref, *refs):
+    outs, turned = refs[:groups], refs[groups]
+    rows = snaps_ref.shape[3]
     me = me_ref[0]
-    steps = [(c, p) for c in range(comps) for p in range(planes)]
-    mask_copy = pltpu.make_async_copy(mask_ref, mask, sems.at[len(steps)])
-    mask_copy.start()
-    copies = [
-        pltpu.make_async_copy(snaps_ref.at[:, c, p], held.at[i], sems.at[i]) for i, (c, p) in enumerate(steps)
-    ]
-    for copy in copies:
-        copy.start()
+    mask = mask_ref[0].astype(jnp.float32)
+    values = snaps_ref[:, 0, 0].astype(jnp.float32) * mask[None]
     edge = jnp.zeros(turned.shape[1:], turned.dtype)
     turned[0] = edge
     turned[rows + 1] = edge
-    mask_copy.wait()
-    for i, (c, p) in enumerate(steps):
-        copies[i].wait()
-        values = held[i].astype(jnp.float32) * mask[p].astype(jnp.float32)[None]
-        turned[1 : rows + 1] = jnp.swapaxes(values, 0, 1).astype(turned.dtype)
-        for m in range(groups):
-            outs[m][c, p] = turned[pl.ds((me ^ m) * width, reach)]
+    turned[1 : rows + 1] = jnp.swapaxes(values, 0, 1).astype(turned.dtype)
+    for m in range(groups):
+        outs[m][0, 0] = turned[pl.ds((me ^ m) * width, width + 2)]
 
 
 def spread(snapshots, free_mask, me, groups):
     members, comps, planes, rows, depth = snapshots.shape
-    block = jax.ShapeDtypeStruct((comps, planes, rows // groups + 2, members, depth), snapshots.dtype)
-    hbm = pl.BlockSpec(memory_space=pltpu.HBM)
-    return pl.pallas_call(
-        functools.partial(spread_kernel, groups),
+    width = rows // groups
+    block = jax.ShapeDtypeStruct((comps, planes, width + 2, members, depth), snapshots.dtype)
+    out_spec = pl.BlockSpec((1, 1, width + 2, members, depth), lambda c, p, me: (c, p, 0, 0, 0))
+    return pl.pallas_call(
+        functools.partial(spread_kernel, groups, width),
         out_shape=[block] * groups,
-        in_specs=[smem_spec(), hbm, hbm],
-        out_specs=[vmem_spec()] * groups,
-        scratch_shapes=[
-            pltpu.VMEM((comps * planes, members, rows, depth), snapshots.dtype),
-            pltpu.VMEM(free_mask.shape, free_mask.dtype),
-            pltpu.VMEM((rows + 2, members, depth), snapshots.dtype),
-            pltpu.SemaphoreType.DMA((comps * planes + 1,)),
-        ],
-        compiler_params=pltpu.CompilerParams(vmem_limit_bytes=16 * 2**20),
+        grid_spec=pltpu.PrefetchScalarGridSpec(
+            num_scalar_prefetch=1,
+            grid=(comps, planes),
+            in_specs=[
+                pl.BlockSpec((members, 1, 1, rows, depth), lambda c, p, me: (0, c, p, 0, 0)),
+                pl.BlockSpec((1, rows, depth), lambda c, p, me: (p, 0, 0)),
+            ],
+            out_specs=[out_spec] * groups,
+            scratch_shapes=[pltpu.VMEM((rows + 2, members, depth), snapshots.dtype)],
+        ),
+        compiler_params=pltpu.CompilerParams(vmem_limit_bytes=32 * 2**20),
         cost_estimate=pl.CostEstimate(flops=0, bytes_accessed=5 * 2**20, transcendentals=0),
     )(me, snapshots, free_mask)
 
@@ -154,18 +145,19 @@
 
 
 def pack_kernel(pairs, me_ref, *refs):
-    blocks, up_ref, down_ref = refs[:pairs], refs[-2], refs[-1]
+    blocks, outs = refs[:pairs], refs[-2:]
     comps, planes, reach, members, depth = blocks[0].shape
     half = (reach - 2) // 2
-    for i, block in enumerate(blocks):
-        for c in range(comps):
-            up_ref[i * comps + c] = block[c, planes - 1, 0 : half + 2]
-            down_ref[i * comps + c] = block[c, 0, half : 2 * half + 2]
-    if up_ref.shape[0] > pairs * comps:
-        labels_ref = refs[pairs]
-        for out, plane, first in ((up_ref, planes - 1, 0), (down_ref, 0, half)):
+    for out, up in ((outs[0], 1 - me_ref[1]), (outs[1], me_ref[1])):
+        first = (1 - up) * half
+        for i, block in enumerate(blocks):
+            for c in range(comps):
+                out[i * comps + c] = block[c, up * (planes - 1), pl.ds(first, half + 2)]
+        if out.shape[0] > pairs * comps:
+            labels_ref = refs[pairs]
             for y in range(half + 2):
-                row = labels_ref[plane, pl.ds(me_ref[0] * 2 * half + first + min(y, half - 1), 1), :]
+                at = me_ref[0] * 2 * half + first + min(y, half - 1)
+                row = labels_ref[up * (planes - 1), pl.ds(at, 1), :]
                 out[pairs * comps, y] = jnp.broadcast_to(row, (members, depth)).astype(jnp.float32).astype(out.dtype)
 
 
@@ -216,9 +208,12 @@
     )(me, density, *blocks, labels, weights)
 
 
-def received_at(side, m, groups, comps, c):
-    each = groups // len(side)
-    return side[m // each].at[(m % each) * comps + c]
+def received_at(side, m, comps, c):
+    part = 0
+    while m >= side[part].shape[0] // comps:
+        m -= side[part].shape[0] // comps
+        part += 1
+    return side[part].at[m * comps + c]
 
 
 def returns_kernel(groups, materials, pairs, me_ref, density_ref, cross_ref, *refs):
@@ -232,18 +227,19 @@
 
     @pl.loop(0, comps)
     def _(c):
-        for g in range(2):
+        for side in range(2):
+            g = me_ref[1] if side else 1 - me_ref[1]
             cross = cross_ref[c, g]
             for y in range(half):
-                label = sides[g][0][(groups // pairs) * comps, y].astype(jnp.float32)
+                label = sides[side][0][sides[side][0].shape[0] - 1, y].astype(jnp.float32)
                 density = density_at(label, density_ref, materials)
                 lanes = pl.ds(pl.multiple_of((c * half + y) * depth, depth), depth)
                 for m in range(groups):
                     start = pl.multiple_of((me ^ m) * members, members)
-                    left[g, pl.ds(start, members), lanes] = received_at(sides[g], m, groups, comps, c)[y + 1]
+                    left[side, pl.ds(start, members), lanes] = received_at(sides[side], m, comps, c)[y + 1]
                     at = (m * half + y) * members
                     put_images(
-                        cross[at : at + members], label, density, right.at[g], start, lanes, count, materials
+                        cross[at : at + members], label, density, right.at[side], start, lanes, count, materials
                     )
 
     below_ref[...] = correlate(left[0], right[0])
@@ -285,10 +281,11 @@
 
     @pl.loop(0, comps)
     def _(c):
-        for g in range(2):
+        for side in range(2):
+            g = me_ref[1] if side else 1 - me_ref[1]
             lhs = jnp.concatenate(
                 [
-                    jnp.concatenate(three_rows(received_at(sides[g], m, groups, comps, c), 0, half), axis=1)
+                    jnp.concatenate(three_rows(received_at(sides[side], m, comps, c), 0, half), axis=1)
                     for m in range(groups)
                 ],
                 axis=0,
@@ -381,34 +378,34 @@
 def body(snapshots, labels, free_mask, density):
     groups, slabs = lax.axis_size("snap"), lax.axis_size("space")
     planes, rows, depth = labels.shape
-    me = lax.axis_index("snap").astype(jnp.int32).reshape(1)
+    me = jnp.stack([lax.axis_index("snap"), lax.axis_index("space") % 2]).astype(jnp.int32)
     with jax.named_scope("spread"):
-        mine = spread(snapshots, free_mask, me, groups)
+        mine = spread(snapshots, free_mask, lax.axis_index("snap").astype(jnp.int32).reshape(1), groups)
     with jax.named_scope("regroup"):
         blocks = [mine[0]] + [
             lax.ppermute(mine[m], "snap", [(i, i ^ m) for i in range(groups)]) for m in range(1, groups)
         ]
     with jax.named_scope("halo"):
-        forward = [(i, i + 1) for i in range(slabs - 1)]
-        backward = [(b, a) for a, b in forward]
-        lows, highs = [], []
+        even = [(i, i ^ 1) for i in range(slabs)]
+        odd = [(i, ((i + 1) ^ 1) - 1) for i in range(1, slabs - 1)]
+        firsts, seconds = [], []
         for start in range(0, groups, 2):
-            pair = blocks[start : start + 2]
-            if lows:
-                pair, *_ = lax.optimization_barrier((pair, sent_up, sent_down))
-            sent_up, sent_down = pack(pair, None if lows else labels, me)
-            if not lows:
-                pair, sent_up, sent_down = lax.optimization_barrier((pair, sent_up, sent_down))
-            lows.append(lax.ppermute(sent_up, "space", forward))
-            highs.append(lax.ppermute(sent_down, "space", backward))
+            some = blocks[start : start + 2]
+            if firsts:
+                some, *_ = lax.optimization_barrier((some, to_even, to_odd))
+            to_even, to_odd = pack(some, None if firsts else labels, me)
+            if not firsts:
+                some, to_even, to_odd = lax.optimization_barrier((some, to_even, to_odd))
+            seconds.append(lax.ppermute(to_odd, "space", odd))
+            firsts.append(lax.ppermute(to_even, "space", even))
     with jax.named_scope("local_tiles"):
         near, edge, cross, left = local_tiles(blocks, labels, density, me)
     with jax.named_scope("return_tiles"):
-        below, above = return_tiles(cross, lows, highs, density, me, groups)
-        from_above = lax.ppermute(below, "space", backward)
-        from_below = lax.ppermute(above, "space", forward)
+        below, above = return_tiles(cross, firsts, seconds, density, me, groups)
+        from_below = lax.ppermute(below, "space", even)
+        from_above = lax.ppermute(above, "space", odd)
     with jax.named_scope("edge_tiles"):
-        part = edge_tiles(near, edge, left, lows, highs, labels, density, me, groups)
+        part = edge_tiles(near, edge, left, firsts, seconds, labels, density, me, groups)
     with jax.named_scope("sums"):
         part, wide = combine(part, (below, above, from_below, from_above), groups)
         sent = lax.all_to_all(wide, ("space", "snap"), 0, 0, tiled=True)

time: 91.2 us -> 89.5 us (0.981)
  starting transfers between devices: 36.6 us -> 33.2 us
  local copies, waits for them, and re-layouts: 3.1 us -> 4.23 us
  Pallas kernels: 16.1 us -> 17.2 us
    ppermute x6, starting transfers between devices: 8.75 us -> 4.96 us  [the longest x1 2.77 us: body(): from_below = lax.ppermute(below, 'space', even)]
    ppermute x6, waiting for transfers between devices: 1.87 us -> 0.02 us  [the longest x2 0.01 us: body(): firsts.append(lax.ppermute(to_even, 'space', even))]
    ppermute x3, waiting for transfers between devices: 22.2 us -> 23.5 us  [body(): lax.ppermute(mine[m], 'snap', [(i, i ^ m) for i in range(groups)])]
    unnamed x14, local copies, waits for them, and re-layouts: 3.1 us -> 4.23 us
    pallas_call x2, Pallas kernels: 0.07 us -> 1.16 us  [pack(): pl.pallas_call(functools.partial(pack_kernel, len(pair)), out_shape=[out,...]
  transfers between devices with their start and end apart: 13 -> 13, of which waited for: 6 -> 5; matrix products, arithmetic and copies ran while one was open for 0% -> 0% of each run, Pallas kernels for 11% -> 13%
where the time goes in v3:
time: 89.5 us; the launch traced here: 89.2 us
  waiting for transfers between devices  33.7 us (38%)
  starting transfers between devices  33.2 us (37%)
  Pallas kernels  17.2 us (19%)
  local copies, waits for them, and re-layouts  4.23 us (5%)
    ppermute x3, waiting for transfers between devices, body(): lax.ppermute(mine[m], 'snap', [(i, i ^ m) for i in range(groups)])  23.5 us
    all_to_all x1, starting transfers between devices, body(): sent = lax.all_to_all(wide, ('space', 'snap'), 0, 0, tiled=True)  16.2 us
    ppermute x3, starting transfers between devices, body(): lax.ppermute(mine[m], 'snap', [(i, i ^ m) for i in range(groups)])  6.56 us
    pallas_call x1, Pallas kernels, local_tiles(): pl.pallas_call(functools.partial(local_kernel, groups, density.shape[0]),...  6.04 us
    ppermute x3, starting transfers between devices, body(): lax.ppermute(part, 'snap', [(i, i ^ m) for i in range(groups)])  5.47 us
    ppermute x3, waiting for transfers between devices, body(): lax.ppermute(part, 'snap', [(i, i ^ m) for i in range(groups)])  5.18 us
    all_to_all x1, waiting for transfers between devices, body(): sent = lax.all_to_all(wide, ('space', 'snap'), 0, 0, tiled=True)  5.02 us
    unnamed x14, local copies, waits for them, and re-layouts  4.23 us
  transfers between devices with their start and end apart: 13, of which 5 were waited for; matrix products, arithmetic and copies ran while one was open for 0% of the time, Pallas kernels for 13%

profile of v3, /device:TPU:1, one launch (start us, length us, event | category | flops | bytes accessed | tf_op | source)
XLA Modules:
  0.0 89.2 jit_solution(10982373117139923135)
XLA Ops:
  0.6 0.0 copy-start.4
  0.6 0.0 copy-start
  0.7 1.4 %copy-done = bf16[16,3,2,64,128]{4,3,2,1,0:T(8,128)(2,1)S(1)} copy-done((bf16[16,3,2,64,128]{4,3,2,1,0:T(8,128)(2,1)S(1)}, bf16[16,3,2,64,128]{4,3,2,1,0:T(8,128)(2,1)}, u32[]{:S(2)}) %copy-start) | copy-done | bytes 1572888
  2.1 0.0 copy-start.1
  2.1 0.8 copy-done.1
  2.9 0.0 copy-start.3
  2.9 1.3 %spread.1 = (bf16[3,2,18,16,128]{4,3,2,1,0:T(8,128)(2,1)S(1)}, bf16[3,2,18,16,128]{4,3,2,1,0:T(8,128)(2,1)S(1)}, bf16[3,2,18,16,128]{4,3,2,1,0:T(8,128)(2,1)S(1)}, bf16[3,2,18,16,128]{4,3,2,1,0:T(8,128)(2,1)S(1)}) custom-call(s32[1]{0:T(128)} %bitcast.me_ref, bf16[16,3,2,64,128]{4,3,2,1,0:T(8,128)(2,1)S(1)} %copy-done, s32[2,64,128]{2,1,0:T(8,128)S(1)} %copy-done.1), custom_call_target="tpu_custom_call" | custom-call | bytes 5242880 | tf_op jit(solution)/shard_map/spread/pallas_call | solution.py:31
  4.2 3.3 %collective-permute-start = (bf16[3,2,18,16,128]{4,3,2,1,0:T(8,128)(2,1)S(1)}, bf16[3,2,18,16,128]{4,3,2,1,0:T(8,128)(2,1)S(1)}, u32[]{:S(2)}, u32[]{:S(2)}) collective-permute-start(bf16[3,2,18,16,128]{4,3,2,1,0:T(8,128)(2,1)S(1)} %get-tuple-element.25), channel_id=1, source_target_pairs={{0,1},{1,0},{2,3},{3,2},{4,5},{5,4},{6,7},{7,6},{8,9},{9,8},{10,11... | collective-permute-start | bytes 1327112 | tf_op jit(solution)/shard_map/regroup/ppermute | solution.py:386
  7.5 1.2 %collective-permute-start.1 = (bf16[3,2,18,16,128]{4,3,2,1,0:T(8,128)(2,1)S(1)}, bf16[3,2,18,16,128]{4,3,2,1,0:T(8,128)(2,1)S(1)}, u32[]{:S(2)}, u32[]{:S(2)}) collective-permute-start(bf16[3,2,18,16,128]{4,3,2,1,0:T(8,128)(2,1)S(1)} %get-tuple-element.26), channel_id=1, source_target_pairs={{0,2},{1,3},{2,0},{3,1},{4,6},{5,7},{6,4},{7,5},{8,10},{9,11},{10,... | collective-permute-start | bytes 1327112 | tf_op jit(solution)/shard_map/regroup/ppermute | solution.py:386
  8.7 2.0 %collective-permute-start.2 = (bf16[3,2,18,16,128]{4,3,2,1,0:T(8,128)(2,1)S(1)}, bf16[3,2,18,16,128]{4,3,2,1,0:T(8,128)(2,1)S(1)}, u32[]{:S(2)}, u32[]{:S(2)}) collective-permute-start(bf16[3,2,18,16,128]{4,3,2,1,0:T(8,128)(2,1)S(1)} %get-tuple-element.27), channel_id=1, source_target_pairs={{0,3},{1,2},{2,1},{3,0},{4,7},{5,6},{6,5},{7,4},{8,11},{9,10},{10,... | collective-permute-start | bytes 1327112 | tf_op jit(solution)/shard_map/regroup/ppermute | solution.py:386
  10.7 0.1 pad_add_fusion.me_ref
  10.8 0.0 collective-permute-done.refs_1_
  10.8 0.8 copy-done.2
  11.7 0.6 halo.2
  12.3 0.1 collective-permute-start.3
  12.4 0.7 collective-permute-start.5
  13.0 7.7 %collective-permute-done.1.refs_2_.refs_0_ = bf16[3,2,18,16,128]{4,3,2,1,0:T(8,128)(2,1)S(1)} collective-permute-done((bf16[3,2,18,16,128]{4,3,2,1,0:T(8,128)(2,1)S(1)}, bf16[3,2,18,16,128]{4,3,2,1,0:T(8,128)(2,1)S(1)}, u32[]{:S(2)}, u32[]{:S(2)}) %collective-permute-start.1) | collective-permute-done | bytes 442400 | tf_op jit(solution)/shard_map/regroup/ppermute | solution.py:386
  20.7 15.8 %collective-permute-done.2.refs_3_.refs_1_ = bf16[3,2,18,16,128]{4,3,2,1,0:T(8,128)(2,1)S(1)} collective-permute-done((bf16[3,2,18,16,128]{4,3,2,1,0:T(8,128)(2,1)S(1)}, bf16[3,2,18,16,128]{4,3,2,1,0:T(8,128)(2,1)S(1)}, u32[]{:S(2)}, u32[]{:S(2)}) %collective-permute-start.2) | collective-permute-done | bytes 442400 | tf_op jit(solution)/shard_map/regroup/ppermute | solution.py:386
  36.6 0.6 halo.3
  37.1 0.1 collective-permute-start.4
  37.2 0.7 collective-permute-start.6
  37.9 0.0 copy-done.4
  37.9 0.0 copy-done.3
  37.9 0.0 copy-start.5
  38.0 1.1 %copy-done.5 = bf16[768,512]{1,0:T(8,128)(2,1)S(1)} copy-done((bf16[768,512]{1,0:T(8,128)(2,1)S(1)}, bf16[768,512]{1,0:T(8,128)(2,1)}, u32[]{:S(2)}) %copy-start.5) | copy-done | bytes 786456
  39.1 6.0 %local_tiles.1 = (f32[64,256]{1,0:T(8,128)S(1)}, f32[3,2,512,256]{3,2,1,0:T(8,128)S(1)}, f32[3,2,512,256]{3,2,1,0:T(8,128)S(1)}, bf16[2,64,3072]{2,1,0:T(8,128)(2,1)S(1)}) custom-call(s32[2]{0:T(128)S(1)} %pad_add_fusion.me_ref, f32[3]{0:T(128)S(1)} %copy-done.4, bf16[3,2,18,16,128]{4,3,2,1,0:T(8,128)(2,1)S(1)} %get-tuple-element.24.refs_0_, ...), custom_call_target="tpu_custom_call" | custom-call | flops 5000000000 | bytes 12582912 | tf_op jit(solution)/shard_map/local_tiles/pallas_call | solution.py:192
  45.1 0.0 collective-permute-done.4.refs_1_
  45.1 0.0 collective-permute-done.6.refs_3_
  45.1 0.0 collective-permute-done.3.refs_0_
  45.2 0.0 collective-permute-done.5.refs_2_
  45.2 0.0 copy-start.6
  45.2 2.9 %return_tiles.1 = (f32[64,256]{1,0:T(8,128)S(1)}, f32[64,256]{1,0:T(8,128)S(1)}) custom-call(s32[2]{0:T(128)S(1)} %pad_add_fusion.me_ref, f32[3]{0:T(128)S(1)} %copy-done.4, f32[3,2,512,256]{3,2,1,0:T(8,128)S(1)} %get-tuple-element.39.cross_ref, bf16[7,10,16,128]{3,2,1,0:T(8,128)(2,1)S(1)} %collective-permute-done.3.refs_0_, ...), custom_call_target="tpu_custom_call" | custom-call | flops 3000000000 | bytes 6291456 | tf_op jit(solution)/shard_map/return_tiles/pallas_call | solution.py:258
  48.1 2.8 %collective-permute-start.7 = (f32[64,256]{1,0:T(8,128)S(1)}, f32[64,256]{1,0:T(8,128)S(1)}, u32[]{:S(2)}, u32[]{:S(2)}) collective-permute-start(f32[64,256]{1,0:T(8,128)S(1)} %get-tuple-element.40.below_ref), channel_id=1, source_target_pairs={{0,4},{4,0},{8,12},{12,8},{16,20},{20,16},{24,28},{28,24},{32,36},... | collective-permute-start | bytes 196616 | tf_op jit(solution)/shard_map/return_tiles/ppermute | solution.py:405
  50.9 0.7 collective-permute-start.8
  51.6 0.0 copy-done.6
  51.6 4.0 %edge_tiles.1.part_ref = f32[64,256]{1,0:T(8,128)S(1)} custom-call(s32[2]{0:T(128)S(1)} %pad_add_fusion.me_ref, f32[3]{0:T(128)S(1)} %copy-done.4, f32[64,256]{1,0:T(8,128)S(1)} %get-tuple-element.28.near_ref, f32[3,2,512,256]{3,2,1,0:T(8,128)S(1)} %get-tuple-element.29.edge_ref, bf16[2,64,3072]{2,1,0:T(8,128)(2,1)S(1)} %get-tuple-element.30.left_ref, ...), custom_call_target="tpu_custom_call" | custom-call | flops 5000000000 | bytes 20971520 | tf_op jit(solution)/shard_map/edge_tiles/pallas_call | solution.py:340
  55.5 0.0 collective-permute-done.7.from_below_ref
  55.5 0.0 collective-permute-done.8.from_above_ref
  55.6 0.8 sums.2
  56.3 16.2 %all-to-all-start = ((f32[256,1,256]{2,1,0:T(1,128)}), f32[256,1,256]{2,1,0:T(1,128)S(1)}, u32[]{:S(2)}, u32[]{:S(2)}) async-start(f32[256,1,256]{2,1,0:T(1,128)} %get-tuple-element.43), calls=%async_computation | async-start | bytes 524288 | tf_op jit(solution)/shard_map/sums/all_to_all | solution.py:411
  72.5 2.2 %collective-permute-start.9 = (f32[64,256]{1,0:T(8,128)S(1)}, f32[64,256]{1,0:T(8,128)S(1)}, u32[]{:S(2)}, u32[]{:S(2)}) collective-permute-start(f32[64,256]{1,0:T(8,128)S(1)} %get-tuple-element.42.refs_0_), channel_id=1, source_target_pairs={{0,1},{1,0},{2,3},{3,2},{4,5},{5,4},{6,7},{7,6},{8,9},{9,8},{10,11... | collective-permute-start | bytes 196616 | tf_op jit(solution)/shard_map/sums/ppermute | solution.py:413
  74.7 1.1 %collective-permute-start.10 = (f32[64,256]{1,0:T(8,128)S(1)}, f32[64,256]{1,0:T(8,128)S(1)}, u32[]{:S(2)}, u32[]{:S(2)}) collective-permute-start(f32[64,256]{1,0:T(8,128)S(1)} %get-tuple-element.42.refs_0_), channel_id=1, source_target_pairs={{0,2},{1,3},{2,0},{3,1},{4,6},{5,7},{6,4},{7,5},{8,10},{9,11},{10,... | collective-permute-start | bytes 196616 | tf_op jit(solution)/shard_map/sums/ppermute | solution.py:413
  75.9 2.1 %collective-permute-start.11 = (f32[64,256]{1,0:T(8,128)S(1)}, f32[64,256]{1,0:T(8,128)S(1)}, u32[]{:S(2)}, u32[]{:S(2)}) collective-permute-start(f32[64,256]{1,0:T(8,128)S(1)} %get-tuple-element.42.refs_0_), channel_id=1, source_target_pairs={{0,3},{1,2},{2,1},{3,0},{4,7},{5,6},{6,5},{7,4},{8,11},{9,10},{10,... | collective-permute-start | bytes 196616 | tf_op jit(solution)/shard_map/sums/ppermute | solution.py:413
  78.0 0.0 collective-permute-done.9.refs_1_
  78.0 2.4 %collective-permute-done.10.refs_2_ = f32[64,256]{1,0:T(8,128)S(1)} collective-permute-done((f32[64,256]{1,0:T(8,128)S(1)}, f32[64,256]{1,0:T(8,128)S(1)}, u32[]{:S(2)}, u32[]{:S(2)}) %collective-permute-start.10) | collective-permute-done | bytes 65568 | tf_op jit(solution)/shard_map/sums/ppermute | solution.py:413
  80.4 2.8 %collective-permute-done.11.refs_3_ = f32[64,256]{1,0:T(8,128)S(1)} collective-permute-done((f32[64,256]{1,0:T(8,128)S(1)}, f32[64,256]{1,0:T(8,128)S(1)}, u32[]{:S(2)}, u32[]{:S(2)}) %collective-permute-start.11) | collective-permute-done | bytes 65568 | tf_op jit(solution)/shard_map/sums/ppermute | solution.py:413
  83.2 5.0 %all-to-all-done.refs_4_ = f32[256,1,256]{2,1,0:T(1,128)S(1)} async-done(((f32[256,1,256]{2,1,0:T(1,128)}), f32[256,1,256]{2,1,0:T(1,128)S(1)}, u32[]{:S(2)}, u32[]{:S(2)}) %all-to-all-start) | async-done | bytes 262176 | tf_op jit(solution)/shard_map/sums/all_to_all | solution.py:411
  88.2 1.0 %sums.3 = (f32[1,4,64,64]{3,2,1,0:T(8,128)}, f32[4,1,64]{2,1,0:T(1,128)}) custom-call(f32[64,256]{1,0:T(8,128)S(1)} %get-tuple-element.42.refs_0_, f32[64,256]{1,0:T(8,128)S(1)} %collective-permute-done.9.refs_1_, f32[64,256]{1,0:T(8,128)S(1)} %collective-permute-done.10.refs_2_, f32[64,256]{1,0:T(8,128)S(1)} %collective-permute-done.11.refs_3_, ...), custom_call_target="tpu_custom_call" | custom-call | tf_op jit(solution)/shard_map/sums/pallas_call | solution.py:366
  (1 shorter events, 0.0 us)
Async XLA Ops:
  0.6 37.3 %copy-start.4 = (f32[3]{0:T(128)S(1)}, f32[3]{0:T(128)}, u32[]{:S(2)}) copy-start(f32[3]{0:T(128)} %density_ref.5) | copy-start | bytes 40
  0.6 1.4 %copy-start = (bf16[16,3,2,64,128]{4,3,2,1,0:T(8,128)(2,1)S(1)}, bf16[16,3,2,64,128]{4,3,2,1,0:T(8,128)(2,1)}, u32[]{:S(2)}) copy-start(bf16[16,3,2,64,128]{4,3,2,1,0:T(8,128)(2,1)} %snaps_ref.1) | copy-start | bytes 4718596
  2.1 0.8 copy-start.1
  2.9 35.0 %copy-start.3 = (s32[2,64,128]{2,1,0:T(8,128)S(1)}, s32[2,64,128]{2,1,0:T(8,128)}, u32[]{:S(2)}) copy-start(s32[2,64,128]{2,1,0:T(8,128)} %refs_4_.3) | copy-start | bytes 196612
  4.2 6.6 %collective-permute-start = (bf16[3,2,18,16,128]{4,3,2,1,0:T(8,128)(2,1)S(1)}, bf16[3,2,18,16,128]{4,3,2,1,0:T(8,128)(2,1)S(1)}, u32[]{:S(2)}, u32[]{:S(2)}) collective-permute-start(bf16[3,2,18,16,128]{4,3,2,1,0:T(8,128)(2,1)S(1)} %get-tuple-element.25), channel_id=1, source_target_pairs={{0,1},{1,0},{2,3},{3,2},{4,5},{5,4},{6,7},{7,6},{8,9},{9,8},{10,11... | collective-permute-start | bytes 1327112 | tf_op jit(solution)/shard_map/regroup/ppermute | solution.py:386
  7.5 13.2 %collective-permute-start.1 = (bf16[3,2,18,16,128]{4,3,2,1,0:T(8,128)(2,1)S(1)}, bf16[3,2,18,16,128]{4,3,2,1,0:T(8,128)(2,1)S(1)}, u32[]{:S(2)}, u32[]{:S(2)}) collective-permute-start(bf16[3,2,18,16,128]{4,3,2,1,0:T(8,128)(2,1)S(1)} %get-tuple-element.26), channel_id=1, source_target_pairs={{0,2},{1,3},{2,0},{3,1},{4,6},{5,7},{6,4},{7,5},{8,10},{9,11},{10,... | collective-permute-start | bytes 1327112 | tf_op jit(solution)/shard_map/regroup/ppermute | solution.py:386
  8.7 27.8 %collective-permute-start.2 = (bf16[3,2,18,16,128]{4,3,2,1,0:T(8,128)(2,1)S(1)}, bf16[3,2,18,16,128]{4,3,2,1,0:T(8,128)(2,1)S(1)}, u32[]{:S(2)}, u32[]{:S(2)}) collective-permute-start(bf16[3,2,18,16,128]{4,3,2,1,0:T(8,128)(2,1)S(1)} %get-tuple-element.27), channel_id=1, source_target_pairs={{0,3},{1,2},{2,1},{3,0},{4,7},{5,6},{6,5},{7,4},{8,11},{9,10},{10,... | collective-permute-start | bytes 1327112 | tf_op jit(solution)/shard_map/regroup/ppermute | solution.py:386
  10.8 0.8 copy-start.2
  12.3 32.9 %collective-permute-start.3 = (bf16[7,10,16,128]{3,2,1,0:T(8,128)(2,1)S(1)}, bf16[7,10,16,128]{3,2,1,0:T(8,128)(2,1)S(1)}, u32[]{:S(2)}, u32[]{:S(2)}) collective-permute-start(bf16[7,10,16,128]{3,2,1,0:T(8,128)(2,1)S(1)} %get-tuple-element.33), channel_id=1, source_target_pairs={{0,4},{4,0},{8,12},{12,8},{16,20},{20,16},{24,28},{28,24},{32,36},... | collective-permute-start | bytes 860168 | tf_op jit(solution)/shard_map/halo/ppermute | solution.py:400
  12.4 32.8 %collective-permute-start.5 = (bf16[7,10,16,128]{3,2,1,0:T(8,128)(2,1)S(1)}, bf16[7,10,16,128]{3,2,1,0:T(8,128)(2,1)S(1)}, u32[]{:S(2)}, u32[]{:S(2)}) collective-permute-start(bf16[7,10,16,128]{3,2,1,0:T(8,128)(2,1)S(1)} %get-tuple-element.34), channel_id=1, source_target_pairs={{4,8},{8,4},{12,16},{16,12},{20,24},{24,20},{28,32},{32,28},{36,40... | collective-permute-start | bytes 860168 | tf_op jit(solution)/shard_map/halo/ppermute | solution.py:399
  37.1 8.0 %collective-permute-start.4 = (bf16[6,10,16,128]{3,2,1,0:T(8,128)(2,1)S(1)}, bf16[6,10,16,128]{3,2,1,0:T(8,128)(2,1)S(1)}, u32[]{:S(2)}, u32[]{:S(2)}) collective-permute-start(bf16[6,10,16,128]{3,2,1,0:T(8,128)(2,1)S(1)} %get-tuple-element.37), channel_id=1, source_target_pairs={{0,4},{4,0},{8,12},{12,8},{16,20},{20,16},{24,28},{28,24},{32,36},... | collective-permute-start | bytes 737288 | tf_op jit(solution)/shard_map/halo/ppermute | solution.py:400
  37.2 7.9 %collective-permute-start.6 = (bf16[6,10,16,128]{3,2,1,0:T(8,128)(2,1)S(1)}, bf16[6,10,16,128]{3,2,1,0:T(8,128)(2,1)S(1)}, u32[]{:S(2)}, u32[]{:S(2)}) collective-permute-start(bf16[6,10,16,128]{3,2,1,0:T(8,128)(2,1)S(1)} %get-tuple-element.38), channel_id=1, source_target_pairs={{4,8},{8,4},{12,16},{16,12},{20,24},{24,20},{28,32},{32,28},{36,40... | collective-permute-start | bytes 737288 | tf_op jit(solution)/shard_map/halo/ppermute | solution.py:399
  37.9 1.1 %copy-start.5 = (bf16[768,512]{1,0:T(8,128)(2,1)S(1)}, bf16[768,512]{1,0:T(8,128)(2,1)}, u32[]{:S(2)}) copy-start(bf16[768,512]{1,0:T(8,128)(2,1)} %constant.26.clone.refs_5_) | copy-start | bytes 2359300
  45.2 6.4 %copy-start.6 = (bf16[384,256]{1,0:T(8,128)(2,1)S(1)}, bf16[384,256]{1,0:T(8,128)(2,1)}, u32[]{:S(2)}) copy-start(bf16[384,256]{1,0:T(8,128)(2,1)} %constant.27.clone.refs_5_) | copy-start | bytes 589828
  48.1 7.4 %collective-permute-start.7 = (f32[64,256]{1,0:T(8,128)S(1)}, f32[64,256]{1,0:T(8,128)S(1)}, u32[]{:S(2)}, u32[]{:S(2)}) collective-permute-start(f32[64,256]{1,0:T(8,128)S(1)} %get-tuple-element.40.below_ref), channel_id=1, source_target_pairs={{0,4},{4,0},{8,12},{12,8},{16,20},{20,16},{24,28},{28,24},{32,36},... | collective-permute-start | bytes 196616 | tf_op jit(solution)/shard_map/return_tiles/ppermute | solution.py:405
  50.9 4.7 %collective-permute-start.8 = (f32[64,256]{1,0:T(8,128)S(1)}, f32[64,256]{1,0:T(8,128)S(1)}, u32[]{:S(2)}, u32[]{:S(2)}) collective-permute-start(f32[64,256]{1,0:T(8,128)S(1)} %get-tuple-element.41.above_ref), channel_id=1, source_target_pairs={{4,8},{8,4},{12,16},{16,12},{20,24},{24,20},{28,32},{32,28},{36,40... | collective-permute-start | bytes 196616 | tf_op jit(solution)/shard_map/return_tiles/ppermute | solution.py:406
  56.3 31.8 %all-to-all-start = ((f32[256,1,256]{2,1,0:T(1,128)}), f32[256,1,256]{2,1,0:T(1,128)S(1)}, u32[]{:S(2)}, u32[]{:S(2)}) async-start(f32[256,1,256]{2,1,0:T(1,128)} %get-tuple-element.43), calls=%async_computation | async-start | bytes 524288 | tf_op jit(solution)/shard_map/sums/all_to_all | solution.py:411
  72.5 5.5 %collective-permute-start.9 = (f32[64,256]{1,0:T(8,128)S(1)}, f32[64,256]{1,0:T(8,128)S(1)}, u32[]{:S(2)}, u32[]{:S(2)}) collective-permute-start(f32[64,256]{1,0:T(8,128)S(1)} %get-tuple-element.42.refs_0_), channel_id=1, source_target_pairs={{0,1},{1,0},{2,3},{3,2},{4,5},{5,4},{6,7},{7,6},{8,9},{9,8},{10,11... | collective-permute-start | bytes 196616 | tf_op jit(solution)/shard_map/sums/ppermute | solution.py:413
  74.7 5.6 %collective-permute-start.10 = (f32[64,256]{1,0:T(8,128)S(1)}, f32[64,256]{1,0:T(8,128)S(1)}, u32[]{:S(2)}, u32[]{:S(2)}) collective-permute-start(f32[64,256]{1,0:T(8,128)S(1)} %get-tuple-element.42.refs_0_), channel_id=1, source_target_pairs={{0,2},{1,3},{2,0},{3,1},{4,6},{5,7},{6,4},{7,5},{8,10},{9,11},{10,... | collective-permute-start | bytes 196616 | tf_op jit(solution)/shard_map/sums/ppermute | solution.py:413
  75.9 7.3 %collective-permute-start.11 = (f32[64,256]{1,0:T(8,128)S(1)}, f32[64,256]{1,0:T(8,128)S(1)}, u32[]{:S(2)}, u32[]{:S(2)}) collective-permute-start(f32[64,256]{1,0:T(8,128)S(1)} %get-tuple-element.42.refs_0_), channel_id=1, source_target_pairs={{0,3},{1,2},{2,1},{3,0},{4,7},{5,6},{6,5},{7,4},{8,11},{9,10},{10,... | collective-permute-start | bytes 196616 | tf_op jit(solution)/shard_map/sums/ppermute | solution.py:413

commit v4 on v3

--- a/solution.py
+++ b/solution.py
@@ -46,22 +46,26 @@
     )(me, snapshots, free_mask)
 
 
-def stencil_weights(depth):
-    mass = {-1: 1.0, 0: 4.0, 1: 1.0}
-    stiff = {-1: -1.0, 0: 2.0, 1: -1.0}
-    near = np.eye(depth, k=1) + np.eye(depth, k=-1)
-    mass_z = 4.0 * np.eye(depth) + near
-    stiff_z = 2.0 * np.eye(depth) - near
-
-    def plane(dx):
-        blocks = []
-        for dy in (-1, 0, 1):
-            both = mass[dx] * mass[dy]
-            mixed = stiff[dx] * mass[dy] + mass[dx] * stiff[dy]
-            blocks.append(np.concatenate([both * mass_z, mixed * mass_z + both * stiff_z], axis=1))
-        return np.concatenate(blocks, axis=0)
-
-    return plane(0), plane(1)
+def put_stencil(weights_ref, planes):
+    depth = weights_ref.shape[1] // (2 * planes)
+    apart = jnp.abs(
+        lax.broadcasted_iota(jnp.int32, (depth, depth), 0) - lax.broadcasted_iota(jnp.int32, (depth, depth), 1)
+    )
+    mass, stiff = (4.0, 1.0), (2.0, -1.0)
+    for q in range(planes):
+        for dy in range(3):
+            for p in range(planes):
+                x, y = abs(q - p), abs(dy - 1)
+                both = mass[x] * mass[y]
+                mixed = stiff[x] * mass[y] + mass[x] * stiff[y]
+                for kind, (same, beside) in enumerate(
+                    ((4.0 * both, both), (4.0 * mixed + 2.0 * both, mixed - both))
+                ):
+                    block = jnp.where(apart == 0, same, jnp.where(apart == 1, beside, 0.0))
+                    weights_ref[
+                        (q * 3 + dy) * depth : (q * 3 + dy + 1) * depth,
+                        (p * 2 + kind) * depth : (p * 2 + kind + 1) * depth,
+                    ] = block.astype(weights_ref.dtype)
 
 
 def three_rows(block, first, height):
@@ -145,20 +149,24 @@
 
 
 def pack_kernel(pairs, me_ref, *refs):
-    blocks, outs = refs[:pairs], refs[-2:]
+    blocks = refs[:pairs]
     comps, planes, reach, members, depth = blocks[0].shape
+    labelled = len(refs) > pairs + 2
+    outs = refs[pairs + labelled : pairs + labelled + 2]
     half = (reach - 2) // 2
     for out, up in ((outs[0], 1 - me_ref[1]), (outs[1], me_ref[1])):
         first = (1 - up) * half
         for i, block in enumerate(blocks):
             for c in range(comps):
                 out[i * comps + c] = block[c, up * (planes - 1), pl.ds(first, half + 2)]
-        if out.shape[0] > pairs * comps:
+        if labelled:
             labels_ref = refs[pairs]
             for y in range(half + 2):
                 at = me_ref[0] * 2 * half + first + min(y, half - 1)
                 row = labels_ref[up * (planes - 1), pl.ds(at, 1), :]
                 out[pairs * comps, y] = jnp.broadcast_to(row, (members, depth)).astype(jnp.float32).astype(out.dtype)
+    if labelled:
+        put_stencil(refs[-1], planes)
 
 
 def pack(pair, labels, me):
@@ -167,27 +175,25 @@
     out = jax.ShapeDtypeStruct(
         (len(pair) * comps + len(extra), (reach - 2) // 2 + 2, members, depth), pair[0].dtype
     )
+    outs = [out, out]
+    if extra:
+        outs.append(jax.ShapeDtypeStruct((3 * planes * depth, 2 * planes * depth), pair[0].dtype))
     return pl.pallas_call(
         functools.partial(pack_kernel, len(pair)),
-        out_shape=[out, out],
+        out_shape=outs,
         in_specs=[smem_spec()] + [vmem_spec()] * (len(pair) + len(extra)),
-        out_specs=[vmem_spec()] * 2,
+        out_specs=[vmem_spec()] * len(outs),
         compiler_params=pltpu.CompilerParams(vmem_limit_bytes=16 * 2**20),
         cost_estimate=pl.CostEstimate(flops=0, bytes_accessed=2**20, transcendentals=0),
     )(me, *pair, *extra)
 
 
-def local_tiles(blocks, labels, density, me):
+def local_tiles(blocks, labels, density, weights, me):
     groups = len(blocks)
     comps, planes, reach, members, depth = blocks[0].shape
     half = (reach - 2) // 2
     count = groups * members
     columns = (density.shape[0] + 1) * count
-    same, beside = stencil_weights(depth)
-    weights = jnp.asarray(
-        np.concatenate([np.concatenate([same, beside], axis=0), np.concatenate([beside, same], axis=0)], axis=1),
-        jnp.bfloat16,
-    )
     image = jax.ShapeDtypeStruct((comps, 2, groups * half * members, 2 * depth), jnp.float32)
     return pl.pallas_call(
         functools.partial(local_kernel, groups, density.shape[0]),
@@ -290,7 +296,7 @@
                 ],
                 axis=0,
             )
-            image = edge_ref[c, g] + jnp.dot(lhs, weights_ref[...], preferred_element_type=jnp.float32)
+            image = edge_ref[c, g] + jnp.dot(lhs, weights_ref[3 * depth : 6 * depth, : 2 * depth], preferred_element_type=jnp.float32)
             for y in range(half):
                 label = labels_ref[g, pl.ds(me * width + g * half + y, 1), :]
                 density = density_at(label, density_ref, materials)
@@ -331,10 +337,9 @@
     )(part, *returns)
 
 
-def edge_tiles(near, edge, left, lows, highs, labels, density, me, groups):
+def edge_tiles(near, edge, left, lows, highs, labels, density, weights, me, groups):
     count, columns = near.shape
     materials = density.shape[0]
-    weights = jnp.asarray(stencil_weights(labels.shape[2])[1], jnp.bfloat16)
     part = jax.ShapeDtypeStruct((count, columns), jnp.float32)
     halos = [*lows, *highs]
     return pl.pallas_call(
@@ -393,19 +398,20 @@
             some = blocks[start : start + 2]
             if firsts:
                 some, *_ = lax.optimization_barrier((some, to_even, to_odd))
-            to_even, to_odd = pack(some, None if firsts else labels, me)
+            to_even, to_odd, *stencil = pack(some, None if firsts else labels, me)
             if not firsts:
+                weights = stencil[0]
                 some, to_even, to_odd = lax.optimization_barrier((some, to_even, to_odd))
             seconds.append(lax.ppermute(to_odd, "space", odd))
             firsts.append(lax.ppermute(to_even, "space", even))
     with jax.named_scope("local_tiles"):
-        near, edge, cross, left = local_tiles(blocks, labels, density, me)
+        near, edge, cross, left = local_tiles(blocks, labels, density, weights, me)
     with jax.named_scope("return_tiles"):
         below, above = return_tiles(cross, firsts, seconds, density, me, groups)
         from_below = lax.ppermute(below, "space", even)
         from_above = lax.ppermute(above, "space", odd)
     with jax.named_scope("edge_tiles"):
-        part = edge_tiles(near, edge, left, firsts, seconds, labels, density, me, groups)
+        part = edge_tiles(near, edge, left, firsts, seconds, labels, density, weights, me, groups)
     with jax.named_scope("sums"):
         part, wide = combine(part, (below, above, from_below, from_above), groups)
         sent = lax.all_to_all(wide, ("space", "snap"), 0, 0, tiled=True)

time: 89.5 us -> 88.4 us (0.988)
  local copies, waits for them, and re-layouts: 4.23 us -> 3.09 us
    unnamed x14 -> x10, local copies, waits for them, and re-layouts: 4.23 us -> 3.09 us
  transfers between devices with their start and end apart: 13 -> 13, of which waited for: 5 -> 6; matrix products, arithmetic and copies ran while one was open for 0% -> 0% of each run, Pallas kernels for 13% -> 13%
where the time goes in v4:
time: 88.4 us; the launch traced here: 88.1 us
  waiting for transfers between devices  34.2 us (39%)
  starting transfers between devices  32.6 us (37%)
  Pallas kernels  17.3 us (20%)
  local copies, waits for them, and re-layouts  3.09 us (3%)
    ppermute x3, waiting for transfers between devices, body(): lax.ppermute(mine[m], 'snap', [(i, i ^ m) for i in range(groups)])  23.4 us
    all_to_all x1, starting transfers between devices, body(): sent = lax.all_to_all(wide, ('space', 'snap'), 0, 0, tiled=True)  15.3 us
    ppermute x3, starting transfers between devices, body(): lax.ppermute(mine[m], 'snap', [(i, i ^ m) for i in range(groups)])  6.56 us
    pallas_call x1, Pallas kernels, local_tiles(): pl.pallas_call(functools.partial(local_kernel, groups, density.shape[0]),...  6.09 us
    ppermute x3, starting transfers between devices, body(): lax.ppermute(part, 'snap', [(i, i ^ m) for i in range(groups)])  5.47 us
    ppermute x3, waiting for transfers between devices, body(): lax.ppermute(part, 'snap', [(i, i ^ m) for i in range(groups)])  5.18 us
    all_to_all x1, waiting for transfers between devices, body(): sent = lax.all_to_all(wide, ('space', 'snap'), 0, 0, tiled=True)  5.02 us
    pallas_call x1, Pallas kernels, edge_tiles(): pl.pallas_call(functools.partial(edge_kernel, groups, materials, len(lows...  3.96 us
  transfers between devices with their start and end apart: 13, of which 6 were waited for; matrix products, arithmetic and copies ran while one was open for 0% of the time, Pallas kernels for 13%

profile of v4, /device:TPU:1, one launch (start us, length us, event | category | flops | bytes accessed | tf_op | source)
XLA Modules:
  0.0 88.1 jit_solution(15144759134131480301)
XLA Ops:
  0.6 0.0 copy-start.4
  0.6 0.0 copy-start
  0.7 1.4 %copy-done = bf16[16,3,2,64,128]{4,3,2,1,0:T(8,128)(2,1)S(1)} copy-done((bf16[16,3,2,64,128]{4,3,2,1,0:T(8,128)(2,1)S(1)}, bf16[16,3,2,64,128]{4,3,2,1,0:T(8,128)(2,1)}, u32[]{:S(2)}) %copy-start) | copy-done | bytes 1572888
  2.1 0.0 copy-start.1
  2.1 0.8 copy-done.1
  2.9 0.0 copy-start.3
  2.9 1.3 %spread.1 = (bf16[3,2,18,16,128]{4,3,2,1,0:T(8,128)(2,1)S(1)}, bf16[3,2,18,16,128]{4,3,2,1,0:T(8,128)(2,1)S(1)}, bf16[3,2,18,16,128]{4,3,2,1,0:T(8,128)(2,1)S(1)}, bf16[3,2,18,16,128]{4,3,2,1,0:T(8,128)(2,1)S(1)}) custom-call(s32[1]{0:T(128)} %bitcast.me_ref, bf16[16,3,2,64,128]{4,3,2,1,0:T(8,128)(2,1)S(1)} %copy-done, s32[2,64,128]{2,1,0:T(8,128)S(1)} %copy-done.1), custom_call_target="tpu_custom_call" | custom-call | bytes 5242880 | tf_op jit(solution)/shard_map/spread/pallas_call | solution.py:31
  4.2 3.3 %collective-permute-start = (bf16[3,2,18,16,128]{4,3,2,1,0:T(8,128)(2,1)S(1)}, bf16[3,2,18,16,128]{4,3,2,1,0:T(8,128)(2,1)S(1)}, u32[]{:S(2)}, u32[]{:S(2)}) collective-permute-start(bf16[3,2,18,16,128]{4,3,2,1,0:T(8,128)(2,1)S(1)} %get-tuple-element.26), channel_id=1, source_target_pairs={{0,1},{1,0},{2,3},{3,2},{4,5},{5,4},{6,7},{7,6},{8,9},{9,8},{10,11... | collective-permute-start | bytes 1327112 | tf_op jit(solution)/shard_map/regroup/ppermute | solution.py:391
  7.5 1.2 %collective-permute-start.1 = (bf16[3,2,18,16,128]{4,3,2,1,0:T(8,128)(2,1)S(1)}, bf16[3,2,18,16,128]{4,3,2,1,0:T(8,128)(2,1)S(1)}, u32[]{:S(2)}, u32[]{:S(2)}) collective-permute-start(bf16[3,2,18,16,128]{4,3,2,1,0:T(8,128)(2,1)S(1)} %get-tuple-element.27), channel_id=1, source_target_pairs={{0,2},{1,3},{2,0},{3,1},{4,6},{5,7},{6,4},{7,5},{8,10},{9,11},{10,... | collective-permute-start | bytes 1327112 | tf_op jit(solution)/shard_map/regroup/ppermute | solution.py:391
  8.7 2.0 %collective-permute-start.2 = (bf16[3,2,18,16,128]{4,3,2,1,0:T(8,128)(2,1)S(1)}, bf16[3,2,18,16,128]{4,3,2,1,0:T(8,128)(2,1)S(1)}, u32[]{:S(2)}, u32[]{:S(2)}) collective-permute-start(bf16[3,2,18,16,128]{4,3,2,1,0:T(8,128)(2,1)S(1)} %get-tuple-element.28), channel_id=1, source_target_pairs={{0,3},{1,2},{2,1},{3,0},{4,7},{5,6},{6,5},{7,4},{8,11},{9,10},{10,... | collective-permute-start | bytes 1327112 | tf_op jit(solution)/shard_map/regroup/ppermute | solution.py:391
  10.7 0.1 pad_add_fusion.me_ref
  10.8 0.0 collective-permute-done.refs_1_
  10.8 0.0 copy-start.2
  10.8 0.8 copy-done.2
  11.7 0.7 halo.2
  12.4 0.1 collective-permute-start.3
  12.5 0.7 collective-permute-start.5
  13.1 7.6 %collective-permute-done.1.refs_2_.refs_0_ = bf16[3,2,18,16,128]{4,3,2,1,0:T(8,128)(2,1)S(1)} collective-permute-done((bf16[3,2,18,16,128]{4,3,2,1,0:T(8,128)(2,1)S(1)}, bf16[3,2,18,16,128]{4,3,2,1,0:T(8,128)(2,1)S(1)}, u32[]{:S(2)}, u32[]{:S(2)}) %collective-permute-start.1) | collective-permute-done | bytes 442400 | tf_op jit(solution)/shard_map/regroup/ppermute | solution.py:391
  20.7 15.8 %collective-permute-done.2.refs_3_.refs_1_ = bf16[3,2,18,16,128]{4,3,2,1,0:T(8,128)(2,1)S(1)} collective-permute-done((bf16[3,2,18,16,128]{4,3,2,1,0:T(8,128)(2,1)S(1)}, bf16[3,2,18,16,128]{4,3,2,1,0:T(8,128)(2,1)S(1)}, u32[]{:S(2)}, u32[]{:S(2)}) %collective-permute-start.2) | collective-permute-done | bytes 442400 | tf_op jit(solution)/shard_map/regroup/ppermute | solution.py:391
  36.6 0.6 halo.3
  37.1 0.1 collective-permute-start.4
  37.2 0.7 collective-permute-start.6
  37.9 0.0 copy-done.4
  37.9 0.0 copy-done.3
  37.9 6.1 %local_tiles.1 = (f32[64,256]{1,0:T(8,128)S(1)}, f32[3,2,512,256]{3,2,1,0:T(8,128)S(1)}, f32[3,2,512,256]{3,2,1,0:T(8,128)S(1)}, bf16[2,64,3072]{2,1,0:T(8,128)(2,1)S(1)}) custom-call(s32[2]{0:T(128)S(1)} %pad_add_fusion.me_ref, f32[3]{0:T(128)S(1)} %copy-done.4, bf16[3,2,18,16,128]{4,3,2,1,0:T(8,128)(2,1)S(1)} %get-tuple-element.25.refs_0_, ...), custom_call_target="tpu_custom_call" | custom-call | flops 5000000000 | bytes 12582912 | tf_op jit(solution)/shard_map/local_tiles/pallas_call | solution.py:198
  44.0 0.5 collective-permute-done.4.refs_1_
  44.6 0.0 collective-permute-done.6.refs_3_
  44.6 0.0 collective-permute-done.3.refs_0_
  44.6 0.0 collective-permute-done.5.refs_2_
  44.6 2.9 %return_tiles.1 = (f32[64,256]{1,0:T(8,128)S(1)}, f32[64,256]{1,0:T(8,128)S(1)}) custom-call(s32[2]{0:T(128)S(1)} %pad_add_fusion.me_ref, f32[3]{0:T(128)S(1)} %copy-done.4, f32[3,2,512,256]{3,2,1,0:T(8,128)S(1)} %get-tuple-element.41.cross_ref, bf16[7,10,16,128]{3,2,1,0:T(8,128)(2,1)S(1)} %collective-permute-done.3.refs_0_, ...), custom_call_target="tpu_custom_call" | custom-call | flops 3000000000 | bytes 6291456 | tf_op jit(solution)/shard_map/return_tiles/pallas_call | solution.py:264
  47.5 3.1 %collective-permute-start.7 = (f32[64,256]{1,0:T(8,128)S(1)}, f32[64,256]{1,0:T(8,128)S(1)}, u32[]{:S(2)}, u32[]{:S(2)}) collective-permute-start(f32[64,256]{1,0:T(8,128)S(1)} %get-tuple-element.42.below_ref), channel_id=1, source_target_pairs={{0,4},{4,0},{8,12},{12,8},{16,20},{20,16},{24,28},{28,24},{32,36},... | collective-permute-start | bytes 196616 | tf_op jit(solution)/shard_map/return_tiles/ppermute | solution.py:411
  50.6 0.7 collective-permute-start.8
  51.3 4.0 %edge_tiles.1.part_ref = f32[64,256]{1,0:T(8,128)S(1)} custom-call(s32[2]{0:T(128)S(1)} %pad_add_fusion.me_ref, f32[3]{0:T(128)S(1)} %copy-done.4, f32[64,256]{1,0:T(8,128)S(1)} %get-tuple-element.30.near_ref, f32[3,2,512,256]{3,2,1,0:T(8,128)S(1)} %get-tuple-element.31.edge_ref, bf16[2,64,3072]{2,1,0:T(8,128)(2,1)S(1)} %get-tuple-element.32.left_ref, ...), custom_call_target="tpu_custom_call" | custom-call | flops 5000000000 | bytes 20971520 | tf_op jit(solution)/shard_map/edge_tiles/pallas_call | solution.py:345
  55.3 0.0 collective-permute-done.7.from_below_ref
  55.3 0.0 collective-permute-done.8.from_above_ref
  55.3 0.8 sums.2
  56.1 15.3 %all-to-all-start = ((f32[256,1,256]{2,1,0:T(1,128)}), f32[256,1,256]{2,1,0:T(1,128)S(1)}, u32[]{:S(2)}, u32[]{:S(2)}) async-start(f32[256,1,256]{2,1,0:T(1,128)} %get-tuple-element.45), calls=%async_computation | async-start | bytes 524288 | tf_op jit(solution)/shard_map/sums/all_to_all | solution.py:417
  71.4 2.2 %collective-permute-start.9 = (f32[64,256]{1,0:T(8,128)S(1)}, f32[64,256]{1,0:T(8,128)S(1)}, u32[]{:S(2)}, u32[]{:S(2)}) collective-permute-start(f32[64,256]{1,0:T(8,128)S(1)} %get-tuple-element.44.refs_0_), channel_id=1, source_target_pairs={{0,1},{1,0},{2,3},{3,2},{4,5},{5,4},{6,7},{7,6},{8,9},{9,8},{10,11... | collective-permute-start | bytes 196616 | tf_op jit(solution)/shard_map/sums/ppermute | solution.py:419
  73.6 1.1 %collective-permute-start.10 = (f32[64,256]{1,0:T(8,128)S(1)}, f32[64,256]{1,0:T(8,128)S(1)}, u32[]{:S(2)}, u32[]{:S(2)}) collective-permute-start(f32[64,256]{1,0:T(8,128)S(1)} %get-tuple-element.44.refs_0_), channel_id=1, source_target_pairs={{0,2},{1,3},{2,0},{3,1},{4,6},{5,7},{6,4},{7,5},{8,10},{9,11},{10,... | collective-permute-start | bytes 196616 | tf_op jit(solution)/shard_map/sums/ppermute | solution.py:419
  74.7 2.1 %collective-permute-start.11 = (f32[64,256]{1,0:T(8,128)S(1)}, f32[64,256]{1,0:T(8,128)S(1)}, u32[]{:S(2)}, u32[]{:S(2)}) collective-permute-start(f32[64,256]{1,0:T(8,128)S(1)} %get-tuple-element.44.refs_0_), channel_id=1, source_target_pairs={{0,3},{1,2},{2,1},{3,0},{4,7},{5,6},{6,5},{7,4},{8,11},{9,10},{10,... | collective-permute-start | bytes 196616 | tf_op jit(solution)/shard_map/sums/ppermute | solution.py:419
  76.8 0.0 collective-permute-done.9.refs_1_
  76.9 2.4 %collective-permute-done.10.refs_2_ = f32[64,256]{1,0:T(8,128)S(1)} collective-permute-done((f32[64,256]{1,0:T(8,128)S(1)}, f32[64,256]{1,0:T(8,128)S(1)}, u32[]{:S(2)}, u32[]{:S(2)}) %collective-permute-start.10) | collective-permute-done | bytes 65568 | tf_op jit(solution)/shard_map/sums/ppermute | solution.py:419
  79.3 2.7 %collective-permute-done.11.refs_3_ = f32[64,256]{1,0:T(8,128)S(1)} collective-permute-done((f32[64,256]{1,0:T(8,128)S(1)}, f32[64,256]{1,0:T(8,128)S(1)}, u32[]{:S(2)}, u32[]{:S(2)}) %collective-permute-start.11) | collective-permute-done | bytes 65568 | tf_op jit(solution)/shard_map/sums/ppermute | solution.py:419
  82.0 5.0 %all-to-all-done.refs_4_ = f32[256,1,256]{2,1,0:T(1,128)S(1)} async-done(((f32[256,1,256]{2,1,0:T(1,128)}), f32[256,1,256]{2,1,0:T(1,128)S(1)}, u32[]{:S(2)}, u32[]{:S(2)}) %all-to-all-start) | async-done | bytes 262176 | tf_op jit(solution)/shard_map/sums/all_to_all | solution.py:417
  87.1 1.0 %sums.3 = (f32[1,4,64,64]{3,2,1,0:T(8,128)}, f32[4,1,64]{2,1,0:T(1,128)}) custom-call(f32[64,256]{1,0:T(8,128)S(1)} %get-tuple-element.44.refs_0_, f32[64,256]{1,0:T(8,128)S(1)} %collective-permute-done.9.refs_1_, f32[64,256]{1,0:T(8,128)S(1)} %collective-permute-done.10.refs_2_, f32[64,256]{1,0:T(8,128)S(1)} %collective-permute-done.11.refs_3_, ...), custom_call_target="tpu_custom_call" | custom-call | tf_op jit(solution)/shard_map/sums/pallas_call | solution.py:371
Async XLA Ops:
  0.6 37.3 %copy-start.4 = (f32[3]{0:T(128)S(1)}, f32[3]{0:T(128)}, u32[]{:S(2)}) copy-start(f32[3]{0:T(128)} %density_ref.5) | copy-start | bytes 40
  0.6 1.4 %copy-start = (bf16[16,3,2,64,128]{4,3,2,1,0:T(8,128)(2,1)S(1)}, bf16[16,3,2,64,128]{4,3,2,1,0:T(8,128)(2,1)}, u32[]{:S(2)}) copy-start(bf16[16,3,2,64,128]{4,3,2,1,0:T(8,128)(2,1)} %snaps_ref.1) | copy-start | bytes 4718596
  2.1 0.8 copy-start.1
  2.9 35.0 %copy-start.3 = (s32[2,64,128]{2,1,0:T(8,128)S(1)}, s32[2,64,128]{2,1,0:T(8,128)}, u32[]{:S(2)}) copy-start(s32[2,64,128]{2,1,0:T(8,128)} %refs_4_.3) | copy-start | bytes 196612
  4.2 6.6 %collective-permute-start = (bf16[3,2,18,16,128]{4,3,2,1,0:T(8,128)(2,1)S(1)}, bf16[3,2,18,16,128]{4,3,2,1,0:T(8,128)(2,1)S(1)}, u32[]{:S(2)}, u32[]{:S(2)}) collective-permute-start(bf16[3,2,18,16,128]{4,3,2,1,0:T(8,128)(2,1)S(1)} %get-tuple-element.26), channel_id=1, source_target_pairs={{0,1},{1,0},{2,3},{3,2},{4,5},{5,4},{6,7},{7,6},{8,9},{9,8},{10,11... | collective-permute-start | bytes 1327112 | tf_op jit(solution)/shard_map/regroup/ppermute | solution.py:391
  7.5 13.2 %collective-permute-start.1 = (bf16[3,2,18,16,128]{4,3,2,1,0:T(8,128)(2,1)S(1)}, bf16[3,2,18,16,128]{4,3,2,1,0:T(8,128)(2,1)S(1)}, u32[]{:S(2)}, u32[]{:S(2)}) collective-permute-start(bf16[3,2,18,16,128]{4,3,2,1,0:T(8,128)(2,1)S(1)} %get-tuple-element.27), channel_id=1, source_target_pairs={{0,2},{1,3},{2,0},{3,1},{4,6},{5,7},{6,4},{7,5},{8,10},{9,11},{10,... | collective-permute-start | bytes 1327112 | tf_op jit(solution)/shard_map/regroup/ppermute | solution.py:391
  8.7 27.8 %collective-permute-start.2 = (bf16[3,2,18,16,128]{4,3,2,1,0:T(8,128)(2,1)S(1)}, bf16[3,2,18,16,128]{4,3,2,1,0:T(8,128)(2,1)S(1)}, u32[]{:S(2)}, u32[]{:S(2)}) collective-permute-start(bf16[3,2,18,16,128]{4,3,2,1,0:T(8,128)(2,1)S(1)} %get-tuple-element.28), channel_id=1, source_target_pairs={{0,3},{1,2},{2,1},{3,0},{4,7},{5,6},{6,5},{7,4},{8,11},{9,10},{10,... | collective-permute-start | bytes 1327112 | tf_op jit(solution)/shard_map/regroup/ppermute | solution.py:391
  10.8 0.8 copy-start.2
  12.4 32.2 %collective-permute-start.3 = (bf16[7,10,16,128]{3,2,1,0:T(8,128)(2,1)S(1)}, bf16[7,10,16,128]{3,2,1,0:T(8,128)(2,1)S(1)}, u32[]{:S(2)}, u32[]{:S(2)}) collective-permute-start(bf16[7,10,16,128]{3,2,1,0:T(8,128)(2,1)S(1)} %get-tuple-element.35), channel_id=1, source_target_pairs={{0,4},{4,0},{8,12},{12,8},{16,20},{20,16},{24,28},{28,24},{32,36},... | collective-permute-start | bytes 860168 | tf_op jit(solution)/shard_map/halo/ppermute | solution.py:406
  12.5 32.1 %collective-permute-start.5 = (bf16[7,10,16,128]{3,2,1,0:T(8,128)(2,1)S(1)}, bf16[7,10,16,128]{3,2,1,0:T(8,128)(2,1)S(1)}, u32[]{:S(2)}, u32[]{:S(2)}) collective-permute-start(bf16[7,10,16,128]{3,2,1,0:T(8,128)(2,1)S(1)} %get-tuple-element.36), channel_id=1, source_target_pairs={{4,8},{8,4},{12,16},{16,12},{20,24},{24,20},{28,32},{32,28},{36,40... | collective-permute-start | bytes 860168 | tf_op jit(solution)/shard_map/halo/ppermute | solution.py:405
  37.1 7.4 %collective-permute-start.4 = (bf16[6,10,16,128]{3,2,1,0:T(8,128)(2,1)S(1)}, bf16[6,10,16,128]{3,2,1,0:T(8,128)(2,1)S(1)}, u32[]{:S(2)}, u32[]{:S(2)}) collective-permute-start(bf16[6,10,16,128]{3,2,1,0:T(8,128)(2,1)S(1)} %get-tuple-element.39), channel_id=1, source_target_pairs={{0,4},{4,0},{8,12},{12,8},{16,20},{20,16},{24,28},{28,24},{32,36},... | collective-permute-start | bytes 737288 | tf_op jit(solution)/shard_map/halo/ppermute | solution.py:406
  37.2 7.3 %collective-permute-start.6 = (bf16[6,10,16,128]{3,2,1,0:T(8,128)(2,1)S(1)}, bf16[6,10,16,128]{3,2,1,0:T(8,128)(2,1)S(1)}, u32[]{:S(2)}, u32[]{:S(2)}) collective-permute-start(bf16[6,10,16,128]{3,2,1,0:T(8,128)(2,1)S(1)} %get-tuple-element.40), channel_id=1, source_target_pairs={{4,8},{8,4},{12,16},{16,12},{20,24},{24,20},{28,32},{32,28},{36,40... | collective-permute-start | bytes 737288 | tf_op jit(solution)/shard_map/halo/ppermute | solution.py:405
  47.5 7.7 %collective-permute-start.7 = (f32[64,256]{1,0:T(8,128)S(1)}, f32[64,256]{1,0:T(8,128)S(1)}, u32[]{:S(2)}, u32[]{:S(2)}) collective-permute-start(f32[64,256]{1,0:T(8,128)S(1)} %get-tuple-element.42.below_ref), channel_id=1, source_target_pairs={{0,4},{4,0},{8,12},{12,8},{16,20},{20,16},{24,28},{28,24},{32,36},... | collective-permute-start | bytes 196616 | tf_op jit(solution)/shard_map/return_tiles/ppermute | solution.py:411
  50.6 4.6 %collective-permute-start.8 = (f32[64,256]{1,0:T(8,128)S(1)}, f32[64,256]{1,0:T(8,128)S(1)}, u32[]{:S(2)}, u32[]{:S(2)}) collective-permute-start(f32[64,256]{1,0:T(8,128)S(1)} %get-tuple-element.43.above_ref), channel_id=1, source_target_pairs={{4,8},{8,4},{12,16},{16,12},{20,24},{24,20},{28,32},{32,28},{36,40... | collective-permute-start | bytes 196616 | tf_op jit(solution)/shard_map/return_tiles/ppermute | solution.py:412
  56.1 31.0 %all-to-all-start = ((f32[256,1,256]{2,1,0:T(1,128)}), f32[256,1,256]{2,1,0:T(1,128)S(1)}, u32[]{:S(2)}, u32[]{:S(2)}) async-start(f32[256,1,256]{2,1,0:T(1,128)} %get-tuple-element.45), calls=%async_computation | async-start | bytes 524288 | tf_op jit(solution)/shard_map/sums/all_to_all | solution.py:417
  71.4 5.5 %collective-permute-start.9 = (f32[64,256]{1,0:T(8,128)S(1)}, f32[64,256]{1,0:T(8,128)S(1)}, u32[]{:S(2)}, u32[]{:S(2)}) collective-permute-start(f32[64,256]{1,0:T(8,128)S(1)} %get-tuple-element.44.refs_0_), channel_id=1, source_target_pairs={{0,1},{1,0},{2,3},{3,2},{4,5},{5,4},{6,7},{7,6},{8,9},{9,8},{10,11... | collective-permute-start | bytes 196616 | tf_op jit(solution)/shard_map/sums/ppermute | solution.py:419
  73.6 5.7 %collective-permute-start.10 = (f32[64,256]{1,0:T(8,128)S(1)}, f32[64,256]{1,0:T(8,128)S(1)}, u32[]{:S(2)}, u32[]{:S(2)}) collective-permute-start(f32[64,256]{1,0:T(8,128)S(1)} %get-tuple-element.44.refs_0_), channel_id=1, source_target_pairs={{0,2},{1,3},{2,0},{3,1},{4,6},{5,7},{6,4},{7,5},{8,10},{9,11},{10,... | collective-permute-start | bytes 196616 | tf_op jit(solution)/shard_map/sums/ppermute | solution.py:419
  74.7 7.3 %collective-permute-start.11 = (f32[64,256]{1,0:T(8,128)S(1)}, f32[64,256]{1,0:T(8,128)S(1)}, u32[]{:S(2)}, u32[]{:S(2)}) collective-permute-start(f32[64,256]{1,0:T(8,128)S(1)} %get-tuple-element.44.refs_0_), channel_id=1, source_target_pairs={{0,3},{1,2},{2,1},{3,0},{4,7},{5,6},{6,5},{7,4},{8,11},{9,10},{10,... | collective-permute-start | bytes 196616 | tf_op jit(solution)/shard_map/sums/ppermute | solution.py:419

commit v5 on v4

--- a/solution.py
+++ b/solution.py
@@ -73,20 +73,23 @@
     return [block[first + dy : first + dy + height].reshape(height * members, depth) for dy in range(3)]
 
 
-def density_at(label, density_ref, materials):
+def at_cells(label, density_ref, materials, members):
     density = jnp.zeros(label.shape, jnp.float32)
+    shown = []
     for j in range(materials):
-        density = density + jnp.where(label == j, density_ref[j] * (1.0 / 216.0), 0.0)
-    return density
-
-
-def put_images(image, label, density, right, start, lanes, count, materials):
+        here = jnp.where(label == j, 1.0, 0.0)
+        density = density + here * (density_ref[j] * (1.0 / 216.0))
+        shown.append(jnp.broadcast_to(here, (members, label.shape[1])).astype(jnp.bfloat16))
+    return density, shown
+
+
+def put_images(image, shown, density, right, start, lanes, count):
     members, depth = image.shape[0], image.shape[1] // 2
     right[pl.ds(start, members), lanes] = (image[:, :depth] * density).astype(right.dtype)
-    stiff = image[:, depth:] * (1.0 / 36.0)
-    for j in range(materials):
+    stiff = (image[:, depth:] * (1.0 / 36.0)).astype(right.dtype)
+    for j, here in enumerate(shown):
         at = pl.multiple_of((j + 1) * count + start, members)
-        right[pl.ds(at, members), lanes] = jnp.where(label == j, stiff, 0.0).astype(right.dtype)
+        right[pl.ds(at, members), lanes] = stiff * here
 
 
 def correlate(left, right):
@@ -95,7 +98,8 @@
 
 def local_kernel(groups, materials, me_ref, density_ref, *refs):
     sources = refs[:groups]
-    labels_ref, weights_ref, part_ref, edge_ref, cross_ref, left_ref, near_left, near_right = refs[groups:]
+    labels_ref, weights_ref, part_ref, edge_ref, cross_ref, left_ref = refs[groups : groups + 6]
+    scratch = refs[groups + 6 :]
     me = me_ref[0]
     comps, planes, reach, members, depth = sources[0].shape
     width = reach - 2
@@ -103,8 +107,9 @@
     count = groups * members
     wide = 2 * depth
 
-    @pl.loop(0, comps)
-    def _(c):
+    part = 0.0
+    for c in range(comps):
+        near_left, near_right = scratch[2 * c : 2 * c + 2]
         for g in range(2):
             first = g * half
             lhs = jnp.concatenate(
@@ -125,19 +130,20 @@
             inner = both[:, (1 - g) * wide : (2 - g) * wide]
             for y in range(half):
                 label = labels_ref[1 - g, pl.ds(me * width + first + y, 1), :]
-                density = density_at(label, density_ref, materials)
-                near = pl.ds(pl.multiple_of(((c * 2 + g) * half + y) * depth, depth), depth)
-                edge = pl.ds(pl.multiple_of((c * half + y) * depth, depth), depth)
+                density, shown = at_cells(label, density_ref, materials, members)
+                near = slice((g * half + y) * depth, (g * half + y + 1) * depth)
+                edge = slice((c * half + y) * depth, (c * half + y + 1) * depth)
                 for m in range(groups):
                     start = pl.multiple_of((me ^ m) * members, members)
                     near_left[pl.ds(start, members), near] = sources[m][c, 1 - g, first + y + 1]
                     left_ref[g, pl.ds(start, members), edge] = sources[m][c, g, first + y + 1]
                     at = (m * half + y) * members
                     put_images(
-                        inner[at : at + members], label, density, near_right, start, near, count, materials
+                        inner[at : at + members], shown, density, near_right, start, near, count
                     )
 
-    part_ref[...] = correlate(near_left[...], near_right[...])
+        part = part + correlate(near_left[...], near_right[...])
+    part_ref[...] = part
 
 
 def vmem_spec():
@@ -206,9 +212,10 @@
         in_specs=[smem_spec(), smem_spec()] + [vmem_spec()] * (groups + 2),
         out_specs=[vmem_spec()] * 4,
         scratch_shapes=[
-            pltpu.VMEM((count, comps * 2 * half * depth), jnp.bfloat16),
-            pltpu.VMEM((columns, comps * 2 * half * depth), jnp.bfloat16),
-        ],
+            pltpu.VMEM((count, 2 * half * depth), jnp.bfloat16),
+            pltpu.VMEM((columns, 2 * half * depth), jnp.bfloat16),
+        ]
+        * comps,
         compiler_params=pltpu.CompilerParams(vmem_limit_bytes=40 * 2**20),
         cost_estimate=pl.CostEstimate(flops=5 * 10**9, bytes_accessed=12 * 2**20, transcendentals=0),
     )(me, density, *blocks, labels, weights)
@@ -224,32 +231,33 @@
 
 def returns_kernel(groups, materials, pairs, me_ref, density_ref, cross_ref, *refs):
     sides = (refs[:pairs], refs[pairs : 2 * pairs])
-    below_ref, above_ref, left, right = refs[2 * pairs :]
+    below_ref, above_ref = refs[2 * pairs : 2 * pairs + 2]
+    scratch = refs[2 * pairs + 2 :]
     me = me_ref[0]
     comps = cross_ref.shape[0]
     reach, members, depth = sides[0][0].shape[1:]
     half = reach - 2
     count = groups * members
 
-    @pl.loop(0, comps)
-    def _(c):
+    sums = [0.0, 0.0]
+    for c in range(comps):
         for side in range(2):
+            left, right = scratch[2 * (2 * c + side) : 2 * (2 * c + side) + 2]
             g = me_ref[1] if side else 1 - me_ref[1]
             cross = cross_ref[c, g]
             for y in range(half):
                 label = sides[side][0][sides[side][0].shape[0] - 1, y].astype(jnp.float32)
-                density = density_at(label, density_ref, materials)
-                lanes = pl.ds(pl.multiple_of((c * half + y) * depth, depth), depth)
+                density, shown = at_cells(label, density_ref, materials, members)
+                lanes = slice(y * depth, (y + 1) * depth)
                 for m in range(groups):
                     start = pl.multiple_of((me ^ m) * members, members)
-                    left[side, pl.ds(start, members), lanes] = received_at(sides[side], m, comps, c)[y + 1]
+                    left[pl.ds(start, members), lanes] = received_at(sides[side], m, comps, c)[y + 1]
                     at = (m * half + y) * members
-                    put_images(
-                        cross[at : at + members], label, density, right.at[side], start, lanes, count, materials
-                    )
-
-    below_ref[...] = correlate(left[0], right[0])
-    above_ref[...] = correlate(left[1], right[1])
+                    put_images(cross[at : at + members], shown, density, right, start, lanes, count)
+
+            sums[side] = sums[side] + correlate(left[...], right[...])
+    below_ref[...] = sums[0]
+    above_ref[...] = sums[1]
 
 
 def return_tiles(cross, lows, highs, density, me, groups):
@@ -267,9 +275,10 @@
         in_specs=[smem_spec(), smem_spec()] + [vmem_spec()] * (1 + len(halos)),
         out_specs=[vmem_spec()] * 2,
         scratch_shapes=[
-            pltpu.VMEM((2, count, cells), jnp.bfloat16),
-            pltpu.VMEM((2, columns, cells), jnp.bfloat16),
-        ],
+            pltpu.VMEM((count, cells // comps), jnp.bfloat16),
+            pltpu.VMEM((columns, cells // comps), jnp.bfloat16),
+        ]
+        * (2 * comps),
         compiler_params=pltpu.CompilerParams(vmem_limit_bytes=40 * 2**20),
         cost_estimate=pl.CostEstimate(flops=3 * 10**9, bytes_accessed=6 * 2**20, transcendentals=0),
     )(me, density, cross, *halos)
@@ -277,7 +286,8 @@
 
 def edge_kernel(groups, materials, pairs, me_ref, density_ref, near_ref, edge_ref, left_ref, *refs):
     sides = (refs[:pairs], refs[pairs : 2 * pairs])
-    labels_ref, weights_ref, part_ref, right = refs[2 * pairs :]
+    labels_ref, weights_ref, part_ref = refs[2 * pairs : 2 * pairs + 3]
+    rights = refs[2 * pairs + 3 :]
     me = me_ref[0]
     comps = edge_ref.shape[0]
     reach, members, depth = sides[0][0].shape[1:]
@@ -285,9 +295,10 @@
     width = 2 * half
     count = groups * members
 
-    @pl.loop(0, comps)
-    def _(c):
+    part = near_ref[...]
+    for c in range(comps):
         for side in range(2):
+            right = rights[2 * c + side]
             g = me_ref[1] if side else 1 - me_ref[1]
             lhs = jnp.concatenate(
                 [
@@ -299,16 +310,15 @@
             image = edge_ref[c, g] + jnp.dot(lhs, weights_ref[3 * depth : 6 * depth, : 2 * depth], preferred_element_type=jnp.float32)
             for y in range(half):
                 label = labels_ref[g, pl.ds(me * width + g * half + y, 1), :]
-                density = density_at(label, density_ref, materials)
-                lanes = pl.ds(pl.multiple_of((c * half + y) * depth, depth), depth)
+                density, shown = at_cells(label, density_ref, materials, members)
+                lanes = slice(y * depth, (y + 1) * depth)
                 for m in range(groups):
                     start = pl.multiple_of((me ^ m) * members, members)
                     at = (m * half + y) * members
-                    put_images(
-                        image[at : at + members], label, density, right.at[g], start, lanes, count, materials
-                    )
-
-    part_ref[...] = near_ref[...] + correlate(left_ref[0], right[0]) + correlate(left_ref[1], right[1])
+                    put_images(image[at : at + members], shown, density, right, start, lanes, count)
+
+            part = part + correlate(left_ref[g, :, c * half * depth : (c + 1) * half * depth], right[...])
+    part_ref[...] = part
 
 
 def combine_kernel(part_ref, below_ref, above_ref, from_below_ref, from_above_ref, slab_ref, wide_ref):
@@ -347,7 +357,7 @@
         out_shape=part,
         in_specs=[smem_spec(), smem_spec()] + [vmem_spec()] * (5 + len(halos)),
         out_specs=vmem_spec(),
-        scratch_shapes=[pltpu.VMEM((2, columns, left.shape[2]), jnp.bfloat16)],
+        scratch_shapes=[pltpu.VMEM((columns, left.shape[2] // edge.shape[0]), jnp.bfloat16)] * (2 * edge.shape[0]),
         compiler_params=pltpu.CompilerParams(vmem_limit_bytes=40 * 2**20),
         cost_estimate=pl.CostEstimate(flops=5 * 10**9, bytes_accessed=20 * 2**20, transcendentals=0),
     )(me, density, near, edge, left, *halos, labels, weights)

time: 88.4 us -> 87.4 us (0.989)
  Pallas kernels: 17.3 us -> 15.7 us
  transfers between devices with their start and end apart: 13 -> 13, of which waited for: 6 -> 6; matrix products, arithmetic and copies ran while one was open for 0% -> 0% of each run, Pallas kernels for 13% -> 12%
where the time goes in v5:
time: 87.4 us; the launch traced here: 87.1 us
  waiting for transfers between devices  34.3 us (39%)
  starting transfers between devices  33.2 us (38%)
  Pallas kernels  15.7 us (18%)
  local copies, waits for them, and re-layouts  3.09 us (4%)
    ppermute x3, waiting for transfers between devices, body(): lax.ppermute(mine[m], 'snap', [(i, i ^ m) for i in range(groups)])  23.4 us
    all_to_all x1, starting transfers between devices, body(): sent = lax.all_to_all(wide, ('space', 'snap'), 0, 0, tiled=True)  15.8 us
    ppermute x3, starting transfers between devices, body(): lax.ppermute(mine[m], 'snap', [(i, i ^ m) for i in range(groups)])  6.56 us
    pallas_call x1, Pallas kernels, local_tiles(): pl.pallas_call(functools.partial(local_kernel, groups, density.shape[0]),...  5.96 us
    ppermute x3, starting transfers between devices, body(): lax.ppermute(part, 'snap', [(i, i ^ m) for i in range(groups)])  5.47 us
    ppermute x3, waiting for transfers between devices, body(): lax.ppermute(part, 'snap', [(i, i ^ m) for i in range(groups)])  5.18 us
    all_to_all x1, waiting for transfers between devices, body(): sent = lax.all_to_all(wide, ('space', 'snap'), 0, 0, tiled=True)  5.02 us
    pallas_call x1, Pallas kernels, edge_tiles(): pl.pallas_call(functools.partial(edge_kernel, groups, materials, len(lows...  3.17 us
  transfers between devices with their start and end apart: 13, of which 6 were waited for; matrix products, arithmetic and copies ran while one was open for 0% of the time, Pallas kernels for 12%

profile of v5, /device:TPU:1, one launch (start us, length us, event | category | flops | bytes accessed | tf_op | source)
XLA Modules:
  0.0 87.1 jit_solution(17988634038396465448)
XLA Ops:
  0.6 0.0 copy-start.4
  0.6 0.0 copy-start
  0.7 1.4 %copy-done = bf16[16,3,2,64,128]{4,3,2,1,0:T(8,128)(2,1)S(1)} copy-done((bf16[16,3,2,64,128]{4,3,2,1,0:T(8,128)(2,1)S(1)}, bf16[16,3,2,64,128]{4,3,2,1,0:T(8,128)(2,1)}, u32[]{:S(2)}) %copy-start) | copy-done | bytes 1572888
  2.1 0.0 copy-start.1
  2.1 0.8 copy-done.1
  2.9 0.0 copy-start.3
  2.9 1.3 %spread.1 = (bf16[3,2,18,16,128]{4,3,2,1,0:T(8,128)(2,1)S(1)}, bf16[3,2,18,16,128]{4,3,2,1,0:T(8,128)(2,1)S(1)}, bf16[3,2,18,16,128]{4,3,2,1,0:T(8,128)(2,1)S(1)}, bf16[3,2,18,16,128]{4,3,2,1,0:T(8,128)(2,1)S(1)}) custom-call(s32[1]{0:T(128)} %bitcast.me_ref, bf16[16,3,2,64,128]{4,3,2,1,0:T(8,128)(2,1)S(1)} %copy-done, s32[2,64,128]{2,1,0:T(8,128)S(1)} %copy-done.1), custom_call_target="tpu_custom_call" | custom-call | bytes 5242880 | tf_op jit(solution)/shard_map/spread/pallas_call | solution.py:31
  4.2 3.3 %collective-permute-start = (bf16[3,2,18,16,128]{4,3,2,1,0:T(8,128)(2,1)S(1)}, bf16[3,2,18,16,128]{4,3,2,1,0:T(8,128)(2,1)S(1)}, u32[]{:S(2)}, u32[]{:S(2)}) collective-permute-start(bf16[3,2,18,16,128]{4,3,2,1,0:T(8,128)(2,1)S(1)} %get-tuple-element.26), channel_id=1, source_target_pairs={{0,1},{1,0},{2,3},{3,2},{4,5},{5,4},{6,7},{7,6},{8,9},{9,8},{10,11... | collective-permute-start | bytes 1327112 | tf_op jit(solution)/shard_map/regroup/ppermute | solution.py:401
  7.5 1.2 %collective-permute-start.1 = (bf16[3,2,18,16,128]{4,3,2,1,0:T(8,128)(2,1)S(1)}, bf16[3,2,18,16,128]{4,3,2,1,0:T(8,128)(2,1)S(1)}, u32[]{:S(2)}, u32[]{:S(2)}) collective-permute-start(bf16[3,2,18,16,128]{4,3,2,1,0:T(8,128)(2,1)S(1)} %get-tuple-element.27), channel_id=1, source_target_pairs={{0,2},{1,3},{2,0},{3,1},{4,6},{5,7},{6,4},{7,5},{8,10},{9,11},{10,... | collective-permute-start | bytes 1327112 | tf_op jit(solution)/shard_map/regroup/ppermute | solution.py:401
  8.7 2.0 %collective-permute-start.2 = (bf16[3,2,18,16,128]{4,3,2,1,0:T(8,128)(2,1)S(1)}, bf16[3,2,18,16,128]{4,3,2,1,0:T(8,128)(2,1)S(1)}, u32[]{:S(2)}, u32[]{:S(2)}) collective-permute-start(bf16[3,2,18,16,128]{4,3,2,1,0:T(8,128)(2,1)S(1)} %get-tuple-element.28), channel_id=1, source_target_pairs={{0,3},{1,2},{2,1},{3,0},{4,7},{5,6},{6,5},{7,4},{8,11},{9,10},{10,... | collective-permute-start | bytes 1327112 | tf_op jit(solution)/shard_map/regroup/ppermute | solution.py:401
  10.7 0.1 pad_add_fusion.me_ref
  10.8 0.0 collective-permute-done.refs_1_
  10.8 0.0 copy-start.2
  10.8 0.8 copy-done.2
  11.7 0.7 halo.2
  12.4 0.1 collective-permute-start.3
  12.5 0.7 collective-permute-start.5
  13.1 7.6 %collective-permute-done.1.refs_2_.refs_0_ = bf16[3,2,18,16,128]{4,3,2,1,0:T(8,128)(2,1)S(1)} collective-permute-done((bf16[3,2,18,16,128]{4,3,2,1,0:T(8,128)(2,1)S(1)}, bf16[3,2,18,16,128]{4,3,2,1,0:T(8,128)(2,1)S(1)}, u32[]{:S(2)}, u32[]{:S(2)}) %collective-permute-start.1) | collective-permute-done | bytes 442400 | tf_op jit(solution)/shard_map/regroup/ppermute | solution.py:401
  20.7 15.8 %collective-permute-done.2.refs_3_.refs_1_ = bf16[3,2,18,16,128]{4,3,2,1,0:T(8,128)(2,1)S(1)} collective-permute-done((bf16[3,2,18,16,128]{4,3,2,1,0:T(8,128)(2,1)S(1)}, bf16[3,2,18,16,128]{4,3,2,1,0:T(8,128)(2,1)S(1)}, u32[]{:S(2)}, u32[]{:S(2)}) %collective-permute-start.2) | collective-permute-done | bytes 442400 | tf_op jit(solution)/shard_map/regroup/ppermute | solution.py:401
  36.6 0.6 halo.3
  37.1 0.1 collective-permute-start.4
  37.2 0.7 collective-permute-start.6
  37.9 0.0 copy-done.4
  37.9 0.0 copy-done.3
  37.9 6.0 %local_tiles.1 = (f32[64,256]{1,0:T(8,128)S(1)}, f32[3,2,512,256]{3,2,1,0:T(8,128)S(1)}, f32[3,2,512,256]{3,2,1,0:T(8,128)S(1)}, bf16[2,64,3072]{2,1,0:T(8,128)(2,1)S(1)}) custom-call(s32[2]{0:T(128)S(1)} %pad_add_fusion.me_ref, f32[3]{0:T(128)S(1)} %copy-done.4, bf16[3,2,18,16,128]{4,3,2,1,0:T(8,128)(2,1)S(1)} %get-tuple-element.25.refs_0_, ...), custom_call_target="tpu_custom_call" | custom-call | flops 5000000000 | bytes 12582912 | tf_op jit(solution)/shard_map/local_tiles/pallas_call | solution.py:204
  43.9 0.7 collective-permute-done.4.refs_1_
  44.6 0.0 collective-permute-done.6.refs_3_
  44.6 0.0 collective-permute-done.3.refs_0_
  44.6 0.0 collective-permute-done.5.refs_2_
  44.6 2.3 %return_tiles.1 = (f32[64,256]{1,0:T(8,128)S(1)}, f32[64,256]{1,0:T(8,128)S(1)}) custom-call(s32[2]{0:T(128)S(1)} %pad_add_fusion.me_ref, f32[3]{0:T(128)S(1)} %copy-done.4, f32[3,2,512,256]{3,2,1,0:T(8,128)S(1)} %get-tuple-element.41.cross_ref, bf16[7,10,16,128]{3,2,1,0:T(8,128)(2,1)S(1)} %collective-permute-done.3.refs_0_, ...), custom_call_target="tpu_custom_call" | custom-call | flops 3000000000 | bytes 6291456 | tf_op jit(solution)/shard_map/return_tiles/pallas_call | solution.py:272
  46.9 3.1 %collective-permute-start.7 = (f32[64,256]{1,0:T(8,128)S(1)}, f32[64,256]{1,0:T(8,128)S(1)}, u32[]{:S(2)}, u32[]{:S(2)}) collective-permute-start(f32[64,256]{1,0:T(8,128)S(1)} %get-tuple-element.42.below_ref), channel_id=1, source_target_pairs={{0,4},{4,0},{8,12},{12,8},{16,20},{20,16},{24,28},{28,24},{32,36},... | collective-permute-start | bytes 196616 | tf_op jit(solution)/shard_map/return_tiles/ppermute | solution.py:421
  50.0 0.7 collective-permute-start.8
  50.6 3.2 %edge_tiles.1.part_ref = f32[64,256]{1,0:T(8,128)S(1)} custom-call(s32[2]{0:T(128)S(1)} %pad_add_fusion.me_ref, f32[3]{0:T(128)S(1)} %copy-done.4, f32[64,256]{1,0:T(8,128)S(1)} %get-tuple-element.30.near_ref, f32[3,2,512,256]{3,2,1,0:T(8,128)S(1)} %get-tuple-element.31.edge_ref, bf16[2,64,3072]{2,1,0:T(8,128)(2,1)S(1)} %get-tuple-element.32.left_ref, ...), custom_call_target="tpu_custom_call" | custom-call | flops 5000000000 | bytes 20971520 | tf_op jit(solution)/shard_map/edge_tiles/pallas_call | solution.py:355
  53.8 0.0 collective-permute-done.7.from_below_ref
  53.8 0.0 collective-permute-done.8.from_above_ref
  53.8 0.8 sums.2
  54.6 15.8 %all-to-all-start = ((f32[256,1,256]{2,1,0:T(1,128)}), f32[256,1,256]{2,1,0:T(1,128)S(1)}, u32[]{:S(2)}, u32[]{:S(2)}) async-start(f32[256,1,256]{2,1,0:T(1,128)} %get-tuple-element.45), calls=%async_computation | async-start | bytes 524288 | tf_op jit(solution)/shard_map/sums/all_to_all | solution.py:427
  70.5 2.2 %collective-permute-start.9 = (f32[64,256]{1,0:T(8,128)S(1)}, f32[64,256]{1,0:T(8,128)S(1)}, u32[]{:S(2)}, u32[]{:S(2)}) collective-permute-start(f32[64,256]{1,0:T(8,128)S(1)} %get-tuple-element.44.refs_0_), channel_id=1, source_target_pairs={{0,1},{1,0},{2,3},{3,2},{4,5},{5,4},{6,7},{7,6},{8,9},{9,8},{10,11... | collective-permute-start | bytes 196616 | tf_op jit(solution)/shard_map/sums/ppermute | solution.py:429
  72.7 1.1 %collective-permute-start.10 = (f32[64,256]{1,0:T(8,128)S(1)}, f32[64,256]{1,0:T(8,128)S(1)}, u32[]{:S(2)}, u32[]{:S(2)}) collective-permute-start(f32[64,256]{1,0:T(8,128)S(1)} %get-tuple-element.44.refs_0_), channel_id=1, source_target_pairs={{0,2},{1,3},{2,0},{3,1},{4,6},{5,7},{6,4},{7,5},{8,10},{9,11},{10,... | collective-permute-start | bytes 196616 | tf_op jit(solution)/shard_map/sums/ppermute | solution.py:429
  73.8 2.1 %collective-permute-start.11 = (f32[64,256]{1,0:T(8,128)S(1)}, f32[64,256]{1,0:T(8,128)S(1)}, u32[]{:S(2)}, u32[]{:S(2)}) collective-permute-start(f32[64,256]{1,0:T(8,128)S(1)} %get-tuple-element.44.refs_0_), channel_id=1, source_target_pairs={{0,3},{1,2},{2,1},{3,0},{4,7},{5,6},{6,5},{7,4},{8,11},{9,10},{10,... | collective-permute-start | bytes 196616 | tf_op jit(solution)/shard_map/sums/ppermute | solution.py:429
  75.9 0.0 collective-permute-done.9.refs_1_
  75.9 2.4 %collective-permute-done.10.refs_2_ = f32[64,256]{1,0:T(8,128)S(1)} collective-permute-done((f32[64,256]{1,0:T(8,128)S(1)}, f32[64,256]{1,0:T(8,128)S(1)}, u32[]{:S(2)}, u32[]{:S(2)}) %collective-permute-start.10) | collective-permute-done | bytes 65568 | tf_op jit(solution)/shard_map/sums/ppermute | solution.py:429
  78.4 2.7 %collective-permute-done.11.refs_3_ = f32[64,256]{1,0:T(8,128)S(1)} collective-permute-done((f32[64,256]{1,0:T(8,128)S(1)}, f32[64,256]{1,0:T(8,128)S(1)}, u32[]{:S(2)}, u32[]{:S(2)}) %collective-permute-start.11) | collective-permute-done | bytes 65568 | tf_op jit(solution)/shard_map/sums/ppermute | solution.py:429
  81.1 5.0 %all-to-all-done.refs_4_ = f32[256,1,256]{2,1,0:T(1,128)S(1)} async-done(((f32[256,1,256]{2,1,0:T(1,128)}), f32[256,1,256]{2,1,0:T(1,128)S(1)}, u32[]{:S(2)}, u32[]{:S(2)}) %all-to-all-start) | async-done | bytes 262176 | tf_op jit(solution)/shard_map/sums/all_to_all | solution.py:427
  86.1 1.0 %sums.3 = (f32[1,4,64,64]{3,2,1,0:T(8,128)}, f32[4,1,64]{2,1,0:T(1,128)}) custom-call(f32[64,256]{1,0:T(8,128)S(1)} %get-tuple-element.44.refs_0_, f32[64,256]{1,0:T(8,128)S(1)} %collective-permute-done.9.refs_1_, f32[64,256]{1,0:T(8,128)S(1)} %collective-permute-done.10.refs_2_, f32[64,256]{1,0:T(8,128)S(1)} %collective-permute-done.11.refs_3_, ...), custom_call_target="tpu_custom_call" | custom-call | tf_op jit(solution)/shard_map/sums/pallas_call | solution.py:381
Async XLA Ops:
  0.6 37.3 %copy-start.4 = (f32[3]{0:T(128)S(1)}, f32[3]{0:T(128)}, u32[]{:S(2)}) copy-start(f32[3]{0:T(128)} %density_ref.5) | copy-start | bytes 40
  0.6 1.4 %copy-start = (bf16[16,3,2,64,128]{4,3,2,1,0:T(8,128)(2,1)S(1)}, bf16[16,3,2,64,128]{4,3,2,1,0:T(8,128)(2,1)}, u32[]{:S(2)}) copy-start(bf16[16,3,2,64,128]{4,3,2,1,0:T(8,128)(2,1)} %snaps_ref.1) | copy-start | bytes 4718596
  2.1 0.8 copy-start.1
  2.9 35.0 %copy-start.3 = (s32[2,64,128]{2,1,0:T(8,128)S(1)}, s32[2,64,128]{2,1,0:T(8,128)}, u32[]{:S(2)}) copy-start(s32[2,64,128]{2,1,0:T(8,128)} %refs_4_.3) | copy-start | bytes 196612
  4.2 6.6 %collective-permute-start = (bf16[3,2,18,16,128]{4,3,2,1,0:T(8,128)(2,1)S(1)}, bf16[3,2,18,16,128]{4,3,2,1,0:T(8,128)(2,1)S(1)}, u32[]{:S(2)}, u32[]{:S(2)}) collective-permute-start(bf16[3,2,18,16,128]{4,3,2,1,0:T(8,128)(2,1)S(1)} %get-tuple-element.26), channel_id=1, source_target_pairs={{0,1},{1,0},{2,3},{3,2},{4,5},{5,4},{6,7},{7,6},{8,9},{9,8},{10,11... | collective-permute-start | bytes 1327112 | tf_op jit(solution)/shard_map/regroup/ppermute | solution.py:401
  7.5 13.2 %collective-permute-start.1 = (bf16[3,2,18,16,128]{4,3,2,1,0:T(8,128)(2,1)S(1)}, bf16[3,2,18,16,128]{4,3,2,1,0:T(8,128)(2,1)S(1)}, u32[]{:S(2)}, u32[]{:S(2)}) collective-permute-start(bf16[3,2,18,16,128]{4,3,2,1,0:T(8,128)(2,1)S(1)} %get-tuple-element.27), channel_id=1, source_target_pairs={{0,2},{1,3},{2,0},{3,1},{4,6},{5,7},{6,4},{7,5},{8,10},{9,11},{10,... | collective-permute-start | bytes 1327112 | tf_op jit(solution)/shard_map/regroup/ppermute | solution.py:401
  8.7 27.8 %collective-permute-start.2 = (bf16[3,2,18,16,128]{4,3,2,1,0:T(8,128)(2,1)S(1)}, bf16[3,2,18,16,128]{4,3,2,1,0:T(8,128)(2,1)S(1)}, u32[]{:S(2)}, u32[]{:S(2)}) collective-permute-start(bf16[3,2,18,16,128]{4,3,2,1,0:T(8,128)(2,1)S(1)} %get-tuple-element.28), channel_id=1, source_target_pairs={{0,3},{1,2},{2,1},{3,0},{4,7},{5,6},{6,5},{7,4},{8,11},{9,10},{10,... | collective-permute-start | bytes 1327112 | tf_op jit(solution)/shard_map/regroup/ppermute | solution.py:401
  10.8 0.8 copy-start.2
  12.4 32.2 %collective-permute-start.3 = (bf16[7,10,16,128]{3,2,1,0:T(8,128)(2,1)S(1)}, bf16[7,10,16,128]{3,2,1,0:T(8,128)(2,1)S(1)}, u32[]{:S(2)}, u32[]{:S(2)}) collective-permute-start(bf16[7,10,16,128]{3,2,1,0:T(8,128)(2,1)S(1)} %get-tuple-element.35), channel_id=1, source_target_pairs={{0,4},{4,0},{8,12},{12,8},{16,20},{20,16},{24,28},{28,24},{32,36},... | collective-permute-start | bytes 860168 | tf_op jit(solution)/shard_map/halo/ppermute | solution.py:416
  12.5 32.1 %collective-permute-start.5 = (bf16[7,10,16,128]{3,2,1,0:T(8,128)(2,1)S(1)}, bf16[7,10,16,128]{3,2,1,0:T(8,128)(2,1)S(1)}, u32[]{:S(2)}, u32[]{:S(2)}) collective-permute-start(bf16[7,10,16,128]{3,2,1,0:T(8,128)(2,1)S(1)} %get-tuple-element.36), channel_id=1, source_target_pairs={{4,8},{8,4},{12,16},{16,12},{20,24},{24,20},{28,32},{32,28},{36,40... | collective-permute-start | bytes 860168 | tf_op jit(solution)/shard_map/halo/ppermute | solution.py:415
  37.1 7.4 %collective-permute-start.4 = (bf16[6,10,16,128]{3,2,1,0:T(8,128)(2,1)S(1)}, bf16[6,10,16,128]{3,2,1,0:T(8,128)(2,1)S(1)}, u32[]{:S(2)}, u32[]{:S(2)}) collective-permute-start(bf16[6,10,16,128]{3,2,1,0:T(8,128)(2,1)S(1)} %get-tuple-element.39), channel_id=1, source_target_pairs={{0,4},{4,0},{8,12},{12,8},{16,20},{20,16},{24,28},{28,24},{32,36},... | collective-permute-start | bytes 737288 | tf_op jit(solution)/shard_map/halo/ppermute | solution.py:416
  37.2 7.3 %collective-permute-start.6 = (bf16[6,10,16,128]{3,2,1,0:T(8,128)(2,1)S(1)}, bf16[6,10,16,128]{3,2,1,0:T(8,128)(2,1)S(1)}, u32[]{:S(2)}, u32[]{:S(2)}) collective-permute-start(bf16[6,10,16,128]{3,2,1,0:T(8,128)(2,1)S(1)} %get-tuple-element.40), channel_id=1, source_target_pairs={{4,8},{8,4},{12,16},{16,12},{20,24},{24,20},{28,32},{32,28},{36,40... | collective-permute-start | bytes 737288 | tf_op jit(solution)/shard_map/halo/ppermute | solution.py:415
  46.9 6.9 %collective-permute-start.7 = (f32[64,256]{1,0:T(8,128)S(1)}, f32[64,256]{1,0:T(8,128)S(1)}, u32[]{:S(2)}, u32[]{:S(2)}) collective-permute-start(f32[64,256]{1,0:T(8,128)S(1)} %get-tuple-element.42.below_ref), channel_id=1, source_target_pairs={{0,4},{4,0},{8,12},{12,8},{16,20},{20,16},{24,28},{28,24},{32,36},... | collective-permute-start | bytes 196616 | tf_op jit(solution)/shard_map/return_tiles/ppermute | solution.py:421
  50.0 3.9 %collective-permute-start.8 = (f32[64,256]{1,0:T(8,128)S(1)}, f32[64,256]{1,0:T(8,128)S(1)}, u32[]{:S(2)}, u32[]{:S(2)}) collective-permute-start(f32[64,256]{1,0:T(8,128)S(1)} %get-tuple-element.43.above_ref), channel_id=1, source_target_pairs={{4,8},{8,4},{12,16},{16,12},{20,24},{24,20},{28,32},{32,28},{36,40... | collective-permute-start | bytes 196616 | tf_op jit(solution)/shard_map/return_tiles/ppermute | solution.py:422
  54.6 31.5 %all-to-all-start = ((f32[256,1,256]{2,1,0:T(1,128)}), f32[256,1,256]{2,1,0:T(1,128)S(1)}, u32[]{:S(2)}, u32[]{:S(2)}) async-start(f32[256,1,256]{2,1,0:T(1,128)} %get-tuple-element.45), calls=%async_computation | async-start | bytes 524288 | tf_op jit(solution)/shard_map/sums/all_to_all | solution.py:427
  70.5 5.5 %collective-permute-start.9 = (f32[64,256]{1,0:T(8,128)S(1)}, f32[64,256]{1,0:T(8,128)S(1)}, u32[]{:S(2)}, u32[]{:S(2)}) collective-permute-start(f32[64,256]{1,0:T(8,128)S(1)} %get-tuple-element.44.refs_0_), channel_id=1, source_target_pairs={{0,1},{1,0},{2,3},{3,2},{4,5},{5,4},{6,7},{7,6},{8,9},{9,8},{10,11... | collective-permute-start | bytes 196616 | tf_op jit(solution)/shard_map/sums/ppermute | solution.py:429
  72.7 5.7 %collective-permute-start.10 = (f32[64,256]{1,0:T(8,128)S(1)}, f32[64,256]{1,0:T(8,128)S(1)}, u32[]{:S(2)}, u32[]{:S(2)}) collective-permute-start(f32[64,256]{1,0:T(8,128)S(1)} %get-tuple-element.44.refs_0_), channel_id=1, source_target_pairs={{0,2},{1,3},{2,0},{3,1},{4,6},{5,7},{6,4},{7,5},{8,10},{9,11},{10,... | collective-permute-start | bytes 196616 | tf_op jit(solution)/shard_map/sums/ppermute | solution.py:429
  73.8 7.3 %collective-permute-start.11 = (f32[64,256]{1,0:T(8,128)S(1)}, f32[64,256]{1,0:T(8,128)S(1)}, u32[]{:S(2)}, u32[]{:S(2)}) collective-permute-start(f32[64,256]{1,0:T(8,128)S(1)} %get-tuple-element.44.refs_0_), channel_id=1, source_target_pairs={{0,3},{1,2},{2,1},{3,0},{4,7},{5,6},{6,5},{7,4},{8,11},{9,10},{10,... | collective-permute-start | bytes 196616 | tf_op jit(solution)/shard_map/sums/ppermute | solution.py:429

commit v6 on v5

--- a/solution.py
+++ b/solution.py
@@ -327,9 +327,12 @@
     part = part_ref[...]
     slab_ref[...] = part + (from_below_ref[...] + from_above_ref[...])
     total = part + (below_ref[...] + above_ref[...])
+    depth = wide_ref.shape[2]
     for s in range(count):
+        pieces = [total[s : s + 1, i * depth : (i + 1) * depth] for i in range(wide_ref.shape[1])]
+        sent = jnp.concatenate(pieces, axis=0).astype(wide_ref.dtype)
         for r in range(copies):
-            wide_ref[s * copies + r] = total[s : s + 1]
+            wide_ref[s * copies + r] = sent
 
 
 def combine(part, returns, copies):
@@ -338,7 +341,7 @@
         combine_kernel,
         out_shape=[
             jax.ShapeDtypeStruct((count, columns), jnp.float32),
-            jax.ShapeDtypeStruct((count * copies, 1, columns), jnp.float32),
+            jax.ShapeDtypeStruct((count * copies, columns // 128, 128), jnp.bfloat16),
         ],
         in_specs=[vmem_spec()] * (1 + len(returns)),
         out_specs=[vmem_spec()] * 2,
@@ -369,10 +372,11 @@
     while len(terms) > 1:
         terms = [terms[i] + terms[i + 1] for i in range(0, len(terms), 2)]
     slab = terms[0] * slab_scale
-    gram = jnp.sum(rows_ref[...], axis=0) * gram_scale
+    gram = jnp.sum(rows_ref[...].astype(jnp.float32), axis=0) * gram_scale
+    across = gram.shape[1] // count
     for j in range(slab.shape[1] // count):
         slab_ref[0, j] = slab[:, j * count : (j + 1) * count]
-        gram_ref[j] = gram[:, j * count : (j + 1) * count]
+        gram_ref[j] = gram[j // across : j // across + 1, j % across * count : (j % across + 1) * count]
 
 
 def finish(parts, rows, slab_scale, gram_scale):

time: 87.4 us -> 84.8 us (0.970)
  waiting for transfers between devices: 34.3 us -> 31.6 us
    all_to_all x1, waiting for transfers between devices: 5.02 us -> 3.06 us  [body(): sent = lax.all_to_all(wide, ('space', 'snap'), 0, 0, tiled=True)]
where the time goes in v6:
time: 84.8 us; the launch traced here: 84.4 us
  starting transfers between devices  33.2 us (39%)
  waiting for transfers between devices  31.6 us (37%)
  Pallas kernels  15.7 us (19%)
  local copies, waits for them, and re-layouts  3.09 us (4%)
    ppermute x3, waiting for transfers between devices, body(): lax.ppermute(mine[m], 'snap', [(i, i ^ m) for i in range(groups)])  23.4 us
    all_to_all x1, starting transfers between devices, body(): sent = lax.all_to_all(wide, ('space', 'snap'), 0, 0, tiled=True)  15.8 us
    ppermute x3, starting transfers between devices, body(): lax.ppermute(mine[m], 'snap', [(i, i ^ m) for i in range(groups)])  6.56 us
    pallas_call x1, Pallas kernels, local_tiles(): pl.pallas_call(functools.partial(local_kernel, groups, density.shape[0]),...  5.96 us
    ppermute x3, starting transfers between devices, body(): lax.ppermute(part, 'snap', [(i, i ^ m) for i in range(groups)])  5.47 us
    ppermute x3, waiting for transfers between devices, body(): lax.ppermute(part, 'snap', [(i, i ^ m) for i in range(groups)])  4.49 us
    pallas_call x1, Pallas kernels, edge_tiles(): pl.pallas_call(functools.partial(edge_kernel, groups, materials, len(lows...  3.17 us
    ppermute x1, starting transfers between devices, body(): from_below = lax.ppermute(below, 'space', even)  3.11 us
  transfers between devices with their start and end apart: 13, of which 6 were waited for; matrix products, arithmetic and copies ran while one was open for 0% of the time, Pallas kernels for 12%

profile of v6, /device:TPU:1, one launch (start us, length us, event | category | flops | bytes accessed | tf_op | source)
XLA Modules:
  0.0 84.4 jit_solution(6893260742901378916)
XLA Ops:
  0.6 0.0 copy-start.4
  0.6 0.0 copy-start
  0.7 1.4 %copy-done = bf16[16,3,2,64,128]{4,3,2,1,0:T(8,128)(2,1)S(1)} copy-done((bf16[16,3,2,64,128]{4,3,2,1,0:T(8,128)(2,1)S(1)}, bf16[16,3,2,64,128]{4,3,2,1,0:T(8,128)(2,1)}, u32[]{:S(2)}) %copy-start) | copy-done | bytes 1572888
  2.1 0.0 copy-start.1
  2.1 0.8 copy-done.1
  2.9 0.0 copy-start.3
  2.9 1.3 %spread.1 = (bf16[3,2,18,16,128]{4,3,2,1,0:T(8,128)(2,1)S(1)}, bf16[3,2,18,16,128]{4,3,2,1,0:T(8,128)(2,1)S(1)}, bf16[3,2,18,16,128]{4,3,2,1,0:T(8,128)(2,1)S(1)}, bf16[3,2,18,16,128]{4,3,2,1,0:T(8,128)(2,1)S(1)}) custom-call(s32[1]{0:T(128)} %bitcast.me_ref, bf16[16,3,2,64,128]{4,3,2,1,0:T(8,128)(2,1)S(1)} %copy-done, s32[2,64,128]{2,1,0:T(8,128)S(1)} %copy-done.1), custom_call_target="tpu_custom_call" | custom-call | bytes 5242880 | tf_op jit(solution)/shard_map/spread/pallas_call | solution.py:31
  4.2 3.3 %collective-permute-start = (bf16[3,2,18,16,128]{4,3,2,1,0:T(8,128)(2,1)S(1)}, bf16[3,2,18,16,128]{4,3,2,1,0:T(8,128)(2,1)S(1)}, u32[]{:S(2)}, u32[]{:S(2)}) collective-permute-start(bf16[3,2,18,16,128]{4,3,2,1,0:T(8,128)(2,1)S(1)} %get-tuple-element.26), channel_id=1, source_target_pairs={{0,1},{1,0},{2,3},{3,2},{4,5},{5,4},{6,7},{7,6},{8,9},{9,8},{10,11... | collective-permute-start | bytes 1327112 | tf_op jit(solution)/shard_map/regroup/ppermute | solution.py:405
  7.5 1.2 %collective-permute-start.1 = (bf16[3,2,18,16,128]{4,3,2,1,0:T(8,128)(2,1)S(1)}, bf16[3,2,18,16,128]{4,3,2,1,0:T(8,128)(2,1)S(1)}, u32[]{:S(2)}, u32[]{:S(2)}) collective-permute-start(bf16[3,2,18,16,128]{4,3,2,1,0:T(8,128)(2,1)S(1)} %get-tuple-element.27), channel_id=1, source_target_pairs={{0,2},{1,3},{2,0},{3,1},{4,6},{5,7},{6,4},{7,5},{8,10},{9,11},{10,... | collective-permute-start | bytes 1327112 | tf_op jit(solution)/shard_map/regroup/ppermute | solution.py:405
  8.7 2.0 %collective-permute-start.2 = (bf16[3,2,18,16,128]{4,3,2,1,0:T(8,128)(2,1)S(1)}, bf16[3,2,18,16,128]{4,3,2,1,0:T(8,128)(2,1)S(1)}, u32[]{:S(2)}, u32[]{:S(2)}) collective-permute-start(bf16[3,2,18,16,128]{4,3,2,1,0:T(8,128)(2,1)S(1)} %get-tuple-element.28), channel_id=1, source_target_pairs={{0,3},{1,2},{2,1},{3,0},{4,7},{5,6},{6,5},{7,4},{8,11},{9,10},{10,... | collective-permute-start | bytes 1327112 | tf_op jit(solution)/shard_map/regroup/ppermute | solution.py:405
  10.7 0.1 pad_add_fusion.me_ref
  10.8 0.0 collective-permute-done.refs_1_
  10.8 0.0 copy-start.2
  10.8 0.8 copy-done.2
  11.7 0.7 halo.2
  12.4 0.1 collective-permute-start.3
  12.5 0.7 collective-permute-start.5
  13.1 7.6 %collective-permute-done.1.refs_2_.refs_0_ = bf16[3,2,18,16,128]{4,3,2,1,0:T(8,128)(2,1)S(1)} collective-permute-done((bf16[3,2,18,16,128]{4,3,2,1,0:T(8,128)(2,1)S(1)}, bf16[3,2,18,16,128]{4,3,2,1,0:T(8,128)(2,1)S(1)}, u32[]{:S(2)}, u32[]{:S(2)}) %collective-permute-start.1) | collective-permute-done | bytes 442400 | tf_op jit(solution)/shard_map/regroup/ppermute | solution.py:405
  20.7 15.8 %collective-permute-done.2.refs_3_.refs_1_ = bf16[3,2,18,16,128]{4,3,2,1,0:T(8,128)(2,1)S(1)} collective-permute-done((bf16[3,2,18,16,128]{4,3,2,1,0:T(8,128)(2,1)S(1)}, bf16[3,2,18,16,128]{4,3,2,1,0:T(8,128)(2,1)S(1)}, u32[]{:S(2)}, u32[]{:S(2)}) %collective-permute-start.2) | collective-permute-done | bytes 442400 | tf_op jit(solution)/shard_map/regroup/ppermute | solution.py:405
  36.6 0.6 halo.3
  37.1 0.1 collective-permute-start.4
  37.2 0.7 collective-permute-start.6
  37.9 0.0 copy-done.4
  37.9 0.0 copy-done.3
  37.9 6.0 %local_tiles.1 = (f32[64,256]{1,0:T(8,128)S(1)}, f32[3,2,512,256]{3,2,1,0:T(8,128)S(1)}, f32[3,2,512,256]{3,2,1,0:T(8,128)S(1)}, bf16[2,64,3072]{2,1,0:T(8,128)(2,1)S(1)}) custom-call(s32[2]{0:T(128)S(1)} %pad_add_fusion.me_ref, f32[3]{0:T(128)S(1)} %copy-done.4, bf16[3,2,18,16,128]{4,3,2,1,0:T(8,128)(2,1)S(1)} %get-tuple-element.25.refs_0_, ...), custom_call_target="tpu_custom_call" | custom-call | flops 5000000000 | bytes 12582912 | tf_op jit(solution)/shard_map/local_tiles/pallas_call | solution.py:204
  43.9 0.7 collective-permute-done.4.refs_1_
  44.6 0.0 collective-permute-done.6.refs_3_
  44.6 0.0 collective-permute-done.3.refs_0_
  44.6 0.0 collective-permute-done.5.refs_2_
  44.6 2.3 %return_tiles.1 = (f32[64,256]{1,0:T(8,128)S(1)}, f32[64,256]{1,0:T(8,128)S(1)}) custom-call(s32[2]{0:T(128)S(1)} %pad_add_fusion.me_ref, f32[3]{0:T(128)S(1)} %copy-done.4, f32[3,2,512,256]{3,2,1,0:T(8,128)S(1)} %get-tuple-element.41.cross_ref, bf16[7,10,16,128]{3,2,1,0:T(8,128)(2,1)S(1)} %collective-permute-done.3.refs_0_, ...), custom_call_target="tpu_custom_call" | custom-call | flops 3000000000 | bytes 6291456 | tf_op jit(solution)/shard_map/return_tiles/pallas_call | solution.py:272
  46.9 3.1 %collective-permute-start.7 = (f32[64,256]{1,0:T(8,128)S(1)}, f32[64,256]{1,0:T(8,128)S(1)}, u32[]{:S(2)}, u32[]{:S(2)}) collective-permute-start(f32[64,256]{1,0:T(8,128)S(1)} %get-tuple-element.42.below_ref), channel_id=1, source_target_pairs={{0,4},{4,0},{8,12},{12,8},{16,20},{20,16},{24,28},{28,24},{32,36},... | collective-permute-start | bytes 196616 | tf_op jit(solution)/shard_map/return_tiles/ppermute | solution.py:425
  50.0 0.7 collective-permute-start.8
  50.6 3.2 %edge_tiles.1.part_ref = f32[64,256]{1,0:T(8,128)S(1)} custom-call(s32[2]{0:T(128)S(1)} %pad_add_fusion.me_ref, f32[3]{0:T(128)S(1)} %copy-done.4, f32[64,256]{1,0:T(8,128)S(1)} %get-tuple-element.30.near_ref, f32[3,2,512,256]{3,2,1,0:T(8,128)S(1)} %get-tuple-element.31.edge_ref, bf16[2,64,3072]{2,1,0:T(8,128)(2,1)S(1)} %get-tuple-element.32.left_ref, ...), custom_call_target="tpu_custom_call" | custom-call | flops 5000000000 | bytes 20971520 | tf_op jit(solution)/shard_map/edge_tiles/pallas_call | solution.py:358
  53.8 0.0 collective-permute-done.7.from_below_ref
  53.8 0.0 collective-permute-done.8.from_above_ref
  53.8 0.7 sums.2
  54.6 15.8 %all-to-all-start = ((bf16[256,2,128]{2,1,0:T(2,128)(2,1)}), bf16[256,2,128]{2,1,0:T(2,128)(2,1)S(1)}, u32[]{:S(2)}, u32[]{:S(2)}) async-start(bf16[256,2,128]{2,1,0:T(2,128)(2,1)} %get-tuple-element.45), calls=%async_computation | async-start | bytes 262144 | tf_op jit(solution)/shard_map/sums/all_to_all | solution.py:431
  70.4 2.2 %collective-permute-start.9 = (f32[64,256]{1,0:T(8,128)S(1)}, f32[64,256]{1,0:T(8,128)S(1)}, u32[]{:S(2)}, u32[]{:S(2)}) collective-permute-start(f32[64,256]{1,0:T(8,128)S(1)} %get-tuple-element.44.refs_0_), channel_id=1, source_target_pairs={{0,1},{1,0},{2,3},{3,2},{4,5},{5,4},{6,7},{7,6},{8,9},{9,8},{10,11... | collective-permute-start | bytes 196616 | tf_op jit(solution)/shard_map/sums/ppermute | solution.py:433
  72.6 1.1 %collective-permute-start.10 = (f32[64,256]{1,0:T(8,128)S(1)}, f32[64,256]{1,0:T(8,128)S(1)}, u32[]{:S(2)}, u32[]{:S(2)}) collective-permute-start(f32[64,256]{1,0:T(8,128)S(1)} %get-tuple-element.44.refs_0_), channel_id=1, source_target_pairs={{0,2},{1,3},{2,0},{3,1},{4,6},{5,7},{6,4},{7,5},{8,10},{9,11},{10,... | collective-permute-start | bytes 196616 | tf_op jit(solution)/shard_map/sums/ppermute | solution.py:433
  73.8 2.1 %collective-permute-start.11 = (f32[64,256]{1,0:T(8,128)S(1)}, f32[64,256]{1,0:T(8,128)S(1)}, u32[]{:S(2)}, u32[]{:S(2)}) collective-permute-start(f32[64,256]{1,0:T(8,128)S(1)} %get-tuple-element.44.refs_0_), channel_id=1, source_target_pairs={{0,3},{1,2},{2,1},{3,0},{4,7},{5,6},{6,5},{7,4},{8,11},{9,10},{10,... | collective-permute-start | bytes 196616 | tf_op jit(solution)/shard_map/sums/ppermute | solution.py:433
  75.9 0.0 collective-permute-done.9.refs_1_
  75.9 2.2 %collective-permute-done.10.refs_2_ = f32[64,256]{1,0:T(8,128)S(1)} collective-permute-done((f32[64,256]{1,0:T(8,128)S(1)}, f32[64,256]{1,0:T(8,128)S(1)}, u32[]{:S(2)}, u32[]{:S(2)}) %collective-permute-start.10) | collective-permute-done | bytes 65568 | tf_op jit(solution)/shard_map/sums/ppermute | solution.py:433
  78.1 2.3 %collective-permute-done.11.refs_3_ = f32[64,256]{1,0:T(8,128)S(1)} collective-permute-done((f32[64,256]{1,0:T(8,128)S(1)}, f32[64,256]{1,0:T(8,128)S(1)}, u32[]{:S(2)}, u32[]{:S(2)}) %collective-permute-start.11) | collective-permute-done | bytes 65568 | tf_op jit(solution)/shard_map/sums/ppermute | solution.py:433
  80.4 3.1 %all-to-all-done.refs_4_ = bf16[256,2,128]{2,1,0:T(2,128)(2,1)S(1)} async-done(((bf16[256,2,128]{2,1,0:T(2,128)(2,1)}), bf16[256,2,128]{2,1,0:T(2,128)(2,1)S(1)}, u32[]{:S(2)}, u32[]{:S(2)}) %all-to-all-start) | async-done | bytes 131104 | tf_op jit(solution)/shard_map/sums/all_to_all | solution.py:431
  83.4 1.0 %sums.3 = (f32[1,4,64,64]{3,2,1,0:T(8,128)}, f32[4,1,64]{2,1,0:T(1,128)}) custom-call(f32[64,256]{1,0:T(8,128)S(1)} %get-tuple-element.44.refs_0_, f32[64,256]{1,0:T(8,128)S(1)} %collective-permute-done.9.refs_1_, f32[64,256]{1,0:T(8,128)S(1)} %collective-permute-done.10.refs_2_, f32[64,256]{1,0:T(8,128)S(1)} %collective-permute-done.11.refs_3_, ...), custom_call_target="tpu_custom_call" | custom-call | tf_op jit(solution)/shard_map/sums/pallas_call | solution.py:385
Async XLA Ops:
  0.6 37.3 %copy-start.4 = (f32[3]{0:T(128)S(1)}, f32[3]{0:T(128)}, u32[]{:S(2)}) copy-start(f32[3]{0:T(128)} %density_ref.5) | copy-start | bytes 40
  0.6 1.4 %copy-start = (bf16[16,3,2,64,128]{4,3,2,1,0:T(8,128)(2,1)S(1)}, bf16[16,3,2,64,128]{4,3,2,1,0:T(8,128)(2,1)}, u32[]{:S(2)}) copy-start(bf16[16,3,2,64,128]{4,3,2,1,0:T(8,128)(2,1)} %snaps_ref.1) | copy-start | bytes 4718596
  2.1 0.8 copy-start.1
  2.9 35.0 %copy-start.3 = (s32[2,64,128]{2,1,0:T(8,128)S(1)}, s32[2,64,128]{2,1,0:T(8,128)}, u32[]{:S(2)}) copy-start(s32[2,64,128]{2,1,0:T(8,128)} %refs_4_.3) | copy-start | bytes 196612
  4.2 6.6 %collective-permute-start = (bf16[3,2,18,16,128]{4,3,2,1,0:T(8,128)(2,1)S(1)}, bf16[3,2,18,16,128]{4,3,2,1,0:T(8,128)(2,1)S(1)}, u32[]{:S(2)}, u32[]{:S(2)}) collective-permute-start(bf16[3,2,18,16,128]{4,3,2,1,0:T(8,128)(2,1)S(1)} %get-tuple-element.26), channel_id=1, source_target_pairs={{0,1},{1,0},{2,3},{3,2},{4,5},{5,4},{6,7},{7,6},{8,9},{9,8},{10,11... | collective-permute-start | bytes 1327112 | tf_op jit(solution)/shard_map/regroup/ppermute | solution.py:405
  7.5 13.2 %collective-permute-start.1 = (bf16[3,2,18,16,128]{4,3,2,1,0:T(8,128)(2,1)S(1)}, bf16[3,2,18,16,128]{4,3,2,1,0:T(8,128)(2,1)S(1)}, u32[]{:S(2)}, u32[]{:S(2)}) collective-permute-start(bf16[3,2,18,16,128]{4,3,2,1,0:T(8,128)(2,1)S(1)} %get-tuple-element.27), channel_id=1, source_target_pairs={{0,2},{1,3},{2,0},{3,1},{4,6},{5,7},{6,4},{7,5},{8,10},{9,11},{10,... | collective-permute-start | bytes 1327112 | tf_op jit(solution)/shard_map/regroup/ppermute | solution.py:405
  8.7 27.8 %collective-permute-start.2 = (bf16[3,2,18,16,128]{4,3,2,1,0:T(8,128)(2,1)S(1)}, bf16[3,2,18,16,128]{4,3,2,1,0:T(8,128)(2,1)S(1)}, u32[]{:S(2)}, u32[]{:S(2)}) collective-permute-start(bf16[3,2,18,16,128]{4,3,2,1,0:T(8,128)(2,1)S(1)} %get-tuple-element.28), channel_id=1, source_target_pairs={{0,3},{1,2},{2,1},{3,0},{4,7},{5,6},{6,5},{7,4},{8,11},{9,10},{10,... | collective-permute-start | bytes 1327112 | tf_op jit(solution)/shard_map/regroup/ppermute | solution.py:405
  10.8 0.8 copy-start.2
  12.4 32.2 %collective-permute-start.3 = (bf16[7,10,16,128]{3,2,1,0:T(8,128)(2,1)S(1)}, bf16[7,10,16,128]{3,2,1,0:T(8,128)(2,1)S(1)}, u32[]{:S(2)}, u32[]{:S(2)}) collective-permute-start(bf16[7,10,16,128]{3,2,1,0:T(8,128)(2,1)S(1)} %get-tuple-element.35), channel_id=1, source_target_pairs={{0,4},{4,0},{8,12},{12,8},{16,20},{20,16},{24,28},{28,24},{32,36},... | collective-permute-start | bytes 860168 | tf_op jit(solution)/shard_map/halo/ppermute | solution.py:420
  12.5 32.1 %collective-permute-start.5 = (bf16[7,10,16,128]{3,2,1,0:T(8,128)(2,1)S(1)}, bf16[7,10,16,128]{3,2,1,0:T(8,128)(2,1)S(1)}, u32[]{:S(2)}, u32[]{:S(2)}) collective-permute-start(bf16[7,10,16,128]{3,2,1,0:T(8,128)(2,1)S(1)} %get-tuple-element.36), channel_id=1, source_target_pairs={{4,8},{8,4},{12,16},{16,12},{20,24},{24,20},{28,32},{32,28},{36,40... | collective-permute-start | bytes 860168 | tf_op jit(solution)/shard_map/halo/ppermute | solution.py:419
  37.1 7.4 %collective-permute-start.4 = (bf16[6,10,16,128]{3,2,1,0:T(8,128)(2,1)S(1)}, bf16[6,10,16,128]{3,2,1,0:T(8,128)(2,1)S(1)}, u32[]{:S(2)}, u32[]{:S(2)}) collective-permute-start(bf16[6,10,16,128]{3,2,1,0:T(8,128)(2,1)S(1)} %get-tuple-element.39), channel_id=1, source_target_pairs={{0,4},{4,0},{8,12},{12,8},{16,20},{20,16},{24,28},{28,24},{32,36},... | collective-permute-start | bytes 737288 | tf_op jit(solution)/shard_map/halo/ppermute | solution.py:420
  37.2 7.3 %collective-permute-start.6 = (bf16[6,10,16,128]{3,2,1,0:T(8,128)(2,1)S(1)}, bf16[6,10,16,128]{3,2,1,0:T(8,128)(2,1)S(1)}, u32[]{:S(2)}, u32[]{:S(2)}) collective-permute-start(bf16[6,10,16,128]{3,2,1,0:T(8,128)(2,1)S(1)} %get-tuple-element.40), channel_id=1, source_target_pairs={{4,8},{8,4},{12,16},{16,12},{20,24},{24,20},{28,32},{32,28},{36,40... | collective-permute-start | bytes 737288 | tf_op jit(solution)/shard_map/halo/ppermute | solution.py:419
  46.9 6.9 %collective-permute-start.7 = (f32[64,256]{1,0:T(8,128)S(1)}, f32[64,256]{1,0:T(8,128)S(1)}, u32[]{:S(2)}, u32[]{:S(2)}) collective-permute-start(f32[64,256]{1,0:T(8,128)S(1)} %get-tuple-element.42.below_ref), channel_id=1, source_target_pairs={{0,4},{4,0},{8,12},{12,8},{16,20},{20,16},{24,28},{28,24},{32,36},... | collective-permute-start | bytes 196616 | tf_op jit(solution)/shard_map/return_tiles/ppermute | solution.py:425
  50.0 3.9 %collective-permute-start.8 = (f32[64,256]{1,0:T(8,128)S(1)}, f32[64,256]{1,0:T(8,128)S(1)}, u32[]{:S(2)}, u32[]{:S(2)}) collective-permute-start(f32[64,256]{1,0:T(8,128)S(1)} %get-tuple-element.43.above_ref), channel_id=1, source_target_pairs={{4,8},{8,4},{12,16},{16,12},{20,24},{24,20},{28,32},{32,28},{36,40... | collective-permute-start | bytes 196616 | tf_op jit(solution)/shard_map/return_tiles/ppermute | solution.py:426
  54.6 28.9 %all-to-all-start = ((bf16[256,2,128]{2,1,0:T(2,128)(2,1)}), bf16[256,2,128]{2,1,0:T(2,128)(2,1)S(1)}, u32[]{:S(2)}, u32[]{:S(2)}) async-start(bf16[256,2,128]{2,1,0:T(2,128)(2,1)} %get-tuple-element.45), calls=%async_computation | async-start | bytes 262144 | tf_op jit(solution)/shard_map/sums/all_to_all | solution.py:431
  70.4 5.5 %collective-permute-start.9 = (f32[64,256]{1,0:T(8,128)S(1)}, f32[64,256]{1,0:T(8,128)S(1)}, u32[]{:S(2)}, u32[]{:S(2)}) collective-permute-start(f32[64,256]{1,0:T(8,128)S(1)} %get-tuple-element.44.refs_0_), channel_id=1, source_target_pairs={{0,1},{1,0},{2,3},{3,2},{4,5},{5,4},{6,7},{7,6},{8,9},{9,8},{10,11... | collective-permute-start | bytes 196616 | tf_op jit(solution)/shard_map/sums/ppermute | solution.py:433
  72.6 5.4 %collective-permute-start.10 = (f32[64,256]{1,0:T(8,128)S(1)}, f32[64,256]{1,0:T(8,128)S(1)}, u32[]{:S(2)}, u32[]{:S(2)}) collective-permute-start(f32[64,256]{1,0:T(8,128)S(1)} %get-tuple-element.44.refs_0_), channel_id=1, source_target_pairs={{0,2},{1,3},{2,0},{3,1},{4,6},{5,7},{6,4},{7,5},{8,10},{9,11},{10,... | collective-permute-start | bytes 196616 | tf_op jit(solution)/shard_map/sums/ppermute | solution.py:433
  73.8 6.6 %collective-permute-start.11 = (f32[64,256]{1,0:T(8,128)S(1)}, f32[64,256]{1,0:T(8,128)S(1)}, u32[]{:S(2)}, u32[]{:S(2)}) collective-permute-start(f32[64,256]{1,0:T(8,128)S(1)} %get-tuple-element.44.refs_0_), channel_id=1, source_target_pairs={{0,3},{1,2},{2,1},{3,0},{4,7},{5,6},{6,5},{7,4},{8,11},{9,10},{10,... | collective-permute-start | bytes 196616 | tf_op jit(solution)/shard_map/sums/ppermute | solution.py:433

commit v7 on v6

--- a/solution.py
+++ b/solution.py
@@ -229,59 +229,55 @@
     return side[part].at[m * comps + c]
 
 
-def returns_kernel(groups, materials, pairs, me_ref, density_ref, cross_ref, *refs):
-    sides = (refs[:pairs], refs[pairs : 2 * pairs])
-    below_ref, above_ref = refs[2 * pairs : 2 * pairs + 2]
-    scratch = refs[2 * pairs + 2 :]
+def returns_kernel(groups, materials, pairs, side, me_ref, density_ref, cross_ref, *refs):
+    parts = refs[:pairs]
+    back_ref, scratch = refs[pairs], refs[pairs + 1 :]
     me = me_ref[0]
     comps = cross_ref.shape[0]
-    reach, members, depth = sides[0][0].shape[1:]
+    reach, members, depth = parts[0].shape[1:]
     half = reach - 2
     count = groups * members
 
-    sums = [0.0, 0.0]
+    total = 0.0
+    g = me_ref[1] if side else 1 - me_ref[1]
     for c in range(comps):
-        for side in range(2):
-            left, right = scratch[2 * (2 * c + side) : 2 * (2 * c + side) + 2]
-            g = me_ref[1] if side else 1 - me_ref[1]
-            cross = cross_ref[c, g]
-            for y in range(half):
-                label = sides[side][0][sides[side][0].shape[0] - 1, y].astype(jnp.float32)
-                density, shown = at_cells(label, density_ref, materials, members)
-                lanes = slice(y * depth, (y + 1) * depth)
-                for m in range(groups):
-                    start = pl.multiple_of((me ^ m) * members, members)
-                    left[pl.ds(start, members), lanes] = received_at(sides[side], m, comps, c)[y + 1]
-                    at = (m * half + y) * members
-                    put_images(cross[at : at + members], shown, density, right, start, lanes, count)
-
-            sums[side] = sums[side] + correlate(left[...], right[...])
-    below_ref[...] = sums[0]
-    above_ref[...] = sums[1]
-
-
-def return_tiles(cross, lows, highs, density, me, groups):
+        left, right = scratch[2 * c : 2 * c + 2]
+        cross = cross_ref[c, g]
+        for y in range(half):
+            label = parts[0][parts[0].shape[0] - 1, y].astype(jnp.float32)
+            density, shown = at_cells(label, density_ref, materials, members)
+            lanes = slice(y * depth, (y + 1) * depth)
+            for m in range(groups):
+                start = pl.multiple_of((me ^ m) * members, members)
+                left[pl.ds(start, members), lanes] = received_at(parts, m, comps, c)[y + 1]
+                at = (m * half + y) * members
+                put_images(cross[at : at + members], shown, density, right, start, lanes, count)
+
+        total = total + correlate(left[...], right[...])
+    back_ref[...] = total
+
+
+def return_tiles(cross, parts, side, density, me, groups):
     materials = density.shape[0]
     comps = cross.shape[0]
-    reach, members, depth = lows[0].shape[1:]
+    reach, members, depth = parts[0].shape[1:]
     count = groups * members
     cells = comps * (reach - 2) * depth
     columns = (materials + 1) * count
     part = jax.ShapeDtypeStruct((count, columns), jnp.float32)
-    halos = [*lows, *highs]
-    return pl.pallas_call(
-        functools.partial(returns_kernel, groups, materials, len(lows)),
-        out_shape=[part, part],
-        in_specs=[smem_spec(), smem_spec()] + [vmem_spec()] * (1 + len(halos)),
-        out_specs=[vmem_spec()] * 2,
+    return pl.pallas_call(
+        functools.partial(returns_kernel, groups, materials, len(parts), side),
+        out_shape=part,
+        in_specs=[smem_spec(), smem_spec()] + [vmem_spec()] * (1 + len(parts)),
+        out_specs=vmem_spec(),
         scratch_shapes=[
             pltpu.VMEM((count, cells // comps), jnp.bfloat16),
             pltpu.VMEM((columns, cells // comps), jnp.bfloat16),
         ]
-        * (2 * comps),
+        * comps,
         compiler_params=pltpu.CompilerParams(vmem_limit_bytes=40 * 2**20),
         cost_estimate=pl.CostEstimate(flops=3 * 10**9, bytes_accessed=6 * 2**20, transcendentals=0),
-    )(me, density, cross, *halos)
+    )(me, density, cross, *parts)
 
 
 def edge_kernel(groups, materials, pairs, me_ref, density_ref, near_ref, edge_ref, left_ref, *refs):
@@ -421,9 +417,10 @@
     with jax.named_scope("local_tiles"):
         near, edge, cross, left = local_tiles(blocks, labels, density, weights, me)
     with jax.named_scope("return_tiles"):
-        below, above = return_tiles(cross, firsts, seconds, density, me, groups)
+        above = return_tiles(cross, seconds, 1, density, me, groups)
+        from_above = lax.ppermute(above, "space", odd)
+        below = return_tiles(cross, firsts, 0, density, me, groups)
         from_below = lax.ppermute(below, "space", even)
-        from_above = lax.ppermute(above, "space", odd)
     with jax.named_scope("edge_tiles"):
         part = edge_tiles(near, edge, left, firsts, seconds, labels, density, weights, me, groups)
     with jax.named_scope("sums"):

time: 84.8 us -> 84.9 us (level)
    ppermute x1, starting transfers between devices: 3.11 us -> 2.13 us  [body(): from_below = lax.ppermute(below, 'space', even)]
    pallas_call x1 -> x2, Pallas kernels: 2.26 us -> 3.01 us  [return_tiles(): pl.pallas_call(functools.partial(returns_kernel, groups, materials, len(p...]
  transfers between devices with their start and end apart: 13 -> 13, of which waited for: 6 -> 6; matrix products, arithmetic and copies ran while one was open for 0% -> 0% of each run, Pallas kernels for 12% -> 16%
where the time goes in v7:
time: 84.9 us; the launch traced here: 84.6 us
  starting transfers between devices  32.5 us (38%)
  waiting for transfers between devices  31.6 us (37%)
  Pallas kernels  16.4 us (19%)
  local copies, waits for them, and re-layouts  3.09 us (4%)
    ppermute x3, waiting for transfers between devices, body(): lax.ppermute(mine[m], 'snap', [(i, i ^ m) for i in range(groups)])  23.4 us
    all_to_all x1, starting transfers between devices, body(): sent = lax.all_to_all(wide, ('space', 'snap'), 0, 0, tiled=True)  16.2 us
    ppermute x3, starting transfers between devices, body(): lax.ppermute(mine[m], 'snap', [(i, i ^ m) for i in range(groups)])  6.56 us
    pallas_call x1, Pallas kernels, local_tiles(): pl.pallas_call(functools.partial(local_kernel, groups, density.shape[0]),...  5.96 us
    ppermute x3, starting transfers between devices, body(): lax.ppermute(part, 'snap', [(i, i ^ m) for i in range(groups)])  5.47 us
    ppermute x3, waiting for transfers between devices, body(): lax.ppermute(part, 'snap', [(i, i ^ m) for i in range(groups)])  4.49 us
    pallas_call x1, Pallas kernels, edge_tiles(): pl.pallas_call(functools.partial(edge_kernel, groups, materials, len(lows...  3.17 us
    unnamed x10, local copies, waits for them, and re-layouts  3.09 us
  transfers between devices with their start and end apart: 13, of which 6 were waited for; matrix products, arithmetic and copies ran while one was open for 0% of the time, Pallas kernels for 16%

profile of v7, /device:TPU:1, one launch (start us, length us, event | category | flops | bytes accessed | tf_op | source)
XLA Modules:
  0.0 84.6 jit_solution(9680141585909490712)
XLA Ops:
  0.6 0.0 copy-start.4
  0.6 0.0 copy-start
  0.7 1.4 %copy-done = bf16[16,3,2,64,128]{4,3,2,1,0:T(8,128)(2,1)S(1)} copy-done((bf16[16,3,2,64,128]{4,3,2,1,0:T(8,128)(2,1)S(1)}, bf16[16,3,2,64,128]{4,3,2,1,0:T(8,128)(2,1)}, u32[]{:S(2)}) %copy-start) | copy-done | bytes 1572888
  2.1 0.0 copy-start.1
  2.1 0.8 copy-done.1
  2.9 0.0 copy-start.3
  2.9 1.3 %spread.1 = (bf16[3,2,18,16,128]{4,3,2,1,0:T(8,128)(2,1)S(1)}, bf16[3,2,18,16,128]{4,3,2,1,0:T(8,128)(2,1)S(1)}, bf16[3,2,18,16,128]{4,3,2,1,0:T(8,128)(2,1)S(1)}, bf16[3,2,18,16,128]{4,3,2,1,0:T(8,128)(2,1)S(1)}) custom-call(s32[1]{0:T(128)} %bitcast.me_ref, bf16[16,3,2,64,128]{4,3,2,1,0:T(8,128)(2,1)S(1)} %copy-done, s32[2,64,128]{2,1,0:T(8,128)S(1)} %copy-done.1), custom_call_target="tpu_custom_call" | custom-call | bytes 5242880 | tf_op jit(solution)/shard_map/spread/pallas_call | solution.py:31
  4.2 3.3 %collective-permute-start = (bf16[3,2,18,16,128]{4,3,2,1,0:T(8,128)(2,1)S(1)}, bf16[3,2,18,16,128]{4,3,2,1,0:T(8,128)(2,1)S(1)}, u32[]{:S(2)}, u32[]{:S(2)}) collective-permute-start(bf16[3,2,18,16,128]{4,3,2,1,0:T(8,128)(2,1)S(1)} %get-tuple-element.24), channel_id=1, source_target_pairs={{0,1},{1,0},{2,3},{3,2},{4,5},{5,4},{6,7},{7,6},{8,9},{9,8},{10,11... | collective-permute-start | bytes 1327112 | tf_op jit(solution)/shard_map/regroup/ppermute | solution.py:401
  7.5 1.2 %collective-permute-start.1 = (bf16[3,2,18,16,128]{4,3,2,1,0:T(8,128)(2,1)S(1)}, bf16[3,2,18,16,128]{4,3,2,1,0:T(8,128)(2,1)S(1)}, u32[]{:S(2)}, u32[]{:S(2)}) collective-permute-start(bf16[3,2,18,16,128]{4,3,2,1,0:T(8,128)(2,1)S(1)} %get-tuple-element.25), channel_id=1, source_target_pairs={{0,2},{1,3},{2,0},{3,1},{4,6},{5,7},{6,4},{7,5},{8,10},{9,11},{10,... | collective-permute-start | bytes 1327112 | tf_op jit(solution)/shard_map/regroup/ppermute | solution.py:401
  8.7 2.0 %collective-permute-start.2 = (bf16[3,2,18,16,128]{4,3,2,1,0:T(8,128)(2,1)S(1)}, bf16[3,2,18,16,128]{4,3,2,1,0:T(8,128)(2,1)S(1)}, u32[]{:S(2)}, u32[]{:S(2)}) collective-permute-start(bf16[3,2,18,16,128]{4,3,2,1,0:T(8,128)(2,1)S(1)} %get-tuple-element.26), channel_id=1, source_target_pairs={{0,3},{1,2},{2,1},{3,0},{4,7},{5,6},{6,5},{7,4},{8,11},{9,10},{10,... | collective-permute-start | bytes 1327112 | tf_op jit(solution)/shard_map/regroup/ppermute | solution.py:401
  10.7 0.1 pad_add_fusion.me_ref
  10.8 0.0 collective-permute-done.refs_1_
  10.8 0.0 copy-start.2
  10.8 0.8 copy-done.2
  11.7 0.7 halo.2
  12.4 0.1 collective-permute-start.3
  12.5 0.7 collective-permute-start.5
  13.1 7.6 %collective-permute-done.1.refs_2_.refs_0_ = bf16[3,2,18,16,128]{4,3,2,1,0:T(8,128)(2,1)S(1)} collective-permute-done((bf16[3,2,18,16,128]{4,3,2,1,0:T(8,128)(2,1)S(1)}, bf16[3,2,18,16,128]{4,3,2,1,0:T(8,128)(2,1)S(1)}, u32[]{:S(2)}, u32[]{:S(2)}) %collective-permute-start.1) | collective-permute-done | bytes 442400 | tf_op jit(solution)/shard_map/regroup/ppermute | solution.py:401
  20.7 15.8 %collective-permute-done.2.refs_3_.refs_1_ = bf16[3,2,18,16,128]{4,3,2,1,0:T(8,128)(2,1)S(1)} collective-permute-done((bf16[3,2,18,16,128]{4,3,2,1,0:T(8,128)(2,1)S(1)}, bf16[3,2,18,16,128]{4,3,2,1,0:T(8,128)(2,1)S(1)}, u32[]{:S(2)}, u32[]{:S(2)}) %collective-permute-start.2) | collective-permute-done | bytes 442400 | tf_op jit(solution)/shard_map/regroup/ppermute | solution.py:401
  36.6 0.6 halo.3
  37.1 0.1 collective-permute-start.4
  37.2 0.7 collective-permute-start.6
  37.9 0.0 copy-done.4
  37.9 0.0 copy-done.3
  37.9 6.0 %local_tiles.1 = (f32[64,256]{1,0:T(8,128)S(1)}, f32[3,2,512,256]{3,2,1,0:T(8,128)S(1)}, f32[3,2,512,256]{3,2,1,0:T(8,128)S(1)}, bf16[2,64,3072]{2,1,0:T(8,128)(2,1)S(1)}) custom-call(s32[2]{0:T(128)S(1)} %pad_add_fusion.me_ref, f32[3]{0:T(128)S(1)} %copy-done.4, bf16[3,2,18,16,128]{4,3,2,1,0:T(8,128)(2,1)S(1)} %get-tuple-element.23.refs_0_, ...), custom_call_target="tpu_custom_call" | custom-call | flops 5000000000 | bytes 12582912 | tf_op jit(solution)/shard_map/local_tiles/pallas_call | solution.py:204
  43.9 0.7 collective-permute-done.4.refs_1_
  44.6 0.0 collective-permute-done.3.refs_0_
  44.6 1.5 %return_tiles.2.below_ref = f32[64,256]{1,0:T(8,128)S(1)} custom-call(s32[2]{0:T(128)S(1)} %pad_add_fusion.me_ref, f32[3]{0:T(128)S(1)} %copy-done.4, f32[3,2,512,256]{3,2,1,0:T(8,128)S(1)} %get-tuple-element.39.cross_ref, bf16[7,10,16,128]{3,2,1,0:T(8,128)(2,1)S(1)} %collective-permute-done.3.refs_0_, ...), custom_call_target="tpu_custom_call" | custom-call | flops 3000000000 | bytes 6291456 | tf_op jit(solution)/shard_map/return_tiles/pallas_call | solution.py:268
  46.1 2.1 %collective-permute-start.7 = (f32[64,256]{1,0:T(8,128)S(1)}, f32[64,256]{1,0:T(8,128)S(1)}, u32[]{:S(2)}, u32[]{:S(2)}) collective-permute-start(f32[64,256]{1,0:T(8,128)S(1)} %return_tiles.2.below_ref), channel_id=1, source_target_pairs={{0,4},{4,0},{8,12},{12,8},{16,20},{20,16},{24,28},{28,24},{32,36},... | collective-permute-start | bytes 196616 | tf_op jit(solution)/shard_map/return_tiles/ppermute | solution.py:423
  48.2 0.0 collective-permute-done.6.refs_3_.refs_1_
  48.2 0.0 collective-permute-done.5.refs_2_.refs_0_
  48.2 1.5 %return_tiles.3.above_ref = f32[64,256]{1,0:T(8,128)S(1)} custom-call(s32[2]{0:T(128)S(1)} %pad_add_fusion.me_ref, f32[3]{0:T(128)S(1)} %copy-done.4, f32[3,2,512,256]{3,2,1,0:T(8,128)S(1)} %get-tuple-element.39.cross_ref, bf16[7,10,16,128]{3,2,1,0:T(8,128)(2,1)S(1)} %collective-permute-done.5.refs_2_.refs_0_, ...), custom_call_target="tpu_custom_call" | custom-call | flops 3000000000 | bytes 6291456 | tf_op jit(solution)/shard_map/return_tiles/pallas_call | solution.py:268
  49.7 0.7 collective-permute-start.8
  50.4 3.2 %edge_tiles.1.part_ref = f32[64,256]{1,0:T(8,128)S(1)} custom-call(s32[2]{0:T(128)S(1)} %pad_add_fusion.me_ref, f32[3]{0:T(128)S(1)} %copy-done.4, f32[64,256]{1,0:T(8,128)S(1)} %get-tuple-element.28.near_ref, f32[3,2,512,256]{3,2,1,0:T(8,128)S(1)} %get-tuple-element.29.edge_ref, bf16[2,64,3072]{2,1,0:T(8,128)(2,1)S(1)} %get-tuple-element.30.left_ref, ...), custom_call_target="tpu_custom_call" | custom-call | flops 5000000000 | bytes 20971520 | tf_op jit(solution)/shard_map/edge_tiles/pallas_call | solution.py:354
  53.6 0.0 collective-permute-done.7.from_below_ref
  53.6 0.0 collective-permute-done.8.from_above_ref
  53.6 0.7 sums.2
  54.3 16.2 %all-to-all-start = ((bf16[256,2,128]{2,1,0:T(2,128)(2,1)}), bf16[256,2,128]{2,1,0:T(2,128)(2,1)S(1)}, u32[]{:S(2)}, u32[]{:S(2)}) async-start(bf16[256,2,128]{2,1,0:T(2,128)(2,1)} %get-tuple-element.41), calls=%async_computation | async-start | bytes 262144 | tf_op jit(solution)/shard_map/sums/all_to_all | solution.py:428
  70.5 2.2 %collective-permute-start.9 = (f32[64,256]{1,0:T(8,128)S(1)}, f32[64,256]{1,0:T(8,128)S(1)}, u32[]{:S(2)}, u32[]{:S(2)}) collective-permute-start(f32[64,256]{1,0:T(8,128)S(1)} %get-tuple-element.40.refs_0_), channel_id=1, source_target_pairs={{0,1},{1,0},{2,3},{3,2},{4,5},{5,4},{6,7},{7,6},{8,9},{9,8},{10,11... | collective-permute-start | bytes 196616 | tf_op jit(solution)/shard_map/sums/ppermute | solution.py:430
  72.8 1.1 %collective-permute-start.10 = (f32[64,256]{1,0:T(8,128)S(1)}, f32[64,256]{1,0:T(8,128)S(1)}, u32[]{:S(2)}, u32[]{:S(2)}) collective-permute-start(f32[64,256]{1,0:T(8,128)S(1)} %get-tuple-element.40.refs_0_), channel_id=1, source_target_pairs={{0,2},{1,3},{2,0},{3,1},{4,6},{5,7},{6,4},{7,5},{8,10},{9,11},{10,... | collective-permute-start | bytes 196616 | tf_op jit(solution)/shard_map/sums/ppermute | solution.py:430
  73.9 2.1 %collective-permute-start.11 = (f32[64,256]{1,0:T(8,128)S(1)}, f32[64,256]{1,0:T(8,128)S(1)}, u32[]{:S(2)}, u32[]{:S(2)}) collective-permute-start(f32[64,256]{1,0:T(8,128)S(1)} %get-tuple-element.40.refs_0_), channel_id=1, source_target_pairs={{0,3},{1,2},{2,1},{3,0},{4,7},{5,6},{6,5},{7,4},{8,11},{9,10},{10,... | collective-permute-start | bytes 196616 | tf_op jit(solution)/shard_map/sums/ppermute | solution.py:430
  76.0 0.0 collective-permute-done.9.refs_1_
  76.0 2.2 %collective-permute-done.10.refs_2_ = f32[64,256]{1,0:T(8,128)S(1)} collective-permute-done((f32[64,256]{1,0:T(8,128)S(1)}, f32[64,256]{1,0:T(8,128)S(1)}, u32[]{:S(2)}, u32[]{:S(2)}) %collective-permute-start.10) | collective-permute-done | bytes 65568 | tf_op jit(solution)/shard_map/sums/ppermute | solution.py:430
  78.2 2.3 %collective-permute-done.11.refs_3_ = f32[64,256]{1,0:T(8,128)S(1)} collective-permute-done((f32[64,256]{1,0:T(8,128)S(1)}, f32[64,256]{1,0:T(8,128)S(1)}, u32[]{:S(2)}, u32[]{:S(2)}) %collective-permute-start.11) | collective-permute-done | bytes 65568 | tf_op jit(solution)/shard_map/sums/ppermute | solution.py:430
  80.5 3.1 %all-to-all-done.refs_4_ = bf16[256,2,128]{2,1,0:T(2,128)(2,1)S(1)} async-done(((bf16[256,2,128]{2,1,0:T(2,128)(2,1)}), bf16[256,2,128]{2,1,0:T(2,128)(2,1)S(1)}, u32[]{:S(2)}, u32[]{:S(2)}) %all-to-all-start) | async-done | bytes 131104 | tf_op jit(solution)/shard_map/sums/all_to_all | solution.py:428
  83.5 1.0 %sums.3 = (f32[1,4,64,64]{3,2,1,0:T(8,128)}, f32[4,1,64]{2,1,0:T(1,128)}) custom-call(f32[64,256]{1,0:T(8,128)S(1)} %get-tuple-element.40.refs_0_, f32[64,256]{1,0:T(8,128)S(1)} %collective-permute-done.9.refs_1_, f32[64,256]{1,0:T(8,128)S(1)} %collective-permute-done.10.refs_2_, f32[64,256]{1,0:T(8,128)S(1)} %collective-permute-done.11.refs_3_, ...), custom_call_target="tpu_custom_call" | custom-call | tf_op jit(solution)/shard_map/sums/pallas_call | solution.py:381
Async XLA Ops:
  0.6 37.3 %copy-start.4 = (f32[3]{0:T(128)S(1)}, f32[3]{0:T(128)}, u32[]{:S(2)}) copy-start(f32[3]{0:T(128)} %density_ref.7) | copy-start | bytes 40
  0.6 1.4 %copy-start = (bf16[16,3,2,64,128]{4,3,2,1,0:T(8,128)(2,1)S(1)}, bf16[16,3,2,64,128]{4,3,2,1,0:T(8,128)(2,1)}, u32[]{:S(2)}) copy-start(bf16[16,3,2,64,128]{4,3,2,1,0:T(8,128)(2,1)} %snaps_ref.1) | copy-start | bytes 4718596
  2.1 0.8 copy-start.1
  2.9 35.0 %copy-start.3 = (s32[2,64,128]{2,1,0:T(8,128)S(1)}, s32[2,64,128]{2,1,0:T(8,128)}, u32[]{:S(2)}) copy-start(s32[2,64,128]{2,1,0:T(8,128)} %refs_4_.3) | copy-start | bytes 196612
  4.2 6.6 %collective-permute-start = (bf16[3,2,18,16,128]{4,3,2,1,0:T(8,128)(2,1)S(1)}, bf16[3,2,18,16,128]{4,3,2,1,0:T(8,128)(2,1)S(1)}, u32[]{:S(2)}, u32[]{:S(2)}) collective-permute-start(bf16[3,2,18,16,128]{4,3,2,1,0:T(8,128)(2,1)S(1)} %get-tuple-element.24), channel_id=1, source_target_pairs={{0,1},{1,0},{2,3},{3,2},{4,5},{5,4},{6,7},{7,6},{8,9},{9,8},{10,11... | collective-permute-start | bytes 1327112 | tf_op jit(solution)/shard_map/regroup/ppermute | solution.py:401
  7.5 13.2 %collective-permute-start.1 = (bf16[3,2,18,16,128]{4,3,2,1,0:T(8,128)(2,1)S(1)}, bf16[3,2,18,16,128]{4,3,2,1,0:T(8,128)(2,1)S(1)}, u32[]{:S(2)}, u32[]{:S(2)}) collective-permute-start(bf16[3,2,18,16,128]{4,3,2,1,0:T(8,128)(2,1)S(1)} %get-tuple-element.25), channel_id=1, source_target_pairs={{0,2},{1,3},{2,0},{3,1},{4,6},{5,7},{6,4},{7,5},{8,10},{9,11},{10,... | collective-permute-start | bytes 1327112 | tf_op jit(solution)/shard_map/regroup/ppermute | solution.py:401
  8.7 27.8 %collective-permute-start.2 = (bf16[3,2,18,16,128]{4,3,2,1,0:T(8,128)(2,1)S(1)}, bf16[3,2,18,16,128]{4,3,2,1,0:T(8,128)(2,1)S(1)}, u32[]{:S(2)}, u32[]{:S(2)}) collective-permute-start(bf16[3,2,18,16,128]{4,3,2,1,0:T(8,128)(2,1)S(1)} %get-tuple-element.26), channel_id=1, source_target_pairs={{0,3},{1,2},{2,1},{3,0},{4,7},{5,6},{6,5},{7,4},{8,11},{9,10},{10,... | collective-permute-start | bytes 1327112 | tf_op jit(solution)/shard_map/regroup/ppermute | solution.py:401
  10.8 0.8 copy-start.2
  12.4 32.2 %collective-permute-start.3 = (bf16[7,10,16,128]{3,2,1,0:T(8,128)(2,1)S(1)}, bf16[7,10,16,128]{3,2,1,0:T(8,128)(2,1)S(1)}, u32[]{:S(2)}, u32[]{:S(2)}) collective-permute-start(bf16[7,10,16,128]{3,2,1,0:T(8,128)(2,1)S(1)} %get-tuple-element.33), channel_id=1, source_target_pairs={{0,4},{4,0},{8,12},{12,8},{16,20},{20,16},{24,28},{28,24},{32,36},... | collective-permute-start | bytes 860168 | tf_op jit(solution)/shard_map/halo/ppermute | solution.py:416
  12.5 35.8 %collective-permute-start.5 = (bf16[7,10,16,128]{3,2,1,0:T(8,128)(2,1)S(1)}, bf16[7,10,16,128]{3,2,1,0:T(8,128)(2,1)S(1)}, u32[]{:S(2)}, u32[]{:S(2)}) collective-permute-start(bf16[7,10,16,128]{3,2,1,0:T(8,128)(2,1)S(1)} %get-tuple-element.34), channel_id=1, source_target_pairs={{4,8},{8,4},{12,16},{16,12},{20,24},{24,20},{28,32},{32,28},{36,40... | collective-permute-start | bytes 860168 | tf_op jit(solution)/shard_map/halo/ppermute | solution.py:415
  37.1 7.4 %collective-permute-start.4 = (bf16[6,10,16,128]{3,2,1,0:T(8,128)(2,1)S(1)}, bf16[6,10,16,128]{3,2,1,0:T(8,128)(2,1)S(1)}, u32[]{:S(2)}, u32[]{:S(2)}) collective-permute-start(bf16[6,10,16,128]{3,2,1,0:T(8,128)(2,1)S(1)} %get-tuple-element.37), channel_id=1, source_target_pairs={{0,4},{4,0},{8,12},{12,8},{16,20},{20,16},{24,28},{28,24},{32,36},... | collective-permute-start | bytes 737288 | tf_op jit(solution)/shard_map/halo/ppermute | solution.py:416
  37.2 11.0 %collective-permute-start.6 = (bf16[6,10,16,128]{3,2,1,0:T(8,128)(2,1)S(1)}, bf16[6,10,16,128]{3,2,1,0:T(8,128)(2,1)S(1)}, u32[]{:S(2)}, u32[]{:S(2)}) collective-permute-start(bf16[6,10,16,128]{3,2,1,0:T(8,128)(2,1)S(1)} %get-tuple-element.38), channel_id=1, source_target_pairs={{4,8},{8,4},{12,16},{16,12},{20,24},{24,20},{28,32},{32,28},{36,40... | collective-permute-start | bytes 737288 | tf_op jit(solution)/shard_map/halo/ppermute | solution.py:415
  46.1 7.5 %collective-permute-start.7 = (f32[64,256]{1,0:T(8,128)S(1)}, f32[64,256]{1,0:T(8,128)S(1)}, u32[]{:S(2)}, u32[]{:S(2)}) collective-permute-start(f32[64,256]{1,0:T(8,128)S(1)} %return_tiles.2.below_ref), channel_id=1, source_target_pairs={{0,4},{4,0},{8,12},{12,8},{16,20},{20,16},{24,28},{28,24},{32,36},... | collective-permute-start | bytes 196616 | tf_op jit(solution)/shard_map/return_tiles/ppermute | solution.py:423
  49.7 3.9 %collective-permute-start.8 = (f32[64,256]{1,0:T(8,128)S(1)}, f32[64,256]{1,0:T(8,128)S(1)}, u32[]{:S(2)}, u32[]{:S(2)}) collective-permute-start(f32[64,256]{1,0:T(8,128)S(1)} %return_tiles.3.above_ref), channel_id=1, source_target_pairs={{4,8},{8,4},{12,16},{16,12},{20,24},{24,20},{28,32},{32,28},{36,40... | collective-permute-start | bytes 196616 | tf_op jit(solution)/shard_map/return_tiles/ppermute | solution.py:421
  54.3 29.2 %all-to-all-start = ((bf16[256,2,128]{2,1,0:T(2,128)(2,1)}), bf16[256,2,128]{2,1,0:T(2,128)(2,1)S(1)}, u32[]{:S(2)}, u32[]{:S(2)}) async-start(bf16[256,2,128]{2,1,0:T(2,128)(2,1)} %get-tuple-element.41), calls=%async_computation | async-start | bytes 262144 | tf_op jit(solution)/shard_map/sums/all_to_all | solution.py:428
  70.5 5.5 %collective-permute-start.9 = (f32[64,256]{1,0:T(8,128)S(1)}, f32[64,256]{1,0:T(8,128)S(1)}, u32[]{:S(2)}, u32[]{:S(2)}) collective-permute-start(f32[64,256]{1,0:T(8,128)S(1)} %get-tuple-element.40.refs_0_), channel_id=1, source_target_pairs={{0,1},{1,0},{2,3},{3,2},{4,5},{5,4},{6,7},{7,6},{8,9},{9,8},{10,11... | collective-permute-start | bytes 196616 | tf_op jit(solution)/shard_map/sums/ppermute | solution.py:430
  72.8 5.4 %collective-permute-start.10 = (f32[64,256]{1,0:T(8,128)S(1)}, f32[64,256]{1,0:T(8,128)S(1)}, u32[]{:S(2)}, u32[]{:S(2)}) collective-permute-start(f32[64,256]{1,0:T(8,128)S(1)} %get-tuple-element.40.refs_0_), channel_id=1, source_target_pairs={{0,2},{1,3},{2,0},{3,1},{4,6},{5,7},{6,4},{7,5},{8,10},{9,11},{10,... | collective-permute-start | bytes 196616 | tf_op jit(solution)/shard_map/sums/ppermute | solution.py:430
  73.9 6.6 %collective-permute-start.11 = (f32[64,256]{1,0:T(8,128)S(1)}, f32[64,256]{1,0:T(8,128)S(1)}, u32[]{:S(2)}, u32[]{:S(2)}) collective-permute-start(f32[64,256]{1,0:T(8,128)S(1)} %get-tuple-element.40.refs_0_), channel_id=1, source_target_pairs={{0,3},{1,2},{2,1},{3,0},{4,7},{5,6},{6,5},{7,4},{8,11},{9,10},{10,... | collective-permute-start | bytes 196616 | tf_op jit(solution)/shard_map/sums/ppermute | solution.py:430

commit v8 on v7

--- a/solution.py
+++ b/solution.py
@@ -419,6 +419,7 @@
     with jax.named_scope("return_tiles"):
         above = return_tiles(cross, seconds, 1, density, me, groups)
         from_above = lax.ppermute(above, "space", odd)
+        firsts, above = lax.optimization_barrier((firsts, above))
         below = return_tiles(cross, firsts, 0, density, me, groups)
         from_below = lax.ppermute(below, "space", even)
     with jax.named_scope("edge_tiles"):

time: 84.9 us -> 84 us (0.989)
    all_to_all x1, starting transfers between devices: 16.2 us -> 12.6 us  [body(): sent = lax.all_to_all(wide, ('space', 'snap'), 0, 0, tiled=True)]
    ppermute x1, starting transfers between devices: 2.13 us -> 5.47 us  [body(): from_below = lax.ppermute(below, 'space', even)]
  transfers between devices with their start and end apart: 13 -> 13, of which waited for: 6 -> 5; matrix products, arithmetic and copies ran while one was open for 0% -> 0% of each run, Pallas kernels for 16% -> 16%
where the time goes in v8:
time: 84 us; the launch traced here: 83.7 us
  starting transfers between devices  32.3 us (38%)
  waiting for transfers between devices  31 us (37%)
  Pallas kernels  16.4 us (20%)
  local copies, waits for them, and re-layouts  3.09 us (4%)
    ppermute x3, waiting for transfers between devices, body(): lax.ppermute(mine[m], 'snap', [(i, i ^ m) for i in range(groups)])  23.4 us
    all_to_all x1, starting transfers between devices, body(): sent = lax.all_to_all(wide, ('space', 'snap'), 0, 0, tiled=True)  12.6 us
    ppermute x3, starting transfers between devices, body(): lax.ppermute(mine[m], 'snap', [(i, i ^ m) for i in range(groups)])  6.56 us
    pallas_call x1, Pallas kernels, local_tiles(): pl.pallas_call(functools.partial(local_kernel, groups, density.shape[0]),...  5.96 us
    ppermute x1, starting transfers between devices, body(): from_below = lax.ppermute(below, 'space', even)  5.47 us
    ppermute x3, starting transfers between devices, body(): lax.ppermute(part, 'snap', [(i, i ^ m) for i in range(groups)])  5.47 us
    ppermute x3, waiting for transfers between devices, body(): lax.ppermute(part, 'snap', [(i, i ^ m) for i in range(groups)])  4.49 us
    pallas_call x1, Pallas kernels, edge_tiles(): pl.pallas_call(functools.partial(edge_kernel, groups, materials, len(lows...  3.17 us
  transfers between devices with their start and end apart: 13, of which 5 were waited for; matrix products, arithmetic and copies ran while one was open for 0% of the time, Pallas kernels for 16%

profile of v8, /device:TPU:1, one launch (start us, length us, event | category | flops | bytes accessed | tf_op | source)
XLA Modules:
  0.0 83.7 jit_solution(7714196861590333629)
XLA Ops:
  0.6 0.0 copy-start.4
  0.6 0.0 copy-start
  0.7 1.4 %copy-done = bf16[16,3,2,64,128]{4,3,2,1,0:T(8,128)(2,1)S(1)} copy-done((bf16[16,3,2,64,128]{4,3,2,1,0:T(8,128)(2,1)S(1)}, bf16[16,3,2,64,128]{4,3,2,1,0:T(8,128)(2,1)}, u32[]{:S(2)}) %copy-start) | copy-done | bytes 1572888
  2.1 0.0 copy-start.1
  2.1 0.8 %copy-done.1 = s32[2,64,128]{2,1,0:T(8,128)S(1)} copy-done((s32[2,64,128]{2,1,0:T(8,128)S(1)}, s32[2,64,128]{2,1,0:T(8,128)}, u32[]{:S(2)}) %copy-start.1) | copy-done | bytes 65560
  2.9 0.0 copy-start.3
  2.9 1.3 %spread.1 = (bf16[3,2,18,16,128]{4,3,2,1,0:T(8,128)(2,1)S(1)}, bf16[3,2,18,16,128]{4,3,2,1,0:T(8,128)(2,1)S(1)}, bf16[3,2,18,16,128]{4,3,2,1,0:T(8,128)(2,1)S(1)}, bf16[3,2,18,16,128]{4,3,2,1,0:T(8,128)(2,1)S(1)}) custom-call(s32[1]{0:T(128)} %bitcast.me_ref, bf16[16,3,2,64,128]{4,3,2,1,0:T(8,128)(2,1)S(1)} %copy-done, s32[2,64,128]{2,1,0:T(8,128)S(1)} %copy-done.1), custom_call_target="tpu_custom_call" | custom-call | bytes 5242880 | tf_op jit(solution)/shard_map/spread/pallas_call | solution.py:31
  4.2 3.3 %collective-permute-start = (bf16[3,2,18,16,128]{4,3,2,1,0:T(8,128)(2,1)S(1)}, bf16[3,2,18,16,128]{4,3,2,1,0:T(8,128)(2,1)S(1)}, u32[]{:S(2)}, u32[]{:S(2)}) collective-permute-start(bf16[3,2,18,16,128]{4,3,2,1,0:T(8,128)(2,1)S(1)} %get-tuple-element.27), channel_id=1, source_target_pairs={{0,1},{1,0},{2,3},{3,2},{4,5},{5,4},{6,7},{7,6},{8,9},{9,8},{10,11... | collective-permute-start | bytes 1327112 | tf_op jit(solution)/shard_map/regroup/ppermute | solution.py:401
  7.5 1.2 %collective-permute-start.1 = (bf16[3,2,18,16,128]{4,3,2,1,0:T(8,128)(2,1)S(1)}, bf16[3,2,18,16,128]{4,3,2,1,0:T(8,128)(2,1)S(1)}, u32[]{:S(2)}, u32[]{:S(2)}) collective-permute-start(bf16[3,2,18,16,128]{4,3,2,1,0:T(8,128)(2,1)S(1)} %get-tuple-element.28), channel_id=1, source_target_pairs={{0,2},{1,3},{2,0},{3,1},{4,6},{5,7},{6,4},{7,5},{8,10},{9,11},{10,... | collective-permute-start | bytes 1327112 | tf_op jit(solution)/shard_map/regroup/ppermute | solution.py:401
  8.7 2.0 %collective-permute-start.2 = (bf16[3,2,18,16,128]{4,3,2,1,0:T(8,128)(2,1)S(1)}, bf16[3,2,18,16,128]{4,3,2,1,0:T(8,128)(2,1)S(1)}, u32[]{:S(2)}, u32[]{:S(2)}) collective-permute-start(bf16[3,2,18,16,128]{4,3,2,1,0:T(8,128)(2,1)S(1)} %get-tuple-element.29), channel_id=1, source_target_pairs={{0,3},{1,2},{2,1},{3,0},{4,7},{5,6},{6,5},{7,4},{8,11},{9,10},{10,... | collective-permute-start | bytes 1327112 | tf_op jit(solution)/shard_map/regroup/ppermute | solution.py:401
  10.7 0.1 pad_add_fusion.me_ref
  10.8 0.0 collective-permute-done.refs_1_
  10.8 0.0 copy-start.2
  10.8 0.8 %copy-done.2 = s32[2,64,128]{2,1,0:T(8,128)S(1)} copy-done((s32[2,64,128]{2,1,0:T(8,128)S(1)}, s32[2,64,128]{2,1,0:T(8,128)}, u32[]{:S(2)}) %copy-start.2) | copy-done | bytes 65560
  11.7 0.7 halo.2
  12.4 0.1 collective-permute-start.3
  12.5 0.7 collective-permute-start.5
  13.1 7.6 %collective-permute-done.1.refs_2_.refs_0_ = bf16[3,2,18,16,128]{4,3,2,1,0:T(8,128)(2,1)S(1)} collective-permute-done((bf16[3,2,18,16,128]{4,3,2,1,0:T(8,128)(2,1)S(1)}, bf16[3,2,18,16,128]{4,3,2,1,0:T(8,128)(2,1)S(1)}, u32[]{:S(2)}, u32[]{:S(2)}) %collective-permute-start.1) | collective-permute-done | bytes 442400 | tf_op jit(solution)/shard_map/regroup/ppermute | solution.py:401
  20.7 15.8 %collective-permute-done.2.refs_3_.refs_1_ = bf16[3,2,18,16,128]{4,3,2,1,0:T(8,128)(2,1)S(1)} collective-permute-done((bf16[3,2,18,16,128]{4,3,2,1,0:T(8,128)(2,1)S(1)}, bf16[3,2,18,16,128]{4,3,2,1,0:T(8,128)(2,1)S(1)}, u32[]{:S(2)}, u32[]{:S(2)}) %collective-permute-start.2) | collective-permute-done | bytes 442400 | tf_op jit(solution)/shard_map/regroup/ppermute | solution.py:401
  36.6 0.6 halo.3
  37.1 0.1 collective-permute-start.4
  37.2 0.7 collective-permute-start.6
  37.9 0.0 copy-done.4
  37.9 0.0 copy-done.3
  37.9 6.0 %local_tiles.1 = (f32[64,256]{1,0:T(8,128)S(1)}, f32[3,2,512,256]{3,2,1,0:T(8,128)S(1)}, f32[3,2,512,256]{3,2,1,0:T(8,128)S(1)}, bf16[2,64,3072]{2,1,0:T(8,128)(2,1)S(1)}) custom-call(s32[2]{0:T(128)S(1)} %pad_add_fusion.me_ref, f32[3]{0:T(128)S(1)} %copy-done.4, bf16[3,2,18,16,128]{4,3,2,1,0:T(8,128)(2,1)S(1)} %get-tuple-element.26.refs_0_, ...), custom_call_target="tpu_custom_call" | custom-call | flops 5000000000 | bytes 12582912 | tf_op jit(solution)/shard_map/local_tiles/pallas_call | solution.py:204
  43.9 0.0 collective-permute-done.6.refs_1_.refs_3_
  43.9 0.0 collective-permute-done.5.refs_0_.refs_2_
  43.9 1.5 %return_tiles.2.above_ref = f32[64,256]{1,0:T(8,128)S(1)} custom-call(s32[2]{0:T(128)S(1)} %pad_add_fusion.me_ref, f32[3]{0:T(128)S(1)} %copy-done.4, f32[3,2,512,256]{3,2,1,0:T(8,128)S(1)} %get-tuple-element.41.cross_ref, bf16[7,10,16,128]{3,2,1,0:T(8,128)(2,1)S(1)} %collective-permute-done.5.refs_0_.refs_2_, ...), custom_call_target="tpu_custom_call" | custom-call | flops 3000000000 | bytes 6291456 | tf_op jit(solution)/shard_map/return_tiles/pallas_call | solution.py:268
  45.4 0.7 collective-permute-start.8
  46.1 0.0 collective-permute-done.4.refs_1_
  46.1 0.0 collective-permute-done.3.refs_0_
  46.1 1.5 %return_tiles.3.below_ref = f32[64,256]{1,0:T(8,128)S(1)} custom-call(s32[2]{0:T(128)S(1)} %pad_add_fusion.me_ref, f32[3]{0:T(128)S(1)} %copy-done.4, f32[3,2,512,256]{3,2,1,0:T(8,128)S(1)} %get-tuple-element.41.cross_ref, bf16[7,10,16,128]{3,2,1,0:T(8,128)(2,1)S(1)} %collective-permute-done.3.refs_0_, ...), custom_call_target="tpu_custom_call" | custom-call | flops 3000000000 | bytes 6291456 | tf_op jit(solution)/shard_map/return_tiles/pallas_call | solution.py:268
  47.6 5.5 %collective-permute-start.7 = (f32[64,256]{1,0:T(8,128)S(1)}, f32[64,256]{1,0:T(8,128)S(1)}, u32[]{:S(2)}, u32[]{:S(2)}) collective-permute-start(f32[64,256]{1,0:T(8,128)S(1)} %return_tiles.3.below_ref), channel_id=1, source_target_pairs={{0,4},{4,0},{8,12},{12,8},{16,20},{20,16},{24,28},{28,24},{32,36},... | collective-permute-start | bytes 196616 | tf_op jit(solution)/shard_map/return_tiles/ppermute | solution.py:424
  53.1 3.2 %edge_tiles.1.part_ref = f32[64,256]{1,0:T(8,128)S(1)} custom-call(s32[2]{0:T(128)S(1)} %pad_add_fusion.me_ref, f32[3]{0:T(128)S(1)} %copy-done.4, f32[64,256]{1,0:T(8,128)S(1)} %get-tuple-element.31.near_ref, f32[3,2,512,256]{3,2,1,0:T(8,128)S(1)} %get-tuple-element.32.edge_ref, bf16[2,64,3072]{2,1,0:T(8,128)(2,1)S(1)} %get-tuple-element.33.left_ref, ...), custom_call_target="tpu_custom_call" | custom-call | flops 5000000000 | bytes 20971520 | tf_op jit(solution)/shard_map/edge_tiles/pallas_call | solution.py:354
  56.3 0.0 collective-permute-done.7.from_below_ref
  56.3 0.0 collective-permute-done.8.from_above_ref
  56.3 0.7 sums.2
  57.0 12.6 %all-to-all-start = ((bf16[256,2,128]{2,1,0:T(2,128)(2,1)}), bf16[256,2,128]{2,1,0:T(2,128)(2,1)S(1)}, u32[]{:S(2)}, u32[]{:S(2)}) async-start(bf16[256,2,128]{2,1,0:T(2,128)(2,1)} %get-tuple-element.47), calls=%async_computation | async-start | bytes 262144 | tf_op jit(solution)/shard_map/sums/all_to_all | solution.py:429
  69.7 2.2 %collective-permute-start.9 = (f32[64,256]{1,0:T(8,128)S(1)}, f32[64,256]{1,0:T(8,128)S(1)}, u32[]{:S(2)}, u32[]{:S(2)}) collective-permute-start(f32[64,256]{1,0:T(8,128)S(1)} %get-tuple-element.46.refs_0_), channel_id=1, source_target_pairs={{0,1},{1,0},{2,3},{3,2},{4,5},{5,4},{6,7},{7,6},{8,9},{9,8},{10,11... | collective-permute-start | bytes 196616 | tf_op jit(solution)/shard_map/sums/ppermute | solution.py:431
  71.9 1.1 %collective-permute-start.10 = (f32[64,256]{1,0:T(8,128)S(1)}, f32[64,256]{1,0:T(8,128)S(1)}, u32[]{:S(2)}, u32[]{:S(2)}) collective-permute-start(f32[64,256]{1,0:T(8,128)S(1)} %get-tuple-element.46.refs_0_), channel_id=1, source_target_pairs={{0,2},{1,3},{2,0},{3,1},{4,6},{5,7},{6,4},{7,5},{8,10},{9,11},{10,... | collective-permute-start | bytes 196616 | tf_op jit(solution)/shard_map/sums/ppermute | solution.py:431
  73.0 2.1 %collective-permute-start.11 = (f32[64,256]{1,0:T(8,128)S(1)}, f32[64,256]{1,0:T(8,128)S(1)}, u32[]{:S(2)}, u32[]{:S(2)}) collective-permute-start(f32[64,256]{1,0:T(8,128)S(1)} %get-tuple-element.46.refs_0_), channel_id=1, source_target_pairs={{0,3},{1,2},{2,1},{3,0},{4,7},{5,6},{6,5},{7,4},{8,11},{9,10},{10,... | collective-permute-start | bytes 196616 | tf_op jit(solution)/shard_map/sums/ppermute | solution.py:431
  75.1 0.0 collective-permute-done.9.refs_1_
  75.1 2.2 %collective-permute-done.10.refs_2_ = f32[64,256]{1,0:T(8,128)S(1)} collective-permute-done((f32[64,256]{1,0:T(8,128)S(1)}, f32[64,256]{1,0:T(8,128)S(1)}, u32[]{:S(2)}, u32[]{:S(2)}) %collective-permute-start.10) | collective-permute-done | bytes 65568 | tf_op jit(solution)/shard_map/sums/ppermute | solution.py:431
  77.3 2.3 %collective-permute-done.11.refs_3_ = f32[64,256]{1,0:T(8,128)S(1)} collective-permute-done((f32[64,256]{1,0:T(8,128)S(1)}, f32[64,256]{1,0:T(8,128)S(1)}, u32[]{:S(2)}, u32[]{:S(2)}) %collective-permute-start.11) | collective-permute-done | bytes 65568 | tf_op jit(solution)/shard_map/sums/ppermute | solution.py:431
  79.6 3.1 %all-to-all-done.refs_4_ = bf16[256,2,128]{2,1,0:T(2,128)(2,1)S(1)} async-done(((bf16[256,2,128]{2,1,0:T(2,128)(2,1)}), bf16[256,2,128]{2,1,0:T(2,128)(2,1)S(1)}, u32[]{:S(2)}, u32[]{:S(2)}) %all-to-all-start) | async-done | bytes 131104 | tf_op jit(solution)/shard_map/sums/all_to_all | solution.py:429
  82.7 1.0 %sums.3 = (f32[1,4,64,64]{3,2,1,0:T(8,128)}, f32[4,1,64]{2,1,0:T(1,128)}) custom-call(f32[64,256]{1,0:T(8,128)S(1)} %get-tuple-element.46.refs_0_, f32[64,256]{1,0:T(8,128)S(1)} %collective-permute-done.9.refs_1_, f32[64,256]{1,0:T(8,128)S(1)} %collective-permute-done.10.refs_2_, f32[64,256]{1,0:T(8,128)S(1)} %collective-permute-done.11.refs_3_, ...), custom_call_target="tpu_custom_call" | custom-call | tf_op jit(solution)/shard_map/sums/pallas_call | solution.py:381
Async XLA Ops:
  0.6 37.3 %copy-start.4 = (f32[3]{0:T(128)S(1)}, f32[3]{0:T(128)}, u32[]{:S(2)}) copy-start(f32[3]{0:T(128)} %density_ref.7) | copy-start | bytes 40
  0.6 1.4 %copy-start = (bf16[16,3,2,64,128]{4,3,2,1,0:T(8,128)(2,1)S(1)}, bf16[16,3,2,64,128]{4,3,2,1,0:T(8,128)(2,1)}, u32[]{:S(2)}) copy-start(bf16[16,3,2,64,128]{4,3,2,1,0:T(8,128)(2,1)} %snaps_ref.1) | copy-start | bytes 4718596
  2.1 0.8 %copy-start.1 = (s32[2,64,128]{2,1,0:T(8,128)S(1)}, s32[2,64,128]{2,1,0:T(8,128)}, u32[]{:S(2)}) copy-start(s32[2,64,128]{2,1,0:T(8,128)} %mask_ref.1) | copy-start | bytes 196612
  2.9 35.0 %copy-start.3 = (s32[2,64,128]{2,1,0:T(8,128)S(1)}, s32[2,64,128]{2,1,0:T(8,128)}, u32[]{:S(2)}) copy-start(s32[2,64,128]{2,1,0:T(8,128)} %refs_4_.3) | copy-start | bytes 196612
  4.2 6.6 %collective-permute-start = (bf16[3,2,18,16,128]{4,3,2,1,0:T(8,128)(2,1)S(1)}, bf16[3,2,18,16,128]{4,3,2,1,0:T(8,128)(2,1)S(1)}, u32[]{:S(2)}, u32[]{:S(2)}) collective-permute-start(bf16[3,2,18,16,128]{4,3,2,1,0:T(8,128)(2,1)S(1)} %get-tuple-element.27), channel_id=1, source_target_pairs={{0,1},{1,0},{2,3},{3,2},{4,5},{5,4},{6,7},{7,6},{8,9},{9,8},{10,11... | collective-permute-start | bytes 1327112 | tf_op jit(solution)/shard_map/regroup/ppermute | solution.py:401
  7.5 13.2 %collective-permute-start.1 = (bf16[3,2,18,16,128]{4,3,2,1,0:T(8,128)(2,1)S(1)}, bf16[3,2,18,16,128]{4,3,2,1,0:T(8,128)(2,1)S(1)}, u32[]{:S(2)}, u32[]{:S(2)}) collective-permute-start(bf16[3,2,18,16,128]{4,3,2,1,0:T(8,128)(2,1)S(1)} %get-tuple-element.28), channel_id=1, source_target_pairs={{0,2},{1,3},{2,0},{3,1},{4,6},{5,7},{6,4},{7,5},{8,10},{9,11},{10,... | collective-permute-start | bytes 1327112 | tf_op jit(solution)/shard_map/regroup/ppermute | solution.py:401
  8.7 27.8 %collective-permute-start.2 = (bf16[3,2,18,16,128]{4,3,2,1,0:T(8,128)(2,1)S(1)}, bf16[3,2,18,16,128]{4,3,2,1,0:T(8,128)(2,1)S(1)}, u32[]{:S(2)}, u32[]{:S(2)}) collective-permute-start(bf16[3,2,18,16,128]{4,3,2,1,0:T(8,128)(2,1)S(1)} %get-tuple-element.29), channel_id=1, source_target_pairs={{0,3},{1,2},{2,1},{3,0},{4,7},{5,6},{6,5},{7,4},{8,11},{9,10},{10,... | collective-permute-start | bytes 1327112 | tf_op jit(solution)/shard_map/regroup/ppermute | solution.py:401
  10.8 0.8 %copy-start.2 = (s32[2,64,128]{2,1,0:T(8,128)S(1)}, s32[2,64,128]{2,1,0:T(8,128)}, u32[]{:S(2)}) copy-start(s32[2,64,128]{2,1,0:T(8,128)} %refs_4_.3) | copy-start | bytes 196612
  12.4 33.8 %collective-permute-start.3 = (bf16[7,10,16,128]{3,2,1,0:T(8,128)(2,1)S(1)}, bf16[7,10,16,128]{3,2,1,0:T(8,128)(2,1)S(1)}, u32[]{:S(2)}, u32[]{:S(2)}) collective-permute-start(bf16[7,10,16,128]{3,2,1,0:T(8,128)(2,1)S(1)} %get-tuple-element.36), channel_id=1, source_target_pairs={{0,4},{4,0},{8,12},{12,8},{16,20},{20,16},{24,28},{28,24},{32,36},... | collective-permute-start | bytes 860168 | tf_op jit(solution)/shard_map/halo/ppermute | solution.py:416
  12.5 31.5 %collective-permute-start.5 = (bf16[7,10,16,128]{3,2,1,0:T(8,128)(2,1)S(1)}, bf16[7,10,16,128]{3,2,1,0:T(8,128)(2,1)S(1)}, u32[]{:S(2)}, u32[]{:S(2)}) collective-permute-start(bf16[7,10,16,128]{3,2,1,0:T(8,128)(2,1)S(1)} %get-tuple-element.37), channel_id=1, source_target_pairs={{4,8},{8,4},{12,16},{16,12},{20,24},{24,20},{28,32},{32,28},{36,40... | collective-permute-start | bytes 860168 | tf_op jit(solution)/shard_map/halo/ppermute | solution.py:415
  37.1 9.0 %collective-permute-start.4 = (bf16[6,10,16,128]{3,2,1,0:T(8,128)(2,1)S(1)}, bf16[6,10,16,128]{3,2,1,0:T(8,128)(2,1)S(1)}, u32[]{:S(2)}, u32[]{:S(2)}) collective-permute-start(bf16[6,10,16,128]{3,2,1,0:T(8,128)(2,1)S(1)} %get-tuple-element.40), channel_id=1, source_target_pairs={{0,4},{4,0},{8,12},{12,8},{16,20},{20,16},{24,28},{28,24},{32,36},... | collective-permute-start | bytes 737288 | tf_op jit(solution)/shard_map/halo/ppermute | solution.py:416
  37.2 6.7 %collective-permute-start.6 = (bf16[6,10,16,128]{3,2,1,0:T(8,128)(2,1)S(1)}, bf16[6,10,16,128]{3,2,1,0:T(8,128)(2,1)S(1)}, u32[]{:S(2)}, u32[]{:S(2)}) collective-permute-start(bf16[6,10,16,128]{3,2,1,0:T(8,128)(2,1)S(1)} %get-tuple-element.42), channel_id=1, source_target_pairs={{4,8},{8,4},{12,16},{16,12},{20,24},{24,20},{28,32},{32,28},{36,40... | collective-permute-start | bytes 737288 | tf_op jit(solution)/shard_map/halo/ppermute | solution.py:415
  45.4 10.9 %collective-permute-start.8 = (f32[64,256]{1,0:T(8,128)S(1)}, f32[64,256]{1,0:T(8,128)S(1)}, u32[]{:S(2)}, u32[]{:S(2)}) collective-permute-start(f32[64,256]{1,0:T(8,128)S(1)} %return_tiles.2.above_ref), channel_id=1, source_target_pairs={{4,8},{8,4},{12,16},{16,12},{20,24},{24,20},{28,32},{32,28},{36,40... | collective-permute-start | bytes 196616 | tf_op jit(solution)/shard_map/return_tiles/ppermute | solution.py:421
  47.6 8.6 %collective-permute-start.7 = (f32[64,256]{1,0:T(8,128)S(1)}, f32[64,256]{1,0:T(8,128)S(1)}, u32[]{:S(2)}, u32[]{:S(2)}) collective-permute-start(f32[64,256]{1,0:T(8,128)S(1)} %return_tiles.3.below_ref), channel_id=1, source_target_pairs={{0,4},{4,0},{8,12},{12,8},{16,20},{20,16},{24,28},{28,24},{32,36},... | collective-permute-start | bytes 196616 | tf_op jit(solution)/shard_map/return_tiles/ppermute | solution.py:424
  57.0 25.6 %all-to-all-start = ((bf16[256,2,128]{2,1,0:T(2,128)(2,1)}), bf16[256,2,128]{2,1,0:T(2,128)(2,1)S(1)}, u32[]{:S(2)}, u32[]{:S(2)}) async-start(bf16[256,2,128]{2,1,0:T(2,128)(2,1)} %get-tuple-element.47), calls=%async_computation | async-start | bytes 262144 | tf_op jit(solution)/shard_map/sums/all_to_all | solution.py:429
  69.7 5.5 %collective-permute-start.9 = (f32[64,256]{1,0:T(8,128)S(1)}, f32[64,256]{1,0:T(8,128)S(1)}, u32[]{:S(2)}, u32[]{:S(2)}) collective-permute-start(f32[64,256]{1,0:T(8,128)S(1)} %get-tuple-element.46.refs_0_), channel_id=1, source_target_pairs={{0,1},{1,0},{2,3},{3,2},{4,5},{5,4},{6,7},{7,6},{8,9},{9,8},{10,11... | collective-permute-start | bytes 196616 | tf_op jit(solution)/shard_map/sums/ppermute | solution.py:431
  71.9 5.4 %collective-permute-start.10 = (f32[64,256]{1,0:T(8,128)S(1)}, f32[64,256]{1,0:T(8,128)S(1)}, u32[]{:S(2)}, u32[]{:S(2)}) collective-permute-start(f32[64,256]{1,0:T(8,128)S(1)} %get-tuple-element.46.refs_0_), channel_id=1, source_target_pairs={{0,2},{1,3},{2,0},{3,1},{4,6},{5,7},{6,4},{7,5},{8,10},{9,11},{10,... | collective-permute-start | bytes 196616 | tf_op jit(solution)/shard_map/sums/ppermute | solution.py:431
  73.0 6.6 %collective-permute-start.11 = (f32[64,256]{1,0:T(8,128)S(1)}, f32[64,256]{1,0:T(8,128)S(1)}, u32[]{:S(2)}, u32[]{:S(2)}) collective-permute-start(f32[64,256]{1,0:T(8,128)S(1)} %get-tuple-element.46.refs_0_), channel_id=1, source_target_pairs={{0,3},{1,2},{2,1},{3,0},{4,7},{5,6},{6,5},{7,4},{8,11},{9,10},{10,... | collective-permute-start | bytes 196616 | tf_op jit(solution)/shard_map/sums/ppermute | solution.py:431

commit v9 on v8

--- a/solution.py
+++ b/solution.py
@@ -409,6 +409,9 @@
             if firsts:
                 some, *_ = lax.optimization_barrier((some, to_even, to_odd))
             to_even, to_odd, *stencil = pack(some, None if firsts else labels, me)
+            if firsts:
+                some, to_odd = lax.optimization_barrier((some, to_odd))
+                to_even, _ = pack(some, None, me)
             if not firsts:
                 weights = stencil[0]
                 some, to_even, to_odd = lax.optimization_barrier((some, to_even, to_odd))

time: 84 us -> 85.9 us (1.023)
  Pallas kernels: 16.4 us -> 18.4 us
    pallas_call x2 -> x3, Pallas kernels: 1.26 us -> 3.24 us  [pack(): pl.pallas_call(functools.partial(pack_kernel, len(pair)), out_shape=outs,...]
  transfers between devices with their start and end apart: 13 -> 13, of which waited for: 5 -> 5; matrix products, arithmetic and copies ran while one was open for 0% -> 0% of each run, Pallas kernels for 16% -> 18%
where the time goes in v9:
time: 85.9 us; the launch traced here: 85.6 us
  starting transfers between devices  32.2 us (37%)
  waiting for transfers between devices  31 us (36%)
  Pallas kernels  18.4 us (21%)
  local copies, waits for them, and re-layouts  3.09 us (4%)
    ppermute x3, waiting for transfers between devices, body(): lax.ppermute(mine[m], 'snap', [(i, i ^ m) for i in range(groups)])  23.4 us
    all_to_all x1, starting transfers between devices, body(): sent = lax.all_to_all(wide, ('space', 'snap'), 0, 0, tiled=True)  12.6 us
    ppermute x3, starting transfers between devices, body(): lax.ppermute(mine[m], 'snap', [(i, i ^ m) for i in range(groups)])  6.56 us
    pallas_call x1, Pallas kernels, local_tiles(): pl.pallas_call(functools.partial(local_kernel, groups, density.shape[0]),...  5.96 us
    ppermute x1, starting transfers between devices, body(): from_below = lax.ppermute(below, 'space', even)  5.49 us
    ppermute x3, starting transfers between devices, body(): lax.ppermute(part, 'snap', [(i, i ^ m) for i in range(groups)])  5.47 us
    ppermute x3, waiting for transfers between devices, body(): lax.ppermute(part, 'snap', [(i, i ^ m) for i in range(groups)])  4.49 us
    pallas_call x3, Pallas kernels, pack(): pl.pallas_call(functools.partial(pack_kernel, len(pair)), out_shape=outs,...  3.24 us
  transfers between devices with their start and end apart: 13, of which 5 were waited for; matrix products, arithmetic and copies ran while one was open for 0% of the time, Pallas kernels for 18%

profile of v9, /device:TPU:1, one launch (start us, length us, event | category | flops | bytes accessed | tf_op | source)
XLA Modules:
  0.0 85.6 jit_solution(16293992206315569875)
XLA Ops:
  0.6 0.0 copy-start.4
  0.6 0.0 copy-start
  0.7 1.4 %copy-done = bf16[16,3,2,64,128]{4,3,2,1,0:T(8,128)(2,1)S(1)} copy-done((bf16[16,3,2,64,128]{4,3,2,1,0:T(8,128)(2,1)S(1)}, bf16[16,3,2,64,128]{4,3,2,1,0:T(8,128)(2,1)}, u32[]{:S(2)}) %copy-start) | copy-done | bytes 1572888
  2.1 0.0 copy-start.1
  2.1 0.8 copy-done.1
  2.9 0.0 copy-start.3
  2.9 1.3 %spread.1 = (bf16[3,2,18,16,128]{4,3,2,1,0:T(8,128)(2,1)S(1)}, bf16[3,2,18,16,128]{4,3,2,1,0:T(8,128)(2,1)S(1)}, bf16[3,2,18,16,128]{4,3,2,1,0:T(8,128)(2,1)S(1)}, bf16[3,2,18,16,128]{4,3,2,1,0:T(8,128)(2,1)S(1)}) custom-call(s32[1]{0:T(128)} %bitcast.me_ref, bf16[16,3,2,64,128]{4,3,2,1,0:T(8,128)(2,1)S(1)} %copy-done, s32[2,64,128]{2,1,0:T(8,128)S(1)} %copy-done.1), custom_call_target="tpu_custom_call" | custom-call | bytes 5242880 | tf_op jit(solution)/shard_map/spread/pallas_call | solution.py:31
  4.2 3.3 %collective-permute-start = (bf16[3,2,18,16,128]{4,3,2,1,0:T(8,128)(2,1)S(1)}, bf16[3,2,18,16,128]{4,3,2,1,0:T(8,128)(2,1)S(1)}, u32[]{:S(2)}, u32[]{:S(2)}) collective-permute-start(bf16[3,2,18,16,128]{4,3,2,1,0:T(8,128)(2,1)S(1)} %get-tuple-element.30), channel_id=1, source_target_pairs={{0,1},{1,0},{2,3},{3,2},{4,5},{5,4},{6,7},{7,6},{8,9},{9,8},{10,11... | collective-permute-start | bytes 1327112 | tf_op jit(solution)/shard_map/regroup/ppermute | solution.py:401
  7.5 1.2 %collective-permute-start.1 = (bf16[3,2,18,16,128]{4,3,2,1,0:T(8,128)(2,1)S(1)}, bf16[3,2,18,16,128]{4,3,2,1,0:T(8,128)(2,1)S(1)}, u32[]{:S(2)}, u32[]{:S(2)}) collective-permute-start(bf16[3,2,18,16,128]{4,3,2,1,0:T(8,128)(2,1)S(1)} %get-tuple-element.31), channel_id=1, source_target_pairs={{0,2},{1,3},{2,0},{3,1},{4,6},{5,7},{6,4},{7,5},{8,10},{9,11},{10,... | collective-permute-start | bytes 1327112 | tf_op jit(solution)/shard_map/regroup/ppermute | solution.py:401
  8.7 2.0 %collective-permute-start.2 = (bf16[3,2,18,16,128]{4,3,2,1,0:T(8,128)(2,1)S(1)}, bf16[3,2,18,16,128]{4,3,2,1,0:T(8,128)(2,1)S(1)}, u32[]{:S(2)}, u32[]{:S(2)}) collective-permute-start(bf16[3,2,18,16,128]{4,3,2,1,0:T(8,128)(2,1)S(1)} %get-tuple-element.32), channel_id=1, source_target_pairs={{0,3},{1,2},{2,1},{3,0},{4,7},{5,6},{6,5},{7,4},{8,11},{9,10},{10,... | collective-permute-start | bytes 1327112 | tf_op jit(solution)/shard_map/regroup/ppermute | solution.py:401
  10.7 0.1 pad_add_fusion.me_ref
  10.8 0.0 collective-permute-done.refs_1_
  10.8 0.0 copy-start.2
  10.8 0.8 copy-done.2
  11.7 0.7 halo.3
  12.4 0.1 collective-permute-start.3
  12.5 0.7 collective-permute-start.5
  13.1 7.6 %collective-permute-done.1.refs_2_.refs_0_ = bf16[3,2,18,16,128]{4,3,2,1,0:T(8,128)(2,1)S(1)} collective-permute-done((bf16[3,2,18,16,128]{4,3,2,1,0:T(8,128)(2,1)S(1)}, bf16[3,2,18,16,128]{4,3,2,1,0:T(8,128)(2,1)S(1)}, u32[]{:S(2)}, u32[]{:S(2)}) %collective-permute-start.1) | collective-permute-done | bytes 442400 | tf_op jit(solution)/shard_map/regroup/ppermute | solution.py:401
  20.7 15.8 %collective-permute-done.2.refs_3_.refs_1_ = bf16[3,2,18,16,128]{4,3,2,1,0:T(8,128)(2,1)S(1)} collective-permute-done((bf16[3,2,18,16,128]{4,3,2,1,0:T(8,128)(2,1)S(1)}, bf16[3,2,18,16,128]{4,3,2,1,0:T(8,128)(2,1)S(1)}, u32[]{:S(2)}, u32[]{:S(2)}) %collective-permute-start.2) | collective-permute-done | bytes 442400 | tf_op jit(solution)/shard_map/regroup/ppermute | solution.py:401
  36.6 1.3 %halo.4 = (bf16[6,10,16,128]{3,2,1,0:T(8,128)(2,1)}, bf16[6,10,16,128]{3,2,1,0:T(8,128)(2,1)S(1)}) custom-call(s32[2]{0:T(128)S(1)} %pad_add_fusion.me_ref, bf16[3,2,18,16,128]{4,3,2,1,0:T(8,128)(2,1)S(1)} %collective-permute-done.1.refs_2_.refs_0_, bf16[3,2,18,16,128]{4,3,2,1,0:T(8,128)(2,1)S(1)} %collective-permute-done.2.refs_3_.refs_1_), custom_call_target="tpu_custom_call" | custom-call | bytes 1048576 | tf_op jit(solution)/shard_map/halo/pallas_call | solution.py:187
  37.8 1.3 %halo.5 = (bf16[6,10,16,128]{3,2,1,0:T(8,128)(2,1)S(1)}, bf16[6,10,16,128]{3,2,1,0:T(8,128)(2,1)}) custom-call(s32[2]{0:T(128)S(1)} %pad_add_fusion.me_ref, bf16[3,2,18,16,128]{4,3,2,1,0:T(8,128)(2,1)S(1)} %collective-permute-done.1.refs_2_.refs_0_, bf16[3,2,18,16,128]{4,3,2,1,0:T(8,128)(2,1)S(1)} %collective-permute-done.2.refs_3_.refs_1_), custom_call_target="tpu_custom_call" | custom-call | bytes 1048576 | tf_op jit(solution)/shard_map/halo/pallas_call | solution.py:187
  39.1 0.0 collective-permute-start.4
  39.1 0.7 collective-permute-start.6
  39.8 0.0 copy-done.4
  39.8 0.0 copy-done.3
  39.8 6.0 %local_tiles.1 = (f32[64,256]{1,0:T(8,128)S(1)}, f32[3,2,512,256]{3,2,1,0:T(8,128)S(1)}, f32[3,2,512,256]{3,2,1,0:T(8,128)S(1)}, bf16[2,64,3072]{2,1,0:T(8,128)(2,1)S(1)}) custom-call(s32[2]{0:T(128)S(1)} %pad_add_fusion.me_ref, f32[3]{0:T(128)S(1)} %copy-done.4, bf16[3,2,18,16,128]{4,3,2,1,0:T(8,128)(2,1)S(1)} %get-tuple-element.29.refs_0_, ...), custom_call_target="tpu_custom_call" | custom-call | flops 5000000000 | bytes 12582912 | tf_op jit(solution)/shard_map/local_tiles/pallas_call | solution.py:204
  45.8 0.0 collective-permute-done.6.refs_1_.refs_3_
  45.8 0.0 collective-permute-done.5.refs_0_.refs_2_
  45.8 1.5 %return_tiles.2.above_ref = f32[64,256]{1,0:T(8,128)S(1)} custom-call(s32[2]{0:T(128)S(1)} %pad_add_fusion.me_ref, f32[3]{0:T(128)S(1)} %copy-done.4, f32[3,2,512,256]{3,2,1,0:T(8,128)S(1)} %get-tuple-element.47.cross_ref, bf16[7,10,16,128]{3,2,1,0:T(8,128)(2,1)S(1)} %collective-permute-done.5.refs_0_.refs_2_, ...), custom_call_target="tpu_custom_call" | custom-call | flops 3000000000 | bytes 6291456 | tf_op jit(solution)/shard_map/return_tiles/pallas_call | solution.py:268
  47.3 0.7 collective-permute-start.8
  48.0 0.0 collective-permute-done.4.refs_1_
  48.0 0.0 collective-permute-done.3.refs_0_
  48.0 1.5 %return_tiles.3.below_ref = f32[64,256]{1,0:T(8,128)S(1)} custom-call(s32[2]{0:T(128)S(1)} %pad_add_fusion.me_ref, f32[3]{0:T(128)S(1)} %copy-done.4, f32[3,2,512,256]{3,2,1,0:T(8,128)S(1)} %get-tuple-element.47.cross_ref, bf16[7,10,16,128]{3,2,1,0:T(8,128)(2,1)S(1)} %collective-permute-done.3.refs_0_, ...), custom_call_target="tpu_custom_call" | custom-call | flops 3000000000 | bytes 6291456 | tf_op jit(solution)/shard_map/return_tiles/pallas_call | solution.py:268
  49.5 5.5 %collective-permute-start.7 = (f32[64,256]{1,0:T(8,128)S(1)}, f32[64,256]{1,0:T(8,128)S(1)}, u32[]{:S(2)}, u32[]{:S(2)}) collective-permute-start(f32[64,256]{1,0:T(8,128)S(1)} %return_tiles.3.below_ref), channel_id=1, source_target_pairs={{0,4},{4,0},{8,12},{12,8},{16,20},{20,16},{24,28},{28,24},{32,36},... | collective-permute-start | bytes 196616 | tf_op jit(solution)/shard_map/return_tiles/ppermute | solution.py:427
  55.0 3.2 %edge_tiles.1.part_ref = f32[64,256]{1,0:T(8,128)S(1)} custom-call(s32[2]{0:T(128)S(1)} %pad_add_fusion.me_ref, f32[3]{0:T(128)S(1)} %copy-done.4, f32[64,256]{1,0:T(8,128)S(1)} %get-tuple-element.34.near_ref, f32[3,2,512,256]{3,2,1,0:T(8,128)S(1)} %get-tuple-element.35.edge_ref, bf16[2,64,3072]{2,1,0:T(8,128)(2,1)S(1)} %get-tuple-element.36.left_ref, ...), custom_call_target="tpu_custom_call" | custom-call | flops 5000000000 | bytes 20971520 | tf_op jit(solution)/shard_map/edge_tiles/pallas_call | solution.py:354
  58.2 0.0 collective-permute-done.7.from_below_ref
  58.2 0.0 collective-permute-done.8.from_above_ref
  58.2 0.7 sums.2
  58.9 12.6 %all-to-all-start = ((bf16[256,2,128]{2,1,0:T(2,128)(2,1)}), bf16[256,2,128]{2,1,0:T(2,128)(2,1)S(1)}, u32[]{:S(2)}, u32[]{:S(2)}) async-start(bf16[256,2,128]{2,1,0:T(2,128)(2,1)} %get-tuple-element.53), calls=%async_computation | async-start | bytes 262144 | tf_op jit(solution)/shard_map/sums/all_to_all | solution.py:432
  71.5 2.2 %collective-permute-start.9 = (f32[64,256]{1,0:T(8,128)S(1)}, f32[64,256]{1,0:T(8,128)S(1)}, u32[]{:S(2)}, u32[]{:S(2)}) collective-permute-start(f32[64,256]{1,0:T(8,128)S(1)} %get-tuple-element.52.refs_0_), channel_id=1, source_target_pairs={{0,1},{1,0},{2,3},{3,2},{4,5},{5,4},{6,7},{7,6},{8,9},{9,8},{10,11... | collective-permute-start | bytes 196616 | tf_op jit(solution)/shard_map/sums/ppermute | solution.py:434
  73.8 1.1 %collective-permute-start.10 = (f32[64,256]{1,0:T(8,128)S(1)}, f32[64,256]{1,0:T(8,128)S(1)}, u32[]{:S(2)}, u32[]{:S(2)}) collective-permute-start(f32[64,256]{1,0:T(8,128)S(1)} %get-tuple-element.52.refs_0_), channel_id=1, source_target_pairs={{0,2},{1,3},{2,0},{3,1},{4,6},{5,7},{6,4},{7,5},{8,10},{9,11},{10,... | collective-permute-start | bytes 196616 | tf_op jit(solution)/shard_map/sums/ppermute | solution.py:434
  74.9 2.1 %collective-permute-start.11 = (f32[64,256]{1,0:T(8,128)S(1)}, f32[64,256]{1,0:T(8,128)S(1)}, u32[]{:S(2)}, u32[]{:S(2)}) collective-permute-start(f32[64,256]{1,0:T(8,128)S(1)} %get-tuple-element.52.refs_0_), channel_id=1, source_target_pairs={{0,3},{1,2},{2,1},{3,0},{4,7},{5,6},{6,5},{7,4},{8,11},{9,10},{10,... | collective-permute-start | bytes 196616 | tf_op jit(solution)/shard_map/sums/ppermute | solution.py:434
  77.0 0.0 collective-permute-done.9.refs_1_
  77.0 2.2 %collective-permute-done.10.refs_2_ = f32[64,256]{1,0:T(8,128)S(1)} collective-permute-done((f32[64,256]{1,0:T(8,128)S(1)}, f32[64,256]{1,0:T(8,128)S(1)}, u32[]{:S(2)}, u32[]{:S(2)}) %collective-permute-start.10) | collective-permute-done | bytes 65568 | tf_op jit(solution)/shard_map/sums/ppermute | solution.py:434
  79.2 2.3 %collective-permute-done.11.refs_3_ = f32[64,256]{1,0:T(8,128)S(1)} collective-permute-done((f32[64,256]{1,0:T(8,128)S(1)}, f32[64,256]{1,0:T(8,128)S(1)}, u32[]{:S(2)}, u32[]{:S(2)}) %collective-permute-start.11) | collective-permute-done | bytes 65568 | tf_op jit(solution)/shard_map/sums/ppermute | solution.py:434
  81.5 3.1 %all-to-all-done.refs_4_ = bf16[256,2,128]{2,1,0:T(2,128)(2,1)S(1)} async-done(((bf16[256,2,128]{2,1,0:T(2,128)(2,1)}), bf16[256,2,128]{2,1,0:T(2,128)(2,1)S(1)}, u32[]{:S(2)}, u32[]{:S(2)}) %all-to-all-start) | async-done | bytes 131104 | tf_op jit(solution)/shard_map/sums/all_to_all | solution.py:432
  84.6 1.0 %sums.3 = (f32[1,4,64,64]{3,2,1,0:T(8,128)}, f32[4,1,64]{2,1,0:T(1,128)}) custom-call(f32[64,256]{1,0:T(8,128)S(1)} %get-tuple-element.52.refs_0_, f32[64,256]{1,0:T(8,128)S(1)} %collective-permute-done.9.refs_1_, f32[64,256]{1,0:T(8,128)S(1)} %collective-permute-done.10.refs_2_, f32[64,256]{1,0:T(8,128)S(1)} %collective-permute-done.11.refs_3_, ...), custom_call_target="tpu_custom_call" | custom-call | tf_op jit(solution)/shard_map/sums/pallas_call | solution.py:381
Async XLA Ops:
  0.6 39.2 %copy-start.4 = (f32[3]{0:T(128)S(1)}, f32[3]{0:T(128)}, u32[]{:S(2)}) copy-start(f32[3]{0:T(128)} %density_ref.7) | copy-start | bytes 40
  0.6 1.4 %copy-start = (bf16[16,3,2,64,128]{4,3,2,1,0:T(8,128)(2,1)S(1)}, bf16[16,3,2,64,128]{4,3,2,1,0:T(8,128)(2,1)}, u32[]{:S(2)}) copy-start(bf16[16,3,2,64,128]{4,3,2,1,0:T(8,128)(2,1)} %snaps_ref.1) | copy-start | bytes 4718596
  2.1 0.8 copy-start.1
  2.9 36.9 %copy-start.3 = (s32[2,64,128]{2,1,0:T(8,128)S(1)}, s32[2,64,128]{2,1,0:T(8,128)}, u32[]{:S(2)}) copy-start(s32[2,64,128]{2,1,0:T(8,128)} %refs_4_.3) | copy-start | bytes 196612
  4.2 6.6 %collective-permute-start = (bf16[3,2,18,16,128]{4,3,2,1,0:T(8,128)(2,1)S(1)}, bf16[3,2,18,16,128]{4,3,2,1,0:T(8,128)(2,1)S(1)}, u32[]{:S(2)}, u32[]{:S(2)}) collective-permute-start(bf16[3,2,18,16,128]{4,3,2,1,0:T(8,128)(2,1)S(1)} %get-tuple-element.30), channel_id=1, source_target_pairs={{0,1},{1,0},{2,3},{3,2},{4,5},{5,4},{6,7},{7,6},{8,9},{9,8},{10,11... | collective-permute-start | bytes 1327112 | tf_op jit(solution)/shard_map/regroup/ppermute | solution.py:401
  7.5 13.2 %collective-permute-start.1 = (bf16[3,2,18,16,128]{4,3,2,1,0:T(8,128)(2,1)S(1)}, bf16[3,2,18,16,128]{4,3,2,1,0:T(8,128)(2,1)S(1)}, u32[]{:S(2)}, u32[]{:S(2)}) collective-permute-start(bf16[3,2,18,16,128]{4,3,2,1,0:T(8,128)(2,1)S(1)} %get-tuple-element.31), channel_id=1, source_target_pairs={{0,2},{1,3},{2,0},{3,1},{4,6},{5,7},{6,4},{7,5},{8,10},{9,11},{10,... | collective-permute-start | bytes 1327112 | tf_op jit(solution)/shard_map/regroup/ppermute | solution.py:401
  8.7 27.8 %collective-permute-start.2 = (bf16[3,2,18,16,128]{4,3,2,1,0:T(8,128)(2,1)S(1)}, bf16[3,2,18,16,128]{4,3,2,1,0:T(8,128)(2,1)S(1)}, u32[]{:S(2)}, u32[]{:S(2)}) collective-permute-start(bf16[3,2,18,16,128]{4,3,2,1,0:T(8,128)(2,1)S(1)} %get-tuple-element.32), channel_id=1, source_target_pairs={{0,3},{1,2},{2,1},{3,0},{4,7},{5,6},{6,5},{7,4},{8,11},{9,10},{10,... | collective-permute-start | bytes 1327112 | tf_op jit(solution)/shard_map/regroup/ppermute | solution.py:401
  10.8 0.8 copy-start.2
  12.4 35.6 %collective-permute-start.3 = (bf16[7,10,16,128]{3,2,1,0:T(8,128)(2,1)S(1)}, bf16[7,10,16,128]{3,2,1,0:T(8,128)(2,1)S(1)}, u32[]{:S(2)}, u32[]{:S(2)}) collective-permute-start(bf16[7,10,16,128]{3,2,1,0:T(8,128)(2,1)S(1)} %get-tuple-element.39), channel_id=1, source_target_pairs={{0,4},{4,0},{8,12},{12,8},{16,20},{20,16},{24,28},{28,24},{32,36},... | collective-permute-start | bytes 860168 | tf_op jit(solution)/shard_map/halo/ppermute | solution.py:419
  12.5 33.3 %collective-permute-start.5 = (bf16[7,10,16,128]{3,2,1,0:T(8,128)(2,1)S(1)}, bf16[7,10,16,128]{3,2,1,0:T(8,128)(2,1)S(1)}, u32[]{:S(2)}, u32[]{:S(2)}) collective-permute-start(bf16[7,10,16,128]{3,2,1,0:T(8,128)(2,1)S(1)} %get-tuple-element.40), channel_id=1, source_target_pairs={{4,8},{8,4},{12,16},{16,12},{20,24},{24,20},{28,32},{32,28},{36,40... | collective-permute-start | bytes 860168 | tf_op jit(solution)/shard_map/halo/ppermute | solution.py:418
  39.1 8.9 %collective-permute-start.4 = (bf16[6,10,16,128]{3,2,1,0:T(8,128)(2,1)S(1)}, bf16[6,10,16,128]{3,2,1,0:T(8,128)(2,1)S(1)}, u32[]{:S(2)}, u32[]{:S(2)}) collective-permute-start(bf16[6,10,16,128]{3,2,1,0:T(8,128)(2,1)S(1)} %get-tuple-element.46), channel_id=1, source_target_pairs={{0,4},{4,0},{8,12},{12,8},{16,20},{20,16},{24,28},{28,24},{32,36},... | collective-permute-start | bytes 737288 | tf_op jit(solution)/shard_map/halo/ppermute | solution.py:419
  39.1 6.7 %collective-permute-start.6 = (bf16[6,10,16,128]{3,2,1,0:T(8,128)(2,1)S(1)}, bf16[6,10,16,128]{3,2,1,0:T(8,128)(2,1)S(1)}, u32[]{:S(2)}, u32[]{:S(2)}) collective-permute-start(bf16[6,10,16,128]{3,2,1,0:T(8,128)(2,1)S(1)} %get-tuple-element.48), channel_id=1, source_target_pairs={{4,8},{8,4},{12,16},{16,12},{20,24},{24,20},{28,32},{32,28},{36,40... | collective-permute-start | bytes 737288 | tf_op jit(solution)/shard_map/halo/ppermute | solution.py:418
  47.3 10.9 %collective-permute-start.8 = (f32[64,256]{1,0:T(8,128)S(1)}, f32[64,256]{1,0:T(8,128)S(1)}, u32[]{:S(2)}, u32[]{:S(2)}) collective-permute-start(f32[64,256]{1,0:T(8,128)S(1)} %return_tiles.2.above_ref), channel_id=1, source_target_pairs={{4,8},{8,4},{12,16},{16,12},{20,24},{24,20},{28,32},{32,28},{36,40... | collective-permute-start | bytes 196616 | tf_op jit(solution)/shard_map/return_tiles/ppermute | solution.py:424
  49.5 8.7 %collective-permute-start.7 = (f32[64,256]{1,0:T(8,128)S(1)}, f32[64,256]{1,0:T(8,128)S(1)}, u32[]{:S(2)}, u32[]{:S(2)}) collective-permute-start(f32[64,256]{1,0:T(8,128)S(1)} %return_tiles.3.below_ref), channel_id=1, source_target_pairs={{0,4},{4,0},{8,12},{12,8},{16,20},{20,16},{24,28},{28,24},{32,36},... | collective-permute-start | bytes 196616 | tf_op jit(solution)/shard_map/return_tiles/ppermute | solution.py:427
  58.9 25.6 %all-to-all-start = ((bf16[256,2,128]{2,1,0:T(2,128)(2,1)}), bf16[256,2,128]{2,1,0:T(2,128)(2,1)S(1)}, u32[]{:S(2)}, u32[]{:S(2)}) async-start(bf16[256,2,128]{2,1,0:T(2,128)(2,1)} %get-tuple-element.53), calls=%async_computation | async-start | bytes 262144 | tf_op jit(solution)/shard_map/sums/all_to_all | solution.py:432
  71.5 5.5 %collective-permute-start.9 = (f32[64,256]{1,0:T(8,128)S(1)}, f32[64,256]{1,0:T(8,128)S(1)}, u32[]{:S(2)}, u32[]{:S(2)}) collective-permute-start(f32[64,256]{1,0:T(8,128)S(1)} %get-tuple-element.52.refs_0_), channel_id=1, source_target_pairs={{0,1},{1,0},{2,3},{3,2},{4,5},{5,4},{6,7},{7,6},{8,9},{9,8},{10,11... | collective-permute-start | bytes 196616 | tf_op jit(solution)/shard_map/sums/ppermute | solution.py:434
  73.8 5.4 %collective-permute-start.10 = (f32[64,256]{1,0:T(8,128)S(1)}, f32[64,256]{1,0:T(8,128)S(1)}, u32[]{:S(2)}, u32[]{:S(2)}) collective-permute-start(f32[64,256]{1,0:T(8,128)S(1)} %get-tuple-element.52.refs_0_), channel_id=1, source_target_pairs={{0,2},{1,3},{2,0},{3,1},{4,6},{5,7},{6,4},{7,5},{8,10},{9,11},{10,... | collective-permute-start | bytes 196616 | tf_op jit(solution)/shard_map/sums/ppermute | solution.py:434
  74.9 6.6 %collective-permute-start.11 = (f32[64,256]{1,0:T(8,128)S(1)}, f32[64,256]{1,0:T(8,128)S(1)}, u32[]{:S(2)}, u32[]{:S(2)}) collective-permute-start(f32[64,256]{1,0:T(8,128)S(1)} %get-tuple-element.52.refs_0_), channel_id=1, source_target_pairs={{0,3},{1,2},{2,1},{3,0},{4,7},{5,6},{6,5},{7,4},{8,11},{9,10},{10,... | collective-permute-start | bytes 196616 | tf_op jit(solution)/shard_map/sums/ppermute | solution.py:434
